TPU v7x, 32 devices: a whole 2x2x4 slice. The times are simulated.
32 devices in a mesh: orb: 8 (over z, x), comp: 4 (over y, core).
Axes of the slice: x: 2, y: 2, z: 4, core: 2. Of those that a mesh axis runs over, the one named last changes fastest.
Arguments:
- psi: bfloat16 [512, 4, 64, 128], P('orb', None, 'comp'), may hold values from -16 to 16
- region_start: int32 [512], replicated, may hold values from 0 to 31
- region_len: int32 [512], replicated, may hold values from 16 to 32
- fine_mask: int32 [64, 8], P('comp'), may hold values 0 or 1
- occupation: int32 [512], replicated, may hold values from 0 to 2
- kinetic_taps: bfloat16 [29, 4, 4], replicated, may hold values from -0.5 to 0.5
- magic_taps: bfloat16 [16, 4], replicated, may hold values from -0.75 to 0.75
- external: float32 [64, 128], P('comp'), may hold values from -12 to 12
Outputs:
- density: float32 [64, 128], P('comp', 'orb')
- psi_next: bfloat16 [512, 4, 64, 128], P(None, None, 'comp', 'orb')
Inputs may be any that keep to these rules, and one draw needn't show every extreme that they name: region_start + region_len <= 64.
All inputs are finite; a program needn't handle non-finite values. No bound on the sum of `fine_mask` on one device may be relied on, other than what follows from the above.
Results may differ from a plain program's by a relative error of at most 0.012.
Values may be sent and summed in bfloat16 or wider, within the bound.
No kernel may reach another device: no remote copies, remote signals or barrier semaphores. Data moves between devices by JAX's collectives and lax.ppermute only.
A program may use at most 128 MiB of HBM per device.

v0:
```python
import jax
import jax.numpy as jnp
from jax import lax
from jax.sharding import PartitionSpec as P

ZB = 16


xc_factor = 0.98474502
step_length = 0.1


def extended(cells, sides, width):
    for axis, dim in sides:
        count = lax.axis_size(axis)
        ends = count - 1
        head = lax.slice_in_dim(cells, 0, width, axis=dim)
        tail = lax.slice_in_dim(cells, cells.shape[dim] - width, cells.shape[dim], axis=dim)
        cells = jnp.concatenate(
            [
                lax.ppermute(tail, axis, [(i, (i + 1) % count) for i in range(ends)]),
                cells,
                lax.ppermute(head, axis, [((i + 1) % count, i) for i in range(ends)]),
            ],
            axis=dim,
        )
    return cells


def onehot_band(window, length, shift, sign, count):
    offset = sign * (jnp.arange(window)[:, None] - jnp.arange(length)[None, :]) + shift
    return (offset[:, :, None] == jnp.arange(count)[None, None, :]).astype(jnp.bfloat16)


def kinetic_kernel(filter_taps, window, length):
    onehot = onehot_band(window, length, 0, 1, filter_taps.shape[0])
    return jnp.einsum(
        "jit,ted->djei", onehot, filter_taps, preferred_element_type=jnp.float32
    ).astype(jnp.bfloat16)


def magic_kernel(magic, window, length):
    onehot = onehot_band(window, length, -7, 1, magic.shape[0])
    return jnp.einsum("jit,td->dji", onehot, magic, preferred_element_type=jnp.float32).astype(
        jnp.bfloat16
    )


def adjoint_kernel(magic, window, length):
    onehot = onehot_band(window, length, 21, -1, magic.shape[0])
    return jnp.einsum("jit,te->jei", onehot, magic, preferred_element_type=jnp.float32).astype(
        jnp.bfloat16
    )


def depth_blocks(values, block_len):
    cells = values.shape[-1]
    blocks = cells // block_len
    config = [(0, 0)] * (values.ndim - 1) + [(14, block_len - 14)]
    padded = jnp.pad(values, config)
    heads = padded[..., :cells].reshape(values.shape[:-1] + (blocks, block_len))
    tails = padded[..., block_len:].reshape(values.shape[:-1] + (blocks, block_len))[..., :28]
    return jnp.concatenate([heads, tails], axis=-1)


def region_support(starts, lengths, first_plane, slab_len, fine_cells, channels):
    planes = first_plane + jnp.arange(slab_len)
    inside = (planes[None, :] >= starts[:, None]) & (planes[None, :] < (starts + lengths)[:, None])
    channel_on = (jnp.arange(channels)[:, None, None] == 0) | (fine_cells[None] > 0)
    return inside[:, None, :, None] & channel_on[None]


def plane_conv(plane_window, filter_taps, slab_len):
    kernel = kinetic_kernel(filter_taps, plane_window.shape[2], slab_len)
    return jnp.einsum("odjz,djei->oeiz", plane_window, kernel, preferred_element_type=jnp.float32)


def depth_apply(depth_window, filter_taps, magic, cells_out):
    window = depth_window.shape[-1]
    block_len = window - 28
    kernel = kinetic_kernel(filter_taps, window, block_len)
    forward = magic_kernel(magic, window, block_len)
    kinetic = jnp.einsum(
        "odxbj,djei->oexbi", depth_window, kernel, preferred_element_type=jnp.float32
    )
    grid_values = jnp.einsum(
        "odxbj,dji->oxbi", depth_window, forward, preferred_element_type=jnp.float32
    )
    shape = depth_window.shape
    return (
        kinetic.reshape(shape[0], shape[1], shape[2], cells_out),
        grid_values.reshape(shape[0], shape[2], cells_out),
    )


def adjoint_apply(value_window, magic, channels, cells_out):
    window = value_window.shape[-1]
    kernel = adjoint_kernel(magic, window, window - 28)
    result = jnp.einsum("oxbj,jei->oexbi", value_window, kernel, preferred_element_type=jnp.float32)
    return result.reshape(value_window.shape[0], channels, value_window.shape[1], cells_out)


def local(psi, region_start, region_len, fine_mask, occupation, kinetic_taps, magic_taps, external):
    orb_dev, channels, slab_len, cells_z = psi.shape
    orb_count = lax.axis_size("orb")
    comp_count = lax.axis_size("comp")
    orbitals = orb_dev * orb_count
    piece_len = cells_z // orb_count
    grid_cells = slab_len * comp_count * cells_z
    first_plane = lax.axis_index("comp") * slab_len
    first_cell = lax.axis_index("orb") * piece_len
    first_orbital = lax.axis_index("orb") * orb_dev
    fine_cells = jnp.repeat(fine_mask, ZB, axis=1)
    starts = lax.dynamic_slice_in_dim(region_start, first_orbital, orb_dev)
    lengths = lax.dynamic_slice_in_dim(region_len, first_orbital, orb_dev)
    support = region_support(starts, lengths, first_plane, slab_len, fine_cells, channels)
    masked = jnp.where(support, psi, jnp.zeros((), psi.dtype))
    occupied = lax.dynamic_slice_in_dim(occupation, first_orbital, orb_dev).astype(jnp.float32)
    plane_window = extended(masked, (("comp", 2),), 14)
    kinetic, grid_values = depth_apply(depth_blocks(masked, 64), kinetic_taps, magic_taps, cells_z)
    kinetic = kinetic + plane_conv(plane_window, kinetic_taps, slab_len)
    partial_density = jnp.sum(occupied[:, None, None] * grid_values * grid_values, axis=0)
    total = lax.psum(partial_density, "orb")
    potential = external - xc_factor * jnp.cbrt(total)
    density = lax.dynamic_slice_in_dim(total, first_cell, piece_len, 1)
    weighted = (potential[None] * grid_values).astype(jnp.bfloat16)
    total_applied = kinetic + adjoint_apply(
        depth_blocks(weighted, 64), magic_taps, channels, cells_z
    )
    applied = jnp.where(support, total_applied, jnp.zeros((), jnp.float32)).astype(jnp.bfloat16)
    masked_t, applied_t = (
        lax.all_to_all(masked, "orb", split_axis=3, concat_axis=0, tiled=True),
        lax.all_to_all(applied, "orb", split_axis=3, concat_axis=0, tiled=True),
    )
    masked_rows = masked_t.reshape(orbitals, -1)
    applied_rows = applied_t.reshape(orbitals, -1)
    intersection_part = jnp.einsum(
        "ik,jk->ij", masked_rows, masked_rows, preferred_element_type=jnp.float32
    )
    lagrange_part = jnp.einsum(
        "ik,jk->ij", applied_rows, masked_rows, preferred_element_type=jnp.float32
    )
    intersection_sum, lagrange_sum = lax.psum((intersection_part, lagrange_part), ("orb", "comp"))
    intersection_round = (intersection_sum / grid_cells).astype(jnp.bfloat16)
    lagrange_round = (lagrange_sum / grid_cells).astype(jnp.bfloat16)
    gradient = applied_rows.astype(jnp.float32) - jnp.dot(
        lagrange_round, masked_rows, preferred_element_type=jnp.float32
    )
    trial = (masked_rows.astype(jnp.float32) - step_length * gradient).astype(jnp.bfloat16)
    following = 1.5 * trial.astype(jnp.float32) - 0.5 * jnp.dot(
        intersection_round, trial, preferred_element_type=jnp.float32
    )
    psi_next = following.astype(jnp.bfloat16).reshape(orbitals, channels, slab_len, piece_len)
    return (density, psi_next)


def solution(mesh):
    return jax.shard_map(
        local,
        mesh=mesh,
        in_specs=(
            P("orb", None, "comp", None),
            P(),
            P(),
            P("comp", None),
            P(),
            P(),
            P(),
            P("comp", None),
        ),
        out_specs=(P("comp", "orb"), P(None, None, "comp", "orb")),
        check_vma=False,
    )
```

profile of v0, /device:TPU:0, one launch (start us, length us, event | category | flops | bytes accessed | tf_op | source)
XLA Modules:
  0.0 300.3 jit_solution(4893629684377063062)
XLA Ops:
  7.2 0.7 broadcast_compare_fusion
  7.9 0.1 copy.84
  8.0 0.1 broadcast_in_dim.8
  8.1 0.1 gt.17
  8.2 0.8 dynamic-slice_add_fusion
  9.0 0.1 compare_and_fusion
  9.1 0.1 copy.83
  9.2 0.1 broadcast_or_fusion
  9.2 1.6 and_select_fusion.1
  10.9 0.5 fusion.49
  11.4 1.5 copy.94
  12.9 1.3 collective-permute-start.1
  14.2 1.6 copy.93
  15.8 4.0 %collective-permute-start = (bf16[64,4,14,128]{3,0,2,1:T(8,128)(2,1)}, bf16[64,4,14,128]{3,0,2,1:T(8,128)(2,1)}, u32[]{:S(2)}, u32[]{:S(2)}) collective-permute-start(bf16[64,4,14,128]{3,0,2,1:T(8,128)(2,1)} %copy.93), channel_id=1, source_target_pairs={{0,1},{1,2},{2,3},{4,5},{5,6},{6,7},{8,9},{9,10},{10,11},{12,13},{... | collective-permute-start | bytes 2752520 | tf_op jit(solution)/shard_map/ppermute | solution.py:21
  19.8 3.5 %copy.88 = bf16[64,4,16,128]{0,2,1,3:T(8,128)(2,1)S(1)} copy(bf16[64,4,16,128]{3,2,1,0:T(8,128)(2,1)S(1)} %and_select_fusion.1) | data formatting | bytes 2097152 | tf_op jit(solution)/shard_map/jit(_where)/select_n | solution.py:117
  23.3 2.7 reshape.182
  26.0 7.3 %all-to-all-start = ((bf16[8,2,32768]{2,1,0:T(2,128)(2,1)}), bf16[8,2,32768]{2,1,0:T(2,128)(2,1)}, u32[]{:S(2)}, u32[]{:S(2)}) async-start(bf16[8,2,32768]{2,1,0:T(2,128)(2,1)} %reshape.182), calls=%async_computation | async-start | bytes 2097152 | tf_op jit(solution)/shard_map/all_to_all | solution.py:132
  33.2 1.6 pad_slice_fusion.1
  34.8 1.9 reshape.157
  36.7 2.9 copy.127
  39.6 5.0 %reshape.156 = bf16[64,4,16,2,64]{4,3,2,1,0:T(2,128)(2,1)} reshape(bf16[64,4,16,128]{3,2,1,0:T(8,128)(2,1)} %get-tuple-element.10) | data formatting | bytes 2097152 | tf_op jit(solution)/shard_map/reshape | solution.py:61
  44.6 3.0 copy.86
  47.6 0.2 fusion.18
  47.8 2.6 fusion.21
  50.5 0.1 reduce_sum.12
  50.6 22.3 %psum.21 = f32[16,128]{1,0:T(8,128)S(1)} all-reduce(f32[16,128]{1,0:T(8,128)S(1)} %reduce_sum.12), channel_id=1, replica_groups=mesh['orb'=8,'comp'=4] {'orb'}, use_global_device_ids=true, to_apply=%region_1.2 | all-reduce | flops 2048 | bytes 16384 | tf_op jit(solution)/shard_map/psum | solution.py:123
  72.9 3.0 %copy.99 = f32[64,16,2,64]{3,2,1,0:T(2,128)} copy(f32[64,16,2,64]{3,0,2,1:T(8,128)} %get-tuple-element.15) | data formatting | bytes 1048576 | tf_op jit(solution)/shard_map/odxbj,dji->oxbi/dot_general | solution.py:86
  75.9 2.6 reshape.160
  78.6 1.1 multiply_convert_fusion.4
  79.7 0.9 pad_slice_fusion.3
  80.6 2.0 reshape.162
  82.5 2.0 copy.128
  84.6 1.0 reshape.161
  85.6 1.2 copy.101
  86.9 0.2 fusion.19
  87.1 3.9 %fusion.23 = f32[4,64,64,16,2]{2,1,4,3,0:T(8,128)} fusion(bf16[64,16,2,28]{3,0,2,1:T(8,128)(2,1)} %copy.128, bf16[64,16,2,64]{3,0,2,1:T(8,128)(2,1)S(1)} %copy.101, bf16[92,4,64,1,1]{2,1,0,4,3:T(4,128)(2,1)S(1)} %fusion.19), kind=kOutput, calls=%fused_computation.40 | convolution fusion | flops 97222656 | bytes 2521088 | tf_op jit(solution)/shard_map/oxbj,jei->oexbi/dot_general | solution.py:99
  91.0 4.2 %copy.125 = f32[64,4,16,128]{3,2,1,0:T(8,128)} copy(f32[64,4,16,128]{0,3,2,1:T(8,128)} %bitcast.106) | data formatting | bytes 4194304 | tf_op jit(solution)/shard_map/reshape | solution.py:100
  95.2 0.4 fusion.15
  95.7 6.0 %fusion.7 = f32[4,64,64,16,2,1]{2,1,5,4,3,0:T(8,128)} fusion(bf16[4,92,4,64,1,1]{3,0,2,1,5,4:T(4,128)(2,1)S(1)} %fusion.15, bf16[64,4,16,2,28]{4,0,1,3,2:T(8,128)(2,1)S(1)} %copy.127, bf16[64,4,16,2,64]{4,0,1,3,2:T(8,128)(2,1)} %copy-done.2), kind=kOutput, calls=%fused_computation.14 | convolution fusion | flops 388890624 | bytes 3792896 | tf_op jit(solution)/shard_map/odxbj,djei->oexbi/dot_general | solution.py:83
  101.7 3.5 %copy.98 = f32[64,4,16,128]{3,2,1,0:T(8,128)S(1)} copy(f32[64,4,16,128]{0,3,2,1:T(8,128)} %bitcast.107) | data formatting | bytes 4194304 | tf_op jit(solution)/shard_map/reshape | solution.py:91
  105.2 0.2 fusion.20
  105.4 1.9 copy.96
  107.4 1.8 copy.95
  109.2 2.6 fusion.5
  111.8 4.7 %copy.104 = bf16[64,4,16,128]{0,2,1,3:T(8,128)(2,1)S(1)} copy(bf16[64,4,16,128]{3,2,1,0:T(8,128)(2,1)} %fusion.5) | data formatting | bytes 2097152 | tf_op jit(solution)/shard_map/convert_element_type | solution.py:130
  116.5 2.7 reshape.180
  119.2 4.3 %all-to-all-start.1 = ((bf16[8,2,32768]{2,1,0:T(2,128)(2,1)}), bf16[8,2,32768]{2,1,0:T(2,128)(2,1)}, u32[]{:S(2)}, u32[]{:S(2)}) async-start(bf16[8,2,32768]{2,1,0:T(2,128)(2,1)} %reshape.180), calls=%async_computation.1 | async-start | bytes 2097152 | tf_op jit(solution)/shard_map/all_to_all | solution.py:133
  123.4 0.3 all-reduce.5.cloned.1.call-start
  123.7 3.1 %reshape.183 = bf16[128,4,16,64]{3,2,1,0:T(8,128)(2,1)S(1)} reshape(bf16[8,2,32768]{2,1,0:T(2,128)(2,1)} %all-to-all-done) | data formatting | bytes 2097152
  126.8 2.7 copy.90
  129.5 3.2 %reshape.158 = bf16[512,1024]{0,1:T(8,128)(2,1)S(1)} reshape(bf16[8,64,4,16,16]{1,0,4,3,2:T(8,128)(2,1)} %copy.90) | data formatting | bytes 2097152 | tf_op jit(solution)/shard_map/reshape | solution.py:135
  132.7 1.7 fusion.51
  134.4 11.4 %all-to-all-done.1 = bf16[8,2,32768]{2,1,0:T(2,128)(2,1)} async-done(((bf16[8,2,32768]{2,1,0:T(2,128)(2,1)}), bf16[8,2,32768]{2,1,0:T(2,128)(2,1)}, u32[]{:S(2)}, u32[]{:S(2)}) %all-to-all-start.1) | async-done | bytes 1048608 | tf_op jit(solution)/shard_map/all_to_all | solution.py:133
  145.8 3.1 %reshape.181 = bf16[128,4,16,64]{3,2,1,0:T(8,128)(2,1)S(1)} reshape(bf16[8,2,32768]{2,1,0:T(2,128)(2,1)} %all-to-all-done.1) | data formatting | bytes 2097152
  148.9 2.7 copy.106
  151.6 3.2 %reshape.164 = bf16[512,1024]{0,1:T(8,128)(2,1)S(1)} reshape(bf16[8,64,4,16,16]{1,0,4,3,2:T(8,128)(2,1)} %copy.106) | data formatting | bytes 2097152 | tf_op jit(solution)/shard_map/reshape | solution.py:136
  154.8 1.7 fusion.50
  156.6 0.7 constant_dynamic-slice_fusion
  157.2 0.5 copy.91
  157.8 1.3 copy.107
  159.1 129.7 %all-reduce.5.cloned.1.call-done = (f32[512,512]{1,0:T(8,128)}, f32[512,512]{1,0:T(8,128)}) async-done(((f32[512,512]{1,0:T(8,128)}, f32[512,512]{1,0:T(8,128)}), (f32[512,512]{1,0:T(8,128)}, f32[512,512]{1,0:T(8,128)})) %all-reduce.5.cloned.1.call-update) | async-done | bytes 2097168 | tf_op jit(solution)/shard_map/psum | solution.py:143
  288.8 2.5 subtract_convert_fusion.1
  291.3 0.7 subtract_convert_fusion
  292.1 1.3 copy.108
  (25 shorter events, 0.1 us)
Async XLA Ops:
  7.2 88.1 %copy-start = (bf16[29,4,4]{0,2,1:T(4,128)(2,1)S(1)}, bf16[29,4,4]{0,2,1:T(4,128)(2,1)}, u32[]{:S(2)}) copy-start(bf16[29,4,4]{0,2,1:T(4,128)(2,1)} %param.13) | copy-start | bytes 2788
  12.9 92.5 %collective-permute-start.1 = (bf16[64,4,14,128]{3,0,2,1:T(8,128)(2,1)}, bf16[64,4,14,128]{3,0,2,1:T(8,128)(2,1)}, u32[]{:S(2)}, u32[]{:S(2)}) collective-permute-start(bf16[64,4,14,128]{3,0,2,1:T(8,128)(2,1)} %copy.94), channel_id=1, source_target_pairs={{1,0},{2,1},{3,2},{5,4},{6,5},{7,6},{9,8},{10,9},{11,10},{13,12},{... | collective-permute-start | bytes 2752520 | tf_op jit(solution)/shard_map/ppermute | solution.py:23
  15.8 91.6 %collective-permute-start = (bf16[64,4,14,128]{3,0,2,1:T(8,128)(2,1)}, bf16[64,4,14,128]{3,0,2,1:T(8,128)(2,1)}, u32[]{:S(2)}, u32[]{:S(2)}) collective-permute-start(bf16[64,4,14,128]{3,0,2,1:T(8,128)(2,1)} %copy.93), channel_id=1, source_target_pairs={{0,1},{1,2},{2,3},{4,5},{5,6},{6,7},{8,9},{9,10},{10,11},{12,13},{... | collective-permute-start | bytes 2752520 | tf_op jit(solution)/shard_map/ppermute | solution.py:21
  26.0 93.2 %all-to-all-start = ((bf16[8,2,32768]{2,1,0:T(2,128)(2,1)}), bf16[8,2,32768]{2,1,0:T(2,128)(2,1)}, u32[]{:S(2)}, u32[]{:S(2)}) async-start(bf16[8,2,32768]{2,1,0:T(2,128)(2,1)} %reshape.182), calls=%async_computation | async-start | bytes 2097152 | tf_op jit(solution)/shard_map/all_to_all | solution.py:132
  44.6 3.0 copy-start.6
  47.6 2.9 copy-start.2
  50.5 28.1 %copy-start.4 = (f32[16,128]{1,0:T(8,128)S(1)}, f32[16,128]{1,0:T(8,128)}, u32[]{:S(2)}) copy-start(f32[16,128]{1,0:T(8,128)} %param.15) | copy-start | bytes 24580
  105.2 3.9 %copy-start.3 = (f32[64,4,16,128]{3,2,1,0:T(8,128)S(1)}, f32[64,4,16,128]{3,2,1,0:T(8,128)}, u32[]{:S(2)}) copy-start(f32[64,4,16,128]{3,2,1,0:T(8,128)} %copy.125) | copy-start | bytes 6291460
  119.2 26.7 %all-to-all-start.1 = ((bf16[8,2,32768]{2,1,0:T(2,128)(2,1)}), bf16[8,2,32768]{2,1,0:T(2,128)(2,1)}, u32[]{:S(2)}, u32[]{:S(2)}) async-start(bf16[8,2,32768]{2,1,0:T(2,128)(2,1)} %reshape.180), calls=%async_computation.1 | async-start | bytes 2097152 | tf_op jit(solution)/shard_map/all_to_all | solution.py:133
  123.4 165.3 %all-reduce.5.cloned.1.call-start = ((), (), s32[]{:S(2)}) async-start(), calls=%async_computation.2 | async-start | bytes 4194304 | tf_op jit(solution)/shard_map/psum | solution.py:143
  288.8 2.6 copy-start.5
  291.3 2.1 copy-start.1
Sparse Core Ops, SparseCore 0:
  156.7 132.0 all-reduce.4
where the time goes:
time: 301 us; the launch traced here: 300 us
  waiting for transfers between devices  141 us (47%)
  local copies, waits for them, and re-layouts  78.1 us (26%)
  matrix products  22.9 us (8%)
  blocking collectives  22.3 us (7%)
  starting transfers between devices  17.1 us (6%)
  between operations  14.3 us (5%)
  other arithmetic  4.44 us (1%)
    psum x1, waiting for transfers between devices, local(): lax.psum((intersection_part, lagrange_part), ('orb', 'comp'))  130 us
    psum x1, blocking collectives, local(): total = lax.psum(partial_density, 'orb')  22.3 us
    unnamed x20, local copies, waits for them, and re-layouts  16.6 us
    all_to_all x1, waiting for transfers between devices, local(): lax.all_to_all(applied, 'orb', split_axis=3, concat_axis=0, tiled=True)  11.4 us
    reshape x4, local copies, waits for them, and re-layouts, depth_blocks(): heads = padded[..., :cells].reshape(values.shape[:-1] + (blocks, block_len))  10.2 us
    all_to_all x1, starting transfers between devices, local(): lax.all_to_all(masked, 'orb', split_axis=3, concat_axis=0, tiled=True)  7.25 us
  transfers between devices with their start and end apart: 5, of which 2 were waited for; matrix products, arithmetic and copies ran while one was open for 28% of the time, Pallas kernels for 0%

commit v1 on v0

v1 whole, which is shorter than its diff:
```python
import functools

import jax
import jax.numpy as jnp
from jax import lax
from jax.experimental import pallas as pl
from jax.experimental.pallas import tpu as pltpu
from jax.sharding import PartitionSpec as P

ZB = 16
LANES = 128
CHUNK = 16

xc_factor = 0.98474502
step_length = 0.1
f32 = jnp.float32
bf16 = jnp.bfloat16
VMEM = pl.BlockSpec(memory_space=pltpu.VMEM)
SMEM = pl.BlockSpec(memory_space=pltpu.SMEM)


def params(mib=40):
    return pltpu.CompilerParams(vmem_limit_bytes=mib * 2**20)


def band(window, length, shift, sign, taps):
    count = taps.shape[0]
    offset = sign * (jnp.arange(window)[:, None] - jnp.arange(length)[None, :]) + shift
    onehot = (offset[:, :, None] == jnp.arange(count)[None, None, :]).astype(bf16)
    return onehot


def depth_matrix(taps, cells):
    onehot = band(cells, cells, 14, 1, taps)
    kernel = jnp.einsum("jit,ted->djei", onehot, taps, preferred_element_type=f32).astype(bf16)
    ch = taps.shape[1]
    return kernel.reshape(ch * cells, ch * cells)


def plane_matrix(taps, slab):
    ch = taps.shape[1]
    parts = []
    for block in (-1, 0, 1):
        onehot = band(slab, slab, 14 + block * slab, 1, taps)
        part = jnp.einsum("jit,ted->eidj", onehot, taps, preferred_element_type=f32).astype(bf16)
        parts.append(part.reshape(ch * slab, ch * slab))
    return jnp.concatenate(parts, axis=1)


def magic_matrix(magic, cells):
    onehot = band(cells, cells, 7, 1, magic)
    kernel = jnp.einsum("jit,td->dji", onehot, magic, preferred_element_type=f32).astype(bf16)
    return kernel.reshape(magic.shape[1] * cells, cells)


def adjoint_matrix(magic, cells):
    onehot = band(cells, cells, 7, -1, magic)
    kernel = jnp.einsum("jit,te->jei", onehot, magic, preferred_element_type=f32).astype(bf16)
    return kernel.reshape(cells, magic.shape[1] * cells)


def spread(scratch, row, value):
    slab = value.shape[0]
    for tile in range(value.shape[1] // LANES):
        scratch[tile, pl.ds(pl.multiple_of(row, slab), slab), :] = value[
            :, tile * LANES : (tile + 1) * LANES
        ]


def pack(scratch, out_ref, rows, piece):
    pieces, groups, orbs, _ = out_ref.shape
    blocks = LANES // piece
    lane = lax.broadcasted_iota(jnp.int32, (CHUNK, LANES), 1) // piece

    def group(g, carry):
        for tile in range(pieces // blocks):
            for start in range(0, orbs, CHUNK):
                held = [
                    scratch[tile, pl.ds(start * rows + g * blocks + c, CHUNK, stride=rows), :]
                    for c in range(blocks)
                ]
                bit = 1
                while bit < blocks:
                    low_lane = (lane & bit) == 0
                    for c in range(blocks):
                        if c & bit:
                            continue
                        low, high = held[c], held[c | bit]
                        held[c] = jnp.where(low_lane, low, pltpu.roll(high, bit * piece, 1))
                        held[c | bit] = jnp.where(
                            low_lane, pltpu.roll(low, LANES - bit * piece, 1), high
                        )
                    bit *= 2
                for c in range(blocks):
                    out_ref[tile * blocks + c, g, pl.ds(start, CHUNK), :] = held[c].astype(bf16)
        return carry

    lax.fori_loop(0, groups, group, 0)


def mask_body(piece, where_ref, start_ref, len_ref, psi_ref, fine_ref, masked_ref, out_ref, scratch):
    orbs, channels, slab, cells = psi_ref.shape
    rows = channels * slab
    first_orbital, first_plane = where_ref[0], where_ref[1]
    plane = first_plane + lax.broadcasted_iota(jnp.int32, (slab, cells), 0)
    fine = fine_ref[...] > 0

    def one(o, carry):
        s = start_ref[first_orbital + o]
        inside = (plane >= s) & (plane < s + len_ref[first_orbital + o])
        both = inside & fine
        for e in range(channels):
            keep = inside if e == 0 else both
            value = jnp.where(keep, psi_ref[o, e].astype(f32), 0.0)
            masked_ref[o, e] = value.astype(bf16)
            spread(scratch, o * rows + e * slab, value)
        return carry

    lax.fori_loop(0, orbs, one, 0, unroll=4)
    pack(scratch, out_ref, rows, piece)


def density_body(where_ref, occ_ref, masked_ref, magic_ref, values_ref, density_ref):
    orbs, channels, slab, cells = masked_ref.shape
    first_orbital = where_ref[0]

    def chunk(k, total):
        o = pl.multiple_of(k * CHUNK, CHUNK)
        lhs = jnp.concatenate(
            [
                masked_ref[pl.ds(o, CHUNK), d].reshape(CHUNK * slab, cells)
                for d in range(channels)
            ],
            axis=1,
        )
        result = jnp.dot(lhs, magic_ref[...], preferred_element_type=f32)
        values_ref[pl.ds(o, CHUNK)] = result.reshape(CHUNK, slab, cells)
        for i in range(CHUNK):
            part = result[i * slab : (i + 1) * slab]
            total = total + occ_ref[first_orbital + o + i].astype(f32) * part * part
        return total

    density_ref[...] = lax.fori_loop(0, orbs // CHUNK, chunk, jnp.zeros((slab, cells), f32))


def kinetic_body(
    where_ref, start_ref, len_ref, masked_ref, before_ref, after_ref, depth_ref, plane_ref, out_ref
):
    orbs, channels, slab, cells = masked_ref.shape
    rows = channels * slab

    def chunk(k, carry):
        o = pl.multiple_of(k * CHUNK, CHUNK)
        lhs = jnp.concatenate(
            [
                masked_ref[pl.ds(o, CHUNK), d].reshape(CHUNK * slab, cells)
                for d in range(channels)
            ],
            axis=1,
        )
        along_z = jnp.dot(lhs, depth_ref[...], preferred_element_type=f32)
        for i in range(0, CHUNK, 2):
            window = jnp.concatenate(
                [
                    jnp.concatenate(
                        [
                            ref[o + i + b].reshape(rows, cells)
                            for ref in (before_ref, masked_ref, after_ref)
                        ],
                        axis=0,
                    )
                    for b in range(2)
                ],
                axis=1,
            )
            along_x = jnp.dot(plane_ref[...], window, preferred_element_type=f32)
            for b in range(2):
                for e in range(channels):
                    out_ref[o + i + b, e] = (
                        along_x[e * slab : (e + 1) * slab, b * cells : (b + 1) * cells]
                        + along_z[
                            (i + b) * slab : (i + b + 1) * slab, e * cells : (e + 1) * cells
                        ]
                    )
        return carry

    lax.fori_loop(0, orbs // CHUNK, chunk, 0)


def applied_body(
    piece,
    where_ref,
    start_ref,
    len_ref,
    kinetic_ref,
    values_ref,
    potential_ref,
    fine_ref,
    adjoint_ref,
    out_ref,
    scratch,
):
    orbs, channels, slab, cells = kinetic_ref.shape
    rows = channels * slab
    first_orbital, first_plane = where_ref[0], where_ref[1]
    plane = first_plane + lax.broadcasted_iota(jnp.int32, (slab, cells), 0)
    fine = fine_ref[...] > 0
    potential = potential_ref[...]

    def chunk(k, carry):
        o = pl.multiple_of(k * CHUNK, CHUNK)
        weighted = (potential[None] * values_ref[pl.ds(o, CHUNK)]).astype(bf16)
        back = jnp.dot(
            weighted.reshape(CHUNK * slab, cells), adjoint_ref[...], preferred_element_type=f32
        )
        for i in range(CHUNK):
            s = start_ref[first_orbital + o + i]
            inside = (plane >= s) & (plane < s + len_ref[first_orbital + o + i])
            both = inside & fine
            for e in range(channels):
                keep = inside if e == 0 else both
                value = (
                    kinetic_ref[o + i, e]
                    + back[i * slab : (i + 1) * slab, e * cells : (e + 1) * cells]
                )
                spread(scratch, (o + i) * rows + e * slab, jnp.where(keep, value, 0.0))
        return carry

    lax.fori_loop(0, orbs // CHUNK, chunk, 0)
    pack(scratch, out_ref, rows, piece)


def unpack(got_ref, rows_ref):
    sources, groups, orbs, lanes = got_ref.shape
    for i in range(sources):
        for g in range(groups):
            rows_ref[pl.ds(i * orbs, orbs), pl.ds(g * lanes, lanes)] = got_ref[i, g]


def self_gram_body(got_ref, rows_ref, gram_ref):
    unpack(got_ref, rows_ref)
    gram_ref[...] = lax.dot_general(
        rows_ref[...], rows_ref[...], (((1,), (1,)), ((), ())), preferred_element_type=f32
    )


def cross_gram_body(got_ref, other_ref, rows_ref, gram_ref):
    unpack(got_ref, rows_ref)
    gram_ref[...] = lax.dot_general(
        rows_ref[...], other_ref[...], (((1,), (1,)), ((), ())), preferred_element_type=f32
    )


def update_body(masked_ref, applied_ref, lagrange_ref, inter_ref, out_ref):
    masked = masked_ref[...]
    gradient = applied_ref[...].astype(f32) - jnp.dot(
        lagrange_ref[...], masked, preferred_element_type=f32
    )
    trial = (masked.astype(f32) - step_length * gradient).astype(bf16)
    following = 1.5 * trial.astype(f32) - 0.5 * jnp.dot(
        inter_ref[...], trial, preferred_element_type=f32
    )
    out_ref[...] = following.T.astype(bf16)


def swap(value, axis, bit):
    count = lax.axis_size(axis)
    return lax.ppermute(value, axis, [(i, i ^ bit) for i in range(count)])


def bits_of(axis):
    bit, bits = 1, []
    while bit < lax.axis_size(axis):
        bits.append(bit)
        bit *= 2
    return bits


def half(value, upper):
    size = value.shape[0] // 2
    return lax.dynamic_slice_in_dim(value, upper * size, size, 0)


def sum_everywhere(part):
    steps = [("comp", b) for b in bits_of("comp")] + [("orb", b) for b in bits_of("orb")]
    halving = len(bits_of("comp")) + 1
    value = part
    taken = []
    for axis, bit in steps[:halving]:
        upper = (lax.axis_index(axis) // bit) % 2
        got = swap(half(value, 1 - upper).astype(bf16), axis, bit)
        value = half(value, upper) + got.astype(f32)
        taken.append((axis, bit, upper))
    for axis, bit in steps[halving:]:
        sent = value.astype(bf16)
        value = sent.astype(f32) + swap(sent, axis, bit).astype(f32)
    return value, taken


def give_everywhere(value, taken):
    for axis, bit, upper in reversed(taken):
        got = swap(value, axis, bit)
        value = jnp.where(
            upper == 0,
            jnp.concatenate([value, got], axis=0),
            jnp.concatenate([got, value], axis=0),
        )
    return value


def local(psi, region_start, region_len, fine_mask, occupation, kinetic_taps, magic_taps, external):
    orbs, channels, slab, cells = psi.shape
    orb_count = lax.axis_size("orb")
    comp_count = lax.axis_size("comp")
    orbitals = orbs * orb_count
    piece = cells // orb_count
    coefs = channels * slab * piece
    groups = coefs // LANES
    grid_cells = slab * comp_count * cells
    first_plane = lax.axis_index("comp") * slab
    first_cell = lax.axis_index("orb") * piece
    first_orbital = lax.axis_index("orb") * orbs
    where = jnp.stack([first_orbital, first_plane]).astype(jnp.int32)
    fine = jnp.repeat(fine_mask, ZB, axis=1)

    packed_shape = jax.ShapeDtypeStruct((orb_count, groups, orbs, LANES), bf16)
    scratch = pltpu.VMEM((cells // LANES, orbs * channels * slab, LANES), f32)
    masked, packed = pl.pallas_call(
        functools.partial(mask_body, piece),
        out_shape=(jax.ShapeDtypeStruct(psi.shape, bf16), packed_shape),
        in_specs=[SMEM, SMEM, SMEM, VMEM, VMEM],
        out_specs=(VMEM, VMEM),
        scratch_shapes=[scratch],
        compiler_params=params(),
        name="mask_pack",
    )(where, region_start, region_len, psi, fine)

    ends = comp_count - 1
    before = lax.ppermute(masked, "comp", [(i, i + 1) for i in range(ends)])
    after = lax.ppermute(masked, "comp", [(i + 1, i) for i in range(ends)])
    masked_got = lax.all_to_all(packed, "orb", split_axis=0, concat_axis=0, tiled=True)

    values, total = pl.pallas_call(
        density_body,
        out_shape=(
            jax.ShapeDtypeStruct((orbs, slab, cells), f32),
            jax.ShapeDtypeStruct((slab, cells), f32),
        ),
        in_specs=[SMEM, SMEM, VMEM, VMEM],
        out_specs=(VMEM, VMEM),
        compiler_params=params(),
        name="values_density",
    )(where, occupation, masked, magic_matrix(magic_taps, cells))
    for bit in bits_of("orb"):
        total = total + swap(total, "orb", bit)
    potential = external - xc_factor * jnp.cbrt(total)
    density = lax.dynamic_slice_in_dim(total, first_cell, piece, 1)

    kinetic = pl.pallas_call(
        kinetic_body,
        out_shape=jax.ShapeDtypeStruct(psi.shape, f32),
        in_specs=[SMEM, SMEM, SMEM, VMEM, VMEM, VMEM, VMEM, VMEM],
        out_specs=VMEM,
        compiler_params=params(),
        name="kinetic",
    )(
        where,
        region_start,
        region_len,
        masked,
        before,
        after,
        depth_matrix(kinetic_taps, cells),
        plane_matrix(kinetic_taps, slab),
    )

    packed_applied = pl.pallas_call(
        functools.partial(applied_body, piece),
        out_shape=packed_shape,
        in_specs=[SMEM, SMEM, SMEM, VMEM, VMEM, VMEM, VMEM, VMEM],
        out_specs=VMEM,
        scratch_shapes=[scratch],
        compiler_params=params(),
        name="applied_pack",
    )(
        where,
        region_start,
        region_len,
        kinetic,
        values,
        potential,
        fine,
        adjoint_matrix(magic_taps, cells),
    )
    applied_got = lax.all_to_all(packed_applied, "orb", split_axis=0, concat_axis=0, tiled=True)

    row_shape = jax.ShapeDtypeStruct((orbitals, coefs), bf16)
    gram_shape = jax.ShapeDtypeStruct((orbitals, orbitals), f32)
    masked_rows, inter_part = pl.pallas_call(
        self_gram_body,
        out_shape=(row_shape, gram_shape),
        in_specs=[VMEM],
        out_specs=(VMEM, VMEM),
        compiler_params=params(),
        name="intersection",
    )(masked_got)
    inter, taken = sum_everywhere(inter_part)
    inter_round = give_everywhere((inter / grid_cells).astype(bf16), taken)

    applied_rows, lagrange_part = pl.pallas_call(
        cross_gram_body,
        out_shape=(row_shape, gram_shape),
        in_specs=[VMEM, VMEM],
        out_specs=(VMEM, VMEM),
        compiler_params=params(),
        name="lagrange",
    )(applied_got, masked_rows)
    lagrange, taken = sum_everywhere(lagrange_part)
    lagrange_round = give_everywhere((lagrange / grid_cells).astype(bf16), taken)

    width = 256
    following = pl.pallas_call(
        update_body,
        grid=(coefs // width,),
        out_shape=jax.ShapeDtypeStruct((coefs, orbitals), bf16),
        in_specs=[
            pl.BlockSpec((orbitals, width), lambda k: (0, k)),
            pl.BlockSpec((orbitals, width), lambda k: (0, k)),
            pl.BlockSpec((orbitals, orbitals), lambda k: (0, 0)),
            pl.BlockSpec((orbitals, orbitals), lambda k: (0, 0)),
        ],
        out_specs=pl.BlockSpec((width, orbitals), lambda k: (k, 0)),
        compiler_params=params(),
        name="update",
    )(masked_rows, applied_rows, lagrange_round, inter_round)
    psi_next = following.reshape(channels, slab, piece, orbitals).transpose(3, 0, 1, 2)
    return (density, psi_next)


def solution(mesh):
    return jax.shard_map(
        local,
        mesh=mesh,
        in_specs=(
            P("orb", None, "comp", None),
            P(),
            P(),
            P("comp", None),
            P(),
            P(),
            P(),
            P("comp", None),
        ),
        out_specs=(P("comp", "orb"), P(None, None, "comp", "orb")),
        check_vma=False,
    )
```

time: 301 us -> 127 us (0.42)
  waiting for transfers between devices: 141 us -> 49.6 us
  local copies, waits for them, and re-layouts: 78.1 us -> 10.1 us
  starting transfers between devices: 17.1 us -> 39.9 us
  blocking collectives: 22.3 us -> 0 us
  Pallas kernels: 0 us -> 20.5 us
  matrix products: 22.9 us -> 3.66 us
  between operations: 14.3 us -> 1.08 us
  other arithmetic: 4.44 us -> 1.14 us
    psum x1 -> x0, waiting for transfers between devices: 130 us -> none  [local(): lax.psum((intersection_part, lagrange_part), ('orb', 'comp'))]
    reshape x13 -> x4, local copies, waits for them, and re-layouts: 32.7 us -> 0.39 us  [the longest x3 0.3 us: plane_matrix(): parts.append(part.reshape(ch * slab, ch * slab))]
    ppermute x2 -> x21, waiting for transfers between devices: 0.01 us -> 26 us  [the longest x19 26 us: swap(): return lax.ppermute(value, axis, [(i, i ^ bit) for i in range(count)])]
    ppermute x2 -> x21, starting transfers between devices: 5.24 us -> 29.1 us  [the longest x19 25.4 us: swap(): return lax.ppermute(value, axis, [(i, i ^ bit) for i in range(count)])]
    psum x1 -> x0, blocking collectives: 22.3 us -> none  [local(): total = lax.psum(partial_density, 'orb')]
    pallas_call x0 -> x7, Pallas kernels: none -> 20.5 us  [the longest x1 5.36 us: local(): pl.pallas_call(functools.partial(applied_body, piece), out_shape=packed_s...]
    dot_general x12 -> x6, matrix products: 22.9 us -> 3.66 us  [the longest x3 1.73 us: plane_matrix(): jnp.einsum('jit,ted->eidj', onehot, taps, preferred_element_type=f32)]
    all_to_all x2, waiting for transfers between devices: 11.4 us -> 23.6 us  [the longest x1 23.6 us: local(): lax.all_to_all(packed_applied, 'orb', split_axis=0, concat_axis=0, tiled=...]
  transfers between devices with their start and end apart: 5 -> 23, of which waited for: 2 -> 16; matrix products, arithmetic and copies ran while one was open for 28% -> 7% of each run, Pallas kernels for 0% -> 9%
where the time goes in v1:
time: 127 us; the launch traced here: 126 us
  waiting for transfers between devices  49.6 us (39%)
  starting transfers between devices  39.9 us (31%)
  Pallas kernels  20.5 us (16%)
  local copies, waits for them, and re-layouts  10.1 us (8%)
  matrix products  3.66 us (3%)
    ppermute x19, waiting for transfers between devices, swap(): return lax.ppermute(value, axis, [(i, i ^ bit) for i in range(count)])  26 us
    ppermute x19, starting transfers between devices, swap(): return lax.ppermute(value, axis, [(i, i ^ bit) for i in range(count)])  25.4 us
    all_to_all x1, waiting for transfers between devices, local(): lax.all_to_all(packed_applied, 'orb', split_axis=0, concat_axis=0, tiled=...  23.6 us
    all_to_all x1, starting transfers between devices, local(): lax.all_to_all(packed, 'orb', split_axis=0, concat_axis=0, tiled=True)  6.65 us
    unnamed x29, local copies, waits for them, and re-layouts  5.58 us
    pallas_call x1, Pallas kernels, local(): pl.pallas_call(functools.partial(applied_body, piece), out_shape=packed_s...  5.36 us
    pallas_call x1, Pallas kernels, local(): pl.pallas_call(functools.partial(mask_body, piece), out_shape=(jax.ShapeD...  4.87 us
    pallas_call x1, Pallas kernels, local(): pl.pallas_call(update_body, grid=(coefs // width,), out_shape=jax.ShapeDt...  4.32 us
  transfers between devices with their start and end apart: 23, of which 16 were waited for; matrix products, arithmetic and copies ran while one was open for 7% of the time, Pallas kernels for 9%

profile of v1, /device:TPU:0, one launch (start us, length us, event | category | flops | bytes accessed | tf_op | source)
XLA Modules:
  0.0 126.0 jit_solution(807722496918936015)
XLA Ops:
  0.7 0.8 copy.10
  1.7 1.2 copy-done.1
  2.9 0.7 copy-done.6
  3.6 0.7 copy-done.8
  4.3 4.9 %mask_pack.1 = (bf16[64,4,16,128]{3,2,1,0:T(8,128)(2,1)S(1)}, bf16[8,8,64,128]{3,2,1,0:T(8,128)(2,1)}) custom-call(s32[2]{0:T(128)S(1)} %pad_add_fusion.where_ref, s32[512]{0:T(512)S(1)} %copy-done.6, s32[512]{0:T(512)S(1)} %copy-done.8, bf16[64,4,16,128]{3,2,1,0:T(8,128)(2,1)S(1)} %copy-done.1, s32[16,128]{1,0:T(8,128)S(1)} %reshape.95.fine_ref), custom_call_target="tpu_custom_call" | custom-call | tf_op jit(solution)/shard_map/mask_pack/pallas_call | solution.py:328
  9.1 2.4 %collective-permute-start.3 = (bf16[64,4,16,128]{3,2,1,0:T(8,128)(2,1)S(1)}, bf16[64,4,16,128]{3,2,1,0:T(8,128)(2,1)S(1)}, u32[]{:S(2)}, u32[]{:S(2)}) collective-permute-start(bf16[64,4,16,128]{3,2,1,0:T(8,128)(2,1)S(1)} %get-tuple-element.10.masked_ref), channel_id=1, source_target_pairs={{0,1},{1,2},{2,3},{4,5},{5,6},{6,7},{8,9},{9,10},{10,11},{12,13},{... | collective-permute-start | bytes 3145736 | tf_op jit(solution)/shard_map/ppermute | solution.py:339
  11.6 1.3 %collective-permute-start.4 = (bf16[64,4,16,128]{3,2,1,0:T(8,128)(2,1)S(1)}, bf16[64,4,16,128]{3,2,1,0:T(8,128)(2,1)}, u32[]{:S(2)}, u32[]{:S(2)}) collective-permute-start(bf16[64,4,16,128]{3,2,1,0:T(8,128)(2,1)S(1)} %get-tuple-element.10.masked_ref), channel_id=1, source_target_pairs={{1,0},{2,1},{3,2},{5,4},{6,5},{7,6},{9,8},{10,9},{11,10},{13,12},{... | collective-permute-start | bytes 3145736 | tf_op jit(solution)/shard_map/ppermute | solution.py:340
  12.9 6.6 %all-to-all-start = ((bf16[8,8,64,128]{3,2,1,0:T(8,128)(2,1)}), bf16[8,8,64,128]{3,2,1,0:T(8,128)(2,1)S(1)}, u32[]{:S(2)}, u32[]{:S(2)}) async-start(bf16[8,8,64,128]{3,2,1,0:T(8,128)(2,1)} %get-tuple-element.12), calls=%async_computation | async-start | bytes 2097152 | tf_op jit(solution)/shard_map/all_to_all | solution.py:341
  19.5 0.3 fusion.9
  19.8 1.4 %values_density.1 = (f32[64,16,128]{2,1,0:T(8,128)S(1)}, f32[16,128]{1,0:T(8,128)S(1)}) custom-call(s32[2]{0:T(128)S(1)} %pad_add_fusion.where_ref, s32[512]{0:T(512)S(1)} %copy-done.10, bf16[64,4,16,128]{3,2,1,0:T(8,128)(2,1)S(1)} %get-tuple-element.10.masked_ref, bf16[512,128]{1,0:T(8,128)(2,1)S(1)} %bitcast.66), custom_call_target="tpu_custom_call" | custom-call | tf_op jit(solution)/shard_map/values_density/pallas_call | solution.py:343
  21.3 0.8 copy-done.4
  22.1 2.0 %collective-permute-start = (f32[16,128]{1,0:T(8,128)S(1)}, f32[16,128]{1,0:T(8,128)S(1)}, u32[]{:S(2)}, u32[]{:S(2)}) collective-permute-start(f32[16,128]{1,0:T(8,128)S(1)} %get-tuple-element.11), channel_id=1, source_target_pairs={{0,4},{4,0},{8,12},{12,8},{16,20},{20,16},{24,28},{28,24},{1,5},{5... | collective-permute-start | bytes 24584 | tf_op jit(solution)/shard_map/ppermute | solution.py:268
  24.2 0.4 fusion.12
  24.5 0.3 convolution_convert_fusion
  24.8 0.4 fusion.10
  25.2 1.4 %fusion.6 = bf16[4,128,4,128]{3,0,2,1:T(4,128)(2,1)} fusion(s32[128,128]{1,0:T(8,128)S(1)} %fusion.25, bf16[29,4,4]{0,2,1:T(4,128)(2,1)S(1)} %copy-done), kind=kOutput, calls=%fused_computation.4 | convolution fusion | flops 15941632 | bytes 590752 | tf_op jit(solution)/shard_map/jit,ted->djei/dot_general | solution.py:35
  26.6 3.7 %collective-permute-start.1 = (f32[16,128]{1,0:T(8,128)S(1)}, f32[16,128]{1,0:T(8,128)S(1)}, u32[]{:S(2)}, u32[]{:S(2)}) collective-permute-start(f32[16,128]{1,0:T(8,128)S(1)} %add.137), channel_id=1, source_target_pairs={{0,8},{4,12},{8,0},{12,4},{16,24},{20,28},{24,16},{28,20},{1,9},{5... | collective-permute-start | bytes 24584 | tf_op jit(solution)/shard_map/ppermute | solution.py:268
  30.3 1.0 fusion.11
  31.3 0.1 copy.15
  31.5 0.1 reshape.100
  31.6 0.1 copy.13
  31.7 0.1 reshape.98
  31.8 1.0 copy.14
  32.9 3.5 %collective-permute-done.1 = f32[16,128]{1,0:T(8,128)S(1)} collective-permute-done((f32[16,128]{1,0:T(8,128)S(1)}, f32[16,128]{1,0:T(8,128)S(1)}, u32[]{:S(2)}, u32[]{:S(2)}) %collective-permute-start.1) | collective-permute-done | bytes 8224 | tf_op jit(solution)/shard_map/ppermute | solution.py:268
  36.4 5.7 %collective-permute-start.2 = (f32[16,128]{1,0:T(8,128)S(1)}, f32[16,128]{1,0:T(8,128)S(1)}, u32[]{:S(2)}, u32[]{:S(2)}) collective-permute-start(f32[16,128]{1,0:T(8,128)S(1)} %add.138), channel_id=1, source_target_pairs={{0,16},{4,20},{8,24},{12,28},{16,0},{20,4},{24,8},{28,12},{1,17},{... | collective-permute-start | bytes 24584 | tf_op jit(solution)/shard_map/ppermute | solution.py:268
  42.1 1.2 copy.12
  43.5 2.9 %collective-permute-done.2 = f32[16,128]{1,0:T(8,128)S(1)} collective-permute-done((f32[16,128]{1,0:T(8,128)S(1)}, f32[16,128]{1,0:T(8,128)S(1)}, u32[]{:S(2)}, u32[]{:S(2)}) %collective-permute-start.2) | collective-permute-done | bytes 8224 | tf_op jit(solution)/shard_map/ppermute | solution.py:268
  46.5 2.9 %kinetic.1.kinetic_ref = f32[64,4,16,128]{3,2,1,0:T(8,128)S(1)} custom-call(s32[2]{0:T(128)S(1)} %pad_add_fusion.where_ref, s32[512]{0:T(512)S(1)} %copy-done.7, s32[512]{0:T(512)S(1)} %copy-done.9, bf16[64,4,16,128]{3,2,1,0:T(8,128)(2,1)S(1)} %get-tuple-element.10.masked_ref, bf16[64,4,16,128]{3,2,1,0:T(8,128)(2,1)S(1)} %collective-permute-done.3.before_ref, ...), custom_call_target="tpu_custom_call" | custom-call | tf_op jit(solution)/shard_map/kinetic/pallas_call | solution.py:359
  49.4 5.4 %applied_pack.1 = bf16[8,8,64,128]{3,2,1,0:T(8,128)(2,1)} custom-call(s32[2]{0:T(128)S(1)} %pad_add_fusion.where_ref, s32[512]{0:T(512)S(1)} %copy-done.7, s32[512]{0:T(512)S(1)} %copy-done.9, f32[64,4,16,128]{3,2,1,0:T(8,128)S(1)} %kinetic.1.kinetic_ref, f32[64,16,128]{2,1,0:T(8,128)S(1)} %copy-done.5, f32[16,128]{1,0:T(8,128)S(1)} %get-tuple-element.18.potential_ref, ...), custom_call_target="tpu_custom_call" | custom-call | tf_op jit(solution)/shard_map/applied_pack/pallas_call | solution.py:377
  54.8 4.2 %all-to-all-start.1 = ((bf16[8,8,64,128]{3,2,1,0:T(8,128)(2,1)}), bf16[8,8,64,128]{3,2,1,0:T(8,128)(2,1)S(1)}, u32[]{:S(2)}, u32[]{:S(2)}) async-start(bf16[8,8,64,128]{3,2,1,0:T(8,128)(2,1)} %applied_pack.1), calls=%async_computation.1 | async-start | bytes 2097152 | tf_op jit(solution)/shard_map/all_to_all | solution.py:395
  59.0 0.8 intersection.1
  59.8 1.0 copy-done.2
  60.8 0.7 dynamic-slice_convert_fusion
  61.5 0.2 collective-permute-start.13
  61.7 23.6 %all-to-all-done.1.got_ref = bf16[8,8,64,128]{3,2,1,0:T(8,128)(2,1)S(1)} async-done(((bf16[8,8,64,128]{3,2,1,0:T(8,128)(2,1)}), bf16[8,8,64,128]{3,2,1,0:T(8,128)(2,1)S(1)}, u32[]{:S(2)}, u32[]{:S(2)}) %all-to-all-start.1) | async-done | bytes 1048608 | tf_op jit(solution)/shard_map/all_to_all | solution.py:395
  85.3 0.8 lagrange.1
  86.2 0.3 copy-done.3
  86.7 2.2 %collective-permute-start.14 = (bf16[128,512]{1,0:T(8,128)(2,1)S(1)}, bf16[128,512]{1,0:T(8,128)(2,1)S(1)}, u32[]{:S(2)}, u32[]{:S(2)}) collective-permute-start(bf16[128,512]{1,0:T(8,128)(2,1)S(1)} %dynamic-slice_convert_fusion.2), channel_id=1, source_target_pairs={{0,2},{1,3},{2,0},{3,1},{4,6},{5,7},{6,4},{7,5},{8,10},{9,11},{10,... | collective-permute-start | bytes 393224 | tf_op jit(solution)/shard_map/ppermute | solution.py:268
  89.0 1.1 collective-permute-start.6
  90.1 3.1 %collective-permute-done.14 = bf16[128,512]{1,0:T(8,128)(2,1)S(1)} collective-permute-done((bf16[128,512]{1,0:T(8,128)(2,1)S(1)}, bf16[128,512]{1,0:T(8,128)(2,1)S(1)}, u32[]{:S(2)}, u32[]{:S(2)}) %collective-permute-start.14) | collective-permute-done | bytes 131104 | tf_op jit(solution)/shard_map/ppermute | solution.py:268
  93.2 1.5 %collective-permute-start.15 = (bf16[64,512]{1,0:T(8,128)(2,1)S(1)}, bf16[64,512]{1,0:T(8,128)(2,1)S(1)}, u32[]{:S(2)}, u32[]{:S(2)}) collective-permute-start(bf16[64,512]{1,0:T(8,128)(2,1)S(1)} %dynamic-slice_convert_fusion.4), channel_id=1, source_target_pairs={{0,4},{4,0},{8,12},{12,8},{16,20},{20,16},{24,28},{28,24},{1,5},{5... | collective-permute-start | bytes 196616 | tf_op jit(solution)/shard_map/ppermute | solution.py:268
  94.7 0.8 collective-permute-done.6
  95.6 1.5 %collective-permute-start.7 = (bf16[64,512]{1,0:T(8,128)(2,1)S(1)}, bf16[64,512]{1,0:T(8,128)(2,1)S(1)}, u32[]{:S(2)}, u32[]{:S(2)}) collective-permute-start(bf16[64,512]{1,0:T(8,128)(2,1)S(1)} %dynamic-slice_convert_fusion.5), channel_id=1, source_target_pairs={{0,4},{4,0},{8,12},{12,8},{16,20},{20,16},{24,28},{28,24},{1,5},{5... | collective-permute-start | bytes 196616 | tf_op jit(solution)/shard_map/ppermute | solution.py:268
  97.1 0.5 collective-permute-done.15
  97.7 2.3 %collective-permute-done.7 = bf16[64,512]{1,0:T(8,128)(2,1)S(1)} collective-permute-done((bf16[64,512]{1,0:T(8,128)(2,1)S(1)}, bf16[64,512]{1,0:T(8,128)(2,1)S(1)}, u32[]{:S(2)}, u32[]{:S(2)}) %collective-permute-start.7) | collective-permute-done | bytes 65568 | tf_op jit(solution)/shard_map/ppermute | solution.py:268
  100.0 2.5 %collective-permute-done.16 = bf16[64,512]{1,0:T(8,128)(2,1)S(1)} collective-permute-done((bf16[64,512]{1,0:T(8,128)(2,1)S(1)}, bf16[64,512]{1,0:T(8,128)(2,1)S(1)}, u32[]{:S(2)}, u32[]{:S(2)}) %collective-permute-start.16) | collective-permute-done | bytes 65568 | tf_op jit(solution)/shard_map/ppermute | solution.py:268
  102.6 0.6 collective-permute-start.17
  103.1 1.9 %collective-permute-done.8 = bf16[64,512]{1,0:T(8,128)(2,1)S(1)} collective-permute-done((bf16[64,512]{1,0:T(8,128)(2,1)S(1)}, bf16[64,512]{1,0:T(8,128)(2,1)S(1)}, u32[]{:S(2)}, u32[]{:S(2)}) %collective-permute-start.8) | collective-permute-done | bytes 65568 | tf_op jit(solution)/shard_map/ppermute | solution.py:268
  105.0 0.6 collective-permute-start.9
  105.6 2.7 %collective-permute-done.17 = bf16[64,512]{1,0:T(8,128)(2,1)S(1)} collective-permute-done((bf16[64,512]{1,0:T(8,128)(2,1)S(1)}, bf16[64,512]{1,0:T(8,128)(2,1)S(1)}, u32[]{:S(2)}, u32[]{:S(2)}) %collective-permute-start.17) | collective-permute-done | bytes 65568 | tf_op jit(solution)/shard_map/ppermute | solution.py:268
  108.4 1.5 %collective-permute-start.18 = (bf16[64,512]{1,0:T(8,128)(2,1)S(1)}, bf16[64,512]{1,0:T(8,128)(2,1)S(1)}, u32[]{:S(2)}, u32[]{:S(2)}) collective-permute-start(bf16[64,512]{1,0:T(8,128)(2,1)S(1)} %multiply_convert_fusion), channel_id=1, source_target_pairs={{0,4},{4,0},{8,12},{12,8},{16,20},{20,16},{24,28},{28,24},{1,5},{5... | collective-permute-start | bytes 196616 | tf_op jit(solution)/shard_map/ppermute | solution.py:268
  109.9 0.5 collective-permute-done.9
  110.4 1.2 collective-permute-start.10
  111.6 1.1 collective-permute-done.18
  112.7 1.6 %collective-permute-start.19 = (bf16[128,512]{1,0:T(8,128)(2,1)S(1)}, bf16[128,512]{1,0:T(8,128)(2,1)S(1)}, u32[]{:S(2)}, u32[]{:S(2)}) collective-permute-start(bf16[128,512]{1,0:T(8,128)(2,1)S(1)} %maximum_select_fusion.5), channel_id=1, source_target_pairs={{0,2},{1,3},{2,0},{3,1},{4,6},{5,7},{6,4},{7,5},{8,10},{9,11},{10,... | collective-permute-start | bytes 393224 | tf_op jit(solution)/shard_map/ppermute | solution.py:268
  114.3 0.4 collective-permute-done.10
  114.7 1.6 %collective-permute-start.11 = (bf16[128,512]{1,0:T(8,128)(2,1)S(1)}, bf16[128,512]{1,0:T(8,128)(2,1)S(1)}, u32[]{:S(2)}, u32[]{:S(2)}) collective-permute-start(bf16[128,512]{1,0:T(8,128)(2,1)S(1)} %maximum_select_fusion.4), channel_id=1, source_target_pairs={{0,2},{1,3},{2,0},{3,1},{4,6},{5,7},{6,4},{7,5},{8,10},{9,11},{10,... | collective-permute-start | bytes 393224 | tf_op jit(solution)/shard_map/ppermute | solution.py:268
  116.3 1.5 %collective-permute-done.19 = bf16[128,512]{1,0:T(8,128)(2,1)S(1)} collective-permute-done((bf16[128,512]{1,0:T(8,128)(2,1)S(1)}, bf16[128,512]{1,0:T(8,128)(2,1)S(1)}, u32[]{:S(2)}, u32[]{:S(2)}) %collective-permute-start.19) | collective-permute-done | bytes 131104 | tf_op jit(solution)/shard_map/ppermute | solution.py:268
  117.9 1.8 %collective-permute-done.11 = bf16[128,512]{1,0:T(8,128)(2,1)S(1)} collective-permute-done((bf16[128,512]{1,0:T(8,128)(2,1)S(1)}, bf16[128,512]{1,0:T(8,128)(2,1)S(1)}, u32[]{:S(2)}, u32[]{:S(2)}) %collective-permute-start.11) | collective-permute-done | bytes 131104 | tf_op jit(solution)/shard_map/ppermute | solution.py:268
  119.9 0.7 constant_dynamic-slice_fusion
  120.6 0.2 maximum_select_fusion.1.inter_ref
  120.8 0.6 collective-permute-done.12
  121.4 0.2 maximum_select_fusion.lagrange_ref
  121.6 4.3 %update.1 = bf16[1024,512]{1,0:T(8,128)(2,1)} custom-call(bf16[512,1024]{1,0:T(8,128)(2,1)S(1)} %get-tuple-element.13.other_ref.masked_ref, bf16[512,1024]{1,0:T(8,128)(2,1)S(1)} %get-tuple-element.15.applied_ref, bf16[512,512]{1,0:T(8,128)(2,1)S(1)} %maximum_select_fusion.lagrange_ref, bf16[512,512]{1,0:T(8,128)(2,1)S(1)} %maximum_select_fusion.1.inter_ref), custom_call_target="tpu_custom_call" | custom-call | tf_op jit(solution)/shard_map/update/pallas_call | solution.py:422
  (68 shorter events, 1.7 us)
Async XLA Ops:
  0.6 23.5 %copy-start = (bf16[29,4,4]{0,2,1:T(4,128)(2,1)S(1)}, bf16[29,4,4]{0,2,1:T(4,128)(2,1)}, u32[]{:S(2)}) copy-start(bf16[29,4,4]{0,2,1:T(4,128)(2,1)} %param.13) | copy-start | bytes 2788
  0.6 18.9 %copy-start.12 = (bf16[16,4]{0,1:T(4,128)(2,1)S(1)}, bf16[16,4]{0,1:T(4,128)(2,1)}, u32[]{:S(2)}) copy-start(bf16[16,4]{0,1:T(4,128)(2,1)} %param.14) | copy-start | bytes 388
  0.7 19.2 %copy-start.10 = (s32[512]{0:T(512)S(1)}, s32[512]{0:T(512)}, u32[]{:S(2)}) copy-start(s32[512]{0:T(512)} %occ_ref.1) | copy-start | bytes 6148
  1.7 1.2 copy-start.1
  2.9 0.7 copy-start.6
  3.6 0.7 copy-start.8
  9.1 37.3 %collective-permute-start.3 = (bf16[64,4,16,128]{3,2,1,0:T(8,128)(2,1)S(1)}, bf16[64,4,16,128]{3,2,1,0:T(8,128)(2,1)S(1)}, u32[]{:S(2)}, u32[]{:S(2)}) collective-permute-start(bf16[64,4,16,128]{3,2,1,0:T(8,128)(2,1)S(1)} %get-tuple-element.10.masked_ref), channel_id=1, source_target_pairs={{0,1},{1,2},{2,3},{4,5},{5,6},{6,7},{8,9},{9,10},{10,11},{12,13},{... | collective-permute-start | bytes 3145736 | tf_op jit(solution)/shard_map/ppermute | solution.py:339
  11.6 34.9 %collective-permute-start.4 = (bf16[64,4,16,128]{3,2,1,0:T(8,128)(2,1)S(1)}, bf16[64,4,16,128]{3,2,1,0:T(8,128)(2,1)}, u32[]{:S(2)}, u32[]{:S(2)}) collective-permute-start(bf16[64,4,16,128]{3,2,1,0:T(8,128)(2,1)S(1)} %get-tuple-element.10.masked_ref), channel_id=1, source_target_pairs={{1,0},{2,1},{3,2},{5,4},{6,5},{7,6},{9,8},{10,9},{11,10},{13,12},{... | collective-permute-start | bytes 3145736 | tf_op jit(solution)/shard_map/ppermute | solution.py:340
  12.9 41.9 %all-to-all-start = ((bf16[8,8,64,128]{3,2,1,0:T(8,128)(2,1)}), bf16[8,8,64,128]{3,2,1,0:T(8,128)(2,1)S(1)}, u32[]{:S(2)}, u32[]{:S(2)}) async-start(bf16[8,8,64,128]{3,2,1,0:T(8,128)(2,1)} %get-tuple-element.12), calls=%async_computation | async-start | bytes 2097152 | tf_op jit(solution)/shard_map/all_to_all | solution.py:341
  21.3 0.8 copy-start.4
  22.1 4.5 %collective-permute-start = (f32[16,128]{1,0:T(8,128)S(1)}, f32[16,128]{1,0:T(8,128)S(1)}, u32[]{:S(2)}, u32[]{:S(2)}) collective-permute-start(f32[16,128]{1,0:T(8,128)S(1)} %get-tuple-element.11), channel_id=1, source_target_pairs={{0,4},{4,0},{8,12},{12,8},{16,20},{20,16},{24,28},{28,24},{1,5},{5... | collective-permute-start | bytes 24584 | tf_op jit(solution)/shard_map/ppermute | solution.py:268
  24.8 21.6 %copy-start.11 = (f32[16,128]{1,0:T(8,128)S(1)}, f32[16,128]{1,0:T(8,128)}, u32[]{:S(2)}) copy-start(f32[16,128]{1,0:T(8,128)} %param.15) | copy-start | bytes 24580
  24.8 21.6 %copy-start.7 = (s32[512]{0:T(512)S(1)}, s32[512]{0:T(512)}, u32[]{:S(2)}) copy-start(s32[512]{0:T(512)} %start_ref.5) | copy-start | bytes 6148
  24.8 21.6 %copy-start.9 = (s32[512]{0:T(512)S(1)}, s32[512]{0:T(512)}, u32[]{:S(2)}) copy-start(s32[512]{0:T(512)} %len_ref.5) | copy-start | bytes 6148
  26.6 9.7 %collective-permute-start.1 = (f32[16,128]{1,0:T(8,128)S(1)}, f32[16,128]{1,0:T(8,128)S(1)}, u32[]{:S(2)}, u32[]{:S(2)}) collective-permute-start(f32[16,128]{1,0:T(8,128)S(1)} %add.137), channel_id=1, source_target_pairs={{0,8},{4,12},{8,0},{12,4},{16,24},{20,28},{24,16},{28,20},{1,9},{5... | collective-permute-start | bytes 24584 | tf_op jit(solution)/shard_map/ppermute | solution.py:268
  36.4 10.0 %collective-permute-start.2 = (f32[16,128]{1,0:T(8,128)S(1)}, f32[16,128]{1,0:T(8,128)S(1)}, u32[]{:S(2)}, u32[]{:S(2)}) collective-permute-start(f32[16,128]{1,0:T(8,128)S(1)} %add.138), channel_id=1, source_target_pairs={{0,16},{4,20},{8,24},{12,28},{16,0},{20,4},{24,8},{28,12},{1,17},{... | collective-permute-start | bytes 24584 | tf_op jit(solution)/shard_map/ppermute | solution.py:268
  46.5 2.9 %copy-start.5 = (f32[64,16,128]{2,1,0:T(8,128)S(1)}, f32[64,16,128]{2,1,0:T(8,128)}, u32[]{:S(2)}) copy-start(f32[64,16,128]{2,1,0:T(8,128)} %copy-done.4) | copy-start | bytes 1572868
  54.8 30.6 %all-to-all-start.1 = ((bf16[8,8,64,128]{3,2,1,0:T(8,128)(2,1)}), bf16[8,8,64,128]{3,2,1,0:T(8,128)(2,1)S(1)}, u32[]{:S(2)}, u32[]{:S(2)}) async-start(bf16[8,8,64,128]{3,2,1,0:T(8,128)(2,1)} %applied_pack.1), calls=%async_computation.1 | async-start | bytes 2097152 | tf_op jit(solution)/shard_map/all_to_all | solution.py:395
  59.8 1.0 copy-start.2
  61.5 24.7 %collective-permute-start.13 = (bf16[256,512]{1,0:T(8,128)(2,1)}, bf16[256,512]{1,0:T(8,128)(2,1)S(1)}, u32[]{:S(2)}, u32[]{:S(2)}) collective-permute-start(bf16[256,512]{1,0:T(8,128)(2,1)} %dynamic-slice_convert_fusion), channel_id=1, source_target_pairs={{0,1},{1,0},{2,3},{3,2},{4,5},{5,4},{6,7},{7,6},{8,9},{9,8},{10,11... | collective-permute-start | bytes 786440 | tf_op jit(solution)/shard_map/ppermute | solution.py:268
  85.3 1.2 copy-start.3
  86.2 2.7 %collective-permute-start.5 = (bf16[256,512]{1,0:T(8,128)(2,1)S(1)}, bf16[256,512]{1,0:T(8,128)(2,1)S(1)}, u32[]{:S(2)}, u32[]{:S(2)}) collective-permute-start(bf16[256,512]{1,0:T(8,128)(2,1)S(1)} %dynamic-slice_convert_fusion.1), channel_id=1, source_target_pairs={{0,1},{1,0},{2,3},{3,2},{4,5},{5,4},{6,7},{7,6},{8,9},{9,8},{10,11... | collective-permute-start | bytes 786440 | tf_op jit(solution)/shard_map/ppermute | solution.py:268
  86.7 6.5 %collective-permute-start.14 = (bf16[128,512]{1,0:T(8,128)(2,1)S(1)}, bf16[128,512]{1,0:T(8,128)(2,1)S(1)}, u32[]{:S(2)}, u32[]{:S(2)}) collective-permute-start(bf16[128,512]{1,0:T(8,128)(2,1)S(1)} %dynamic-slice_convert_fusion.2), channel_id=1, source_target_pairs={{0,2},{1,3},{2,0},{3,1},{4,6},{5,7},{6,4},{7,5},{8,10},{9,11},{10,... | collective-permute-start | bytes 393224 | tf_op jit(solution)/shard_map/ppermute | solution.py:268
  89.0 6.5 %collective-permute-start.6 = (bf16[128,512]{1,0:T(8,128)(2,1)S(1)}, bf16[128,512]{1,0:T(8,128)(2,1)S(1)}, u32[]{:S(2)}, u32[]{:S(2)}) collective-permute-start(bf16[128,512]{1,0:T(8,128)(2,1)S(1)} %dynamic-slice_convert_fusion.3), channel_id=1, source_target_pairs={{0,2},{1,3},{2,0},{3,1},{4,6},{5,7},{6,4},{7,5},{8,10},{9,11},{10,... | collective-permute-start | bytes 393224 | tf_op jit(solution)/shard_map/ppermute | solution.py:268
  93.2 4.3 %collective-permute-start.15 = (bf16[64,512]{1,0:T(8,128)(2,1)S(1)}, bf16[64,512]{1,0:T(8,128)(2,1)S(1)}, u32[]{:S(2)}, u32[]{:S(2)}) collective-permute-start(bf16[64,512]{1,0:T(8,128)(2,1)S(1)} %dynamic-slice_convert_fusion.4), channel_id=1, source_target_pairs={{0,4},{4,0},{8,12},{12,8},{16,20},{20,16},{24,28},{28,24},{1,5},{5... | collective-permute-start | bytes 196616 | tf_op jit(solution)/shard_map/ppermute | solution.py:268
  95.6 4.3 %collective-permute-start.7 = (bf16[64,512]{1,0:T(8,128)(2,1)S(1)}, bf16[64,512]{1,0:T(8,128)(2,1)S(1)}, u32[]{:S(2)}, u32[]{:S(2)}) collective-permute-start(bf16[64,512]{1,0:T(8,128)(2,1)S(1)} %dynamic-slice_convert_fusion.5), channel_id=1, source_target_pairs={{0,4},{4,0},{8,12},{12,8},{16,20},{20,16},{24,28},{28,24},{1,5},{5... | collective-permute-start | bytes 196616 | tf_op jit(solution)/shard_map/ppermute | solution.py:268
  97.6 5.0 %collective-permute-start.16 = (bf16[64,512]{1,0:T(8,128)(2,1)S(1)}, bf16[64,512]{1,0:T(8,128)(2,1)S(1)}, u32[]{:S(2)}, u32[]{:S(2)}) collective-permute-start(bf16[64,512]{1,0:T(8,128)(2,1)S(1)} %add_convert_fusion.1), channel_id=1, source_target_pairs={{0,8},{4,12},{8,0},{12,4},{16,24},{20,28},{24,16},{28,20},{1,9},{5... | collective-permute-start | bytes 196616 | tf_op jit(solution)/shard_map/ppermute | solution.py:268
  99.9 5.0 %collective-permute-start.8 = (bf16[64,512]{1,0:T(8,128)(2,1)S(1)}, bf16[64,512]{1,0:T(8,128)(2,1)S(1)}, u32[]{:S(2)}, u32[]{:S(2)}) collective-permute-start(bf16[64,512]{1,0:T(8,128)(2,1)S(1)} %add_convert_fusion.3), channel_id=1, source_target_pairs={{0,8},{4,12},{8,0},{12,4},{16,24},{20,28},{24,16},{28,20},{1,9},{5... | collective-permute-start | bytes 196616 | tf_op jit(solution)/shard_map/ppermute | solution.py:268
  102.6 5.8 %collective-permute-start.17 = (bf16[64,512]{1,0:T(8,128)(2,1)S(1)}, bf16[64,512]{1,0:T(8,128)(2,1)S(1)}, u32[]{:S(2)}, u32[]{:S(2)}) collective-permute-start(bf16[64,512]{1,0:T(8,128)(2,1)S(1)} %add_convert_fusion), channel_id=1, source_target_pairs={{0,16},{4,20},{8,24},{12,28},{16,0},{20,4},{24,8},{28,12},{1,17},{... | collective-permute-start | bytes 196616 | tf_op jit(solution)/shard_map/ppermute | solution.py:268
  105.0 5.3 %collective-permute-start.9 = (bf16[64,512]{1,0:T(8,128)(2,1)S(1)}, bf16[64,512]{1,0:T(8,128)(2,1)S(1)}, u32[]{:S(2)}, u32[]{:S(2)}) collective-permute-start(bf16[64,512]{1,0:T(8,128)(2,1)S(1)} %add_convert_fusion.2), channel_id=1, source_target_pairs={{0,16},{4,20},{8,24},{12,28},{16,0},{20,4},{24,8},{28,12},{1,17},{... | collective-permute-start | bytes 196616 | tf_op jit(solution)/shard_map/ppermute | solution.py:268
  108.4 4.3 %collective-permute-start.18 = (bf16[64,512]{1,0:T(8,128)(2,1)S(1)}, bf16[64,512]{1,0:T(8,128)(2,1)S(1)}, u32[]{:S(2)}, u32[]{:S(2)}) collective-permute-start(bf16[64,512]{1,0:T(8,128)(2,1)S(1)} %multiply_convert_fusion), channel_id=1, source_target_pairs={{0,4},{4,0},{8,12},{12,8},{16,20},{20,16},{24,28},{28,24},{1,5},{5... | collective-permute-start | bytes 196616 | tf_op jit(solution)/shard_map/ppermute | solution.py:268
  110.4 4.3 %collective-permute-start.10 = (bf16[64,512]{1,0:T(8,128)(2,1)S(1)}, bf16[64,512]{1,0:T(8,128)(2,1)S(1)}, u32[]{:S(2)}, u32[]{:S(2)}) collective-permute-start(bf16[64,512]{1,0:T(8,128)(2,1)S(1)} %multiply_convert_fusion.1), channel_id=1, source_target_pairs={{0,4},{4,0},{8,12},{12,8},{16,20},{20,16},{24,28},{28,24},{1,5},{5... | collective-permute-start | bytes 196616 | tf_op jit(solution)/shard_map/ppermute | solution.py:268
  112.7 5.0 %collective-permute-start.19 = (bf16[128,512]{1,0:T(8,128)(2,1)S(1)}, bf16[128,512]{1,0:T(8,128)(2,1)S(1)}, u32[]{:S(2)}, u32[]{:S(2)}) collective-permute-start(bf16[128,512]{1,0:T(8,128)(2,1)S(1)} %maximum_select_fusion.5), channel_id=1, source_target_pairs={{0,2},{1,3},{2,0},{3,1},{4,6},{5,7},{6,4},{7,5},{8,10},{9,11},{10,... | collective-permute-start | bytes 393224 | tf_op jit(solution)/shard_map/ppermute | solution.py:268
  114.7 5.0 %collective-permute-start.11 = (bf16[128,512]{1,0:T(8,128)(2,1)S(1)}, bf16[128,512]{1,0:T(8,128)(2,1)S(1)}, u32[]{:S(2)}, u32[]{:S(2)}) collective-permute-start(bf16[128,512]{1,0:T(8,128)(2,1)S(1)} %maximum_select_fusion.4), channel_id=1, source_target_pairs={{0,2},{1,3},{2,0},{3,1},{4,6},{5,7},{6,4},{7,5},{8,10},{9,11},{10,... | collective-permute-start | bytes 393224 | tf_op jit(solution)/shard_map/ppermute | solution.py:268
  117.8 2.8 %collective-permute-start.20 = (bf16[256,512]{1,0:T(8,128)(2,1)S(1)}, bf16[256,512]{1,0:T(8,128)(2,1)S(1)}, u32[]{:S(2)}, u32[]{:S(2)}) collective-permute-start(bf16[256,512]{1,0:T(8,128)(2,1)S(1)} %maximum_select_fusion.3), channel_id=1, source_target_pairs={{0,1},{1,0},{2,3},{3,2},{4,5},{5,4},{6,7},{7,6},{8,9},{9,8},{10,11... | collective-permute-start | bytes 786440 | tf_op jit(solution)/shard_map/ppermute | solution.py:268
  119.8 1.6 %collective-permute-start.12 = (bf16[256,512]{1,0:T(8,128)(2,1)S(1)}, bf16[256,512]{1,0:T(8,128)(2,1)S(1)}, u32[]{:S(2)}, u32[]{:S(2)}) collective-permute-start(bf16[256,512]{1,0:T(8,128)(2,1)S(1)} %maximum_select_fusion.2), channel_id=1, source_target_pairs={{0,1},{1,0},{2,3},{3,2},{4,5},{5,4},{6,7},{7,6},{8,9},{9,8},{10,11... | collective-permute-start | bytes 786440 | tf_op jit(solution)/shard_map/ppermute | solution.py:268

commit v2 on v1

v2 whole, which is shorter than its diff:
```python
import functools

import jax
import jax.numpy as jnp
from jax import lax
from jax.experimental import pallas as pl
from jax.experimental.pallas import tpu as pltpu
from jax.sharding import PartitionSpec as P

ZB = 16
LANES = 128
CHUNK = 16
PAD = 8

xc_factor = 0.98474502
step_length = 0.1
f32 = jnp.float32
bf16 = jnp.bfloat16
VMEM = pl.BlockSpec(memory_space=pltpu.VMEM)
ANY = pl.BlockSpec(memory_space=pl.ANY)
SMEM = pl.BlockSpec(memory_space=pltpu.SMEM)


SMALL = pl.CostEstimate(flops=1024, bytes_accessed=1024, transcendentals=0)


def params(mib=20):
    return pltpu.CompilerParams(vmem_limit_bytes=mib * 2**20)


def band(window, length, shift, sign, taps):
    count = taps.shape[0]
    offset = sign * (jnp.arange(window)[:, None] - jnp.arange(length)[None, :]) + shift
    onehot = (offset[:, :, None] == jnp.arange(count)[None, None, :]).astype(bf16)
    return onehot


def depth_matrix(taps, cells):
    onehot = band(cells, cells, 14, 1, taps)
    kernel = jnp.einsum("jit,ted->djei", onehot, taps, preferred_element_type=f32).astype(bf16)
    ch = taps.shape[1]
    return kernel.reshape(ch * cells, ch * cells)


def plane_matrix(taps, slab):
    ch = taps.shape[1]
    parts = []
    for block in (-1, 0, 1):
        onehot = band(slab, slab, 14 + block * slab, 1, taps)
        part = jnp.einsum("jit,ted->eidj", onehot, taps, preferred_element_type=f32).astype(bf16)
        parts.append(part.reshape(ch * slab, ch * slab))
    return jnp.concatenate(parts, axis=1)


def magic_matrix(magic, cells):
    onehot = band(cells, cells, 7, 1, magic)
    kernel = jnp.einsum("jit,td->dji", onehot, magic, preferred_element_type=f32).astype(bf16)
    return kernel.reshape(magic.shape[1] * cells, cells)


def adjoint_matrix(magic, cells):
    onehot = band(cells, cells, 7, -1, magic)
    kernel = jnp.einsum("jit,te->jei", onehot, magic, preferred_element_type=f32).astype(bf16)
    return kernel.reshape(cells, magic.shape[1] * cells)


def spread(scratch, row, value):
    slab = value.shape[0]
    for tile in range(value.shape[1] // LANES):
        scratch[tile, pl.ds(pl.multiple_of(row, 8), slab), :] = value[
            :, tile * LANES : (tile + 1) * LANES
        ]


def pack(scratch, staged, out_ref, sems, orbs, rows, piece):
    pieces = staged.shape[0]
    blocks = LANES // piece
    pitch = scratch.shape[1] // orbs
    lane = lax.broadcasted_iota(jnp.int32, (CHUNK, LANES), 1) // piece

    def group(g, carry):
        for tile in range(pieces // blocks):
            for start in range(0, orbs, CHUNK):
                held = [
                    scratch[
                        tile, pl.ds(start * pitch + g * blocks + c, CHUNK, stride=pitch), :
                    ].astype(bf16)
                    for c in range(blocks)
                ]
                bit = 1
                while bit < blocks:
                    low_lane = (lane & bit) == 0
                    for c in range(blocks):
                        if c & bit:
                            continue
                        low, high = held[c], held[c | bit]
                        held[c] = jnp.where(low_lane, low, pltpu.roll(high, bit * piece, 1))
                        held[c | bit] = jnp.where(
                            low_lane, pltpu.roll(low, LANES - bit * piece, 1), high
                        )
                    bit *= 2
                for c in range(blocks):
                    row = pl.multiple_of(g * orbs + start, CHUNK)
                    staged[tile * blocks + c, pl.ds(row, CHUNK), :] = held[c]
        leave(g).start()
        return carry

    def leave(g):
        share = pl.ds(pl.multiple_of(g * orbs, CHUNK), orbs)
        return pltpu.make_async_copy(
            staged.at[:, share, :], out_ref.at[:, share, :], sems.at[g]
        )

    def finish(g, carry):
        leave(g).wait()
        return carry

    lax.fori_loop(0, rows // blocks, group, 0)
    lax.fori_loop(0, rows // blocks, finish, 0)


def fine_cells(fine_ref, cells):
    blocks = fine_ref.shape[0]
    spot = lax.broadcasted_iota(jnp.int32, (blocks, cells), 1) // ZB
    onehot = (spot == lax.broadcasted_iota(jnp.int32, (blocks, cells), 0)).astype(f32)
    wide = lax.dot_general(
        fine_ref[...].astype(f32), onehot, (((0,), (0,)), ((), ())), preferred_element_type=f32
    )
    return wide > 0.5


def region(table_ref, orbs, o):
    spot = lax.axis_index("orb") * orbs + o
    return table_ref[0, spot], table_ref[0, spot] + table_ref[1, spot]


def mask_body(
    piece,
    table_ref,
    psi_hbm,
    fine_hbm,
    magic_ref,
    masked_ref,
    out_ref,
    scratch,
    staged,
    psi_ref,
    fine_ref,
    sems,
    in_sems,
):
    orbs, channels, slab, cells = psi_ref.shape
    rows = channels * slab
    pitch = scratch.shape[1] // orbs

    def arrive(k):
        share = pl.ds(pl.multiple_of(k * CHUNK, CHUNK), CHUNK)
        return pltpu.make_async_copy(psi_hbm.at[share], psi_ref.at[share], in_sems.at[k])

    fine_copy = pltpu.make_async_copy(fine_hbm, fine_ref, in_sems.at[orbs // CHUNK])
    fine_copy.start()
    for k in range(orbs // CHUNK):
        arrive(k).start()
    first_orbital = lax.axis_index("orb") * orbs
    plane = lax.axis_index("comp") * slab + lax.broadcasted_iota(jnp.int32, (slab, cells), 0)
    fine_copy.wait()
    fine = fine_cells(fine_ref, cells)

    def chunk(k, total):
        o = pl.multiple_of(k * CHUNK, CHUNK)
        arrive(k).wait()
        for i in range(CHUNK):
            least, limit = region(table_ref, orbs, o + i)
            inside = (plane >= least) & (plane < limit)
            both = inside & fine
            for e in range(channels):
                keep = inside if e == 0 else both
                value = jnp.where(keep, psi_ref[o + i, e].astype(f32), 0.0)
                masked_ref[o + i, e] = value.astype(bf16)
                spread(scratch, (o + i) * pitch + e * slab, value)
        lhs = jnp.concatenate(
            [
                masked_ref[pl.ds(o, CHUNK), d].reshape(CHUNK * slab, cells)
                for d in range(channels)
            ],
            axis=1,
        )
        result = jnp.dot(lhs, magic_ref[...], preferred_element_type=f32)
        for i in range(CHUNK):
            part = result[i * slab : (i + 1) * slab]
            total = total + table_ref[2, first_orbital + o + i].astype(f32) * part * part
        return total

    density = lax.fori_loop(0, orbs // CHUNK, chunk, jnp.zeros((slab, cells), f32))
    coarse = density.astype(bf16)
    rest = (density - coarse.astype(f32)).astype(bf16)
    body = orbs * rows * piece // LANES
    for j in range(staged.shape[0]):
        row = body
        for part in (coarse, rest):
            for tile in range(cells // LANES):
                staged[j, row : row + slab, :] = part[:, tile * LANES : (tile + 1) * LANES]
                row += slab
    extra = pltpu.make_async_copy(
        staged.at[:, body:, :], out_ref.at[:, body:, :], sems.at[rows * piece // LANES]
    )
    extra.start()
    pack(scratch, staged, out_ref, sems, orbs, rows, piece)
    extra.wait()


def kinetic_body(
    masked_ref, before_ref, after_ref, depth_ref, plane_ref, magic_ref, out_ref, values_ref
):
    orbs, channels, slab, cells = masked_ref.shape
    rows = channels * slab

    def chunk(k, carry):
        o = pl.multiple_of(k * CHUNK, CHUNK)
        lhs = jnp.concatenate(
            [
                masked_ref[pl.ds(o, CHUNK), d].reshape(CHUNK * slab, cells)
                for d in range(channels)
            ],
            axis=1,
        )
        along_z = jnp.dot(lhs, depth_ref[...], preferred_element_type=f32)
        values_ref[pl.ds(o, CHUNK)] = jnp.dot(
            lhs, magic_ref[...], preferred_element_type=f32
        ).reshape(CHUNK, slab, cells)
        for i in range(0, CHUNK, 2):
            window = jnp.concatenate(
                [
                    jnp.concatenate(
                        [
                            ref[o + i + b].reshape(rows, cells)
                            for ref in (before_ref, masked_ref, after_ref)
                        ],
                        axis=0,
                    )
                    for b in range(2)
                ],
                axis=1,
            )
            along_x = jnp.dot(plane_ref[...], window, preferred_element_type=f32)
            for b in range(2):
                for e in range(channels):
                    out_ref[o + i + b, e] = (
                        along_x[e * slab : (e + 1) * slab, b * cells : (b + 1) * cells]
                        + along_z[
                            (i + b) * slab : (i + b + 1) * slab, e * cells : (e + 1) * cells
                        ]
                    )
        return carry

    lax.fori_loop(0, orbs // CHUNK, chunk, 0)


def applied_body(
    piece,
    table_ref,
    kinetic_ref,
    values_ref,
    potential_ref,
    fine_ref,
    adjoint_ref,
    out_ref,
    scratch,
    staged,
    sems,
):
    orbs, channels, slab, cells = kinetic_ref.shape
    rows = channels * slab
    pitch = scratch.shape[1] // orbs
    plane = lax.axis_index("comp") * slab + lax.broadcasted_iota(jnp.int32, (slab, cells), 0)
    fine = fine_cells(fine_ref, cells)
    potential = potential_ref[...]

    def chunk(k, carry):
        o = pl.multiple_of(k * CHUNK, CHUNK)
        weighted = (potential[None] * values_ref[pl.ds(o, CHUNK)]).astype(bf16)
        back = jnp.dot(
            weighted.reshape(CHUNK * slab, cells), adjoint_ref[...], preferred_element_type=f32
        )
        for i in range(CHUNK):
            least, limit = region(table_ref, orbs, o + i)
            inside = (plane >= least) & (plane < limit)
            both = inside & fine
            for e in range(channels):
                keep = inside if e == 0 else both
                value = (
                    kinetic_ref[o + i, e]
                    + back[i * slab : (i + 1) * slab, e * cells : (e + 1) * cells]
                )
                spread(scratch, (o + i) * pitch + e * slab, jnp.where(keep, value, 0.0))
        return carry

    lax.fori_loop(0, orbs // CHUNK, chunk, 0)
    pack(scratch, staged, out_ref, sems, orbs, rows, piece)


def unpack(got_ref, rows_ref):
    sources = got_ref.shape[0]
    orbs = rows_ref.shape[0] // sources
    for i in range(sources):
        for g in range(rows_ref.shape[1] // LANES):
            rows_ref[pl.ds(i * orbs, orbs), pl.ds(g * LANES, LANES)] = got_ref[
                i, g * orbs : (g + 1) * orbs, :
            ]


def gram_halves(left_ref, right_ref, kept_ref, sent_ref):
    half = kept_ref.shape[0]
    mine = lax.axis_index("comp") % 2
    for place, ref in ((mine, kept_ref), (1 - mine, sent_ref)):
        row = pl.multiple_of(place * half, half)
        ref[...] = lax.dot_general(
            left_ref[pl.ds(row, half), :],
            right_ref[...],
            (((1,), (1,)), ((), ())),
            preferred_element_type=f32,
        ).astype(ref.dtype)


def self_gram_body(got_ref, rows_ref, kept_ref, sent_ref):
    unpack(got_ref, rows_ref)
    gram_halves(rows_ref, rows_ref, kept_ref, sent_ref)


def cross_gram_body(got_ref, other_ref, rows_ref, kept_ref, sent_ref):
    unpack(got_ref, rows_ref)
    gram_halves(rows_ref, other_ref, kept_ref, sent_ref)


def update_body(masked_ref, applied_ref, lagrange_ref, inter_ref, out_ref):
    masked = masked_ref[...]
    gradient = applied_ref[...].astype(f32) - jnp.dot(
        lagrange_ref[...], masked, preferred_element_type=f32
    )
    trial = (masked.astype(f32) - step_length * gradient).astype(bf16)
    following = 1.5 * trial.astype(f32) - 0.5 * jnp.dot(
        inter_ref[...], trial, preferred_element_type=f32
    )
    out_ref[...] = following.astype(bf16).T


def swap(value, axis, bit):
    count = lax.axis_size(axis)
    return lax.ppermute(value, axis, [(i, i ^ bit) for i in range(count)])


def bits_of(axis):
    bit, bits = 1, []
    while bit < lax.axis_size(axis):
        bits.append(bit)
        bit *= 2
    return bits


def stages():
    comp, orb = bits_of("comp"), bits_of("orb")
    groups = [[("comp", comp[0])]]
    for index, bit in enumerate(comp[1:]):
        groups.append([("comp", bit), ("orb", orb[index])])
    return groups, [("orb", bit) for bit in orb[len(comp) - 1 :]]


def place(group):
    return sum(((lax.axis_index(a) // b) % 2) << k for k, (a, b) in enumerate(group))


def pass_on(value, group, distance):
    flips = {}
    for k, (axis, bit) in enumerate(group):
        if distance >> k & 1:
            flips[axis] = flips.get(axis, 0) ^ bit
    axes = tuple(a for a in ("orb", "comp") if a in flips)
    if len(axes) == 1:
        return swap(value, axes[0], flips[axes[0]])
    sizes = [lax.axis_size(a) for a in axes]
    pairs = []
    for i in range(sizes[0]):
        for j in range(sizes[1]):
            to = (i ^ flips[axes[0]], j ^ flips[axes[1]])
            pairs.append((i * sizes[1] + j, to[0] * sizes[1] + to[1]))
    return lax.ppermute(value, axes, pairs)


def add_partner(kept, sent):
    return kept + pass_on(sent, stages()[0][0], 1).astype(f32)


def share_out(value):
    for group in stages()[0][1:]:
        members = 1 << len(group)
        size = value.shape[0] // members
        me = place(group)
        sent = value.astype(bf16)
        total = lax.dynamic_slice_in_dim(value, me * size, size, 0)
        for distance in range(1, members):
            share = lax.dynamic_slice_in_dim(sent, (me ^ distance) * size, size, 0)
            total = total + pass_on(share, group, distance).astype(f32)
        value = total
    return value


def exchange(value, step):
    axis, bit = step
    sent = value.astype(bf16)
    return sent.astype(f32) + swap(sent, axis, bit).astype(f32)


def give_everywhere(value):
    for group in reversed(stages()[0]):
        members = 1 << len(group)
        size = value.shape[0]
        me = place(group)
        got = [value] + [pass_on(value, group, d) for d in range(1, members)]
        whole = jnp.zeros((members * size,) + value.shape[1:], value.dtype)
        for distance, block in enumerate(got):
            whole = lax.dynamic_update_slice_in_dim(whole, block, (me ^ distance) * size, 0)
        value = whole
    return value


def local(psi, region_start, region_len, fine_mask, occupation, kinetic_taps, magic_taps, external):
    orbs, channels, slab, cells = psi.shape
    orb_count = lax.axis_size("orb")
    comp_count = lax.axis_size("comp")
    orbitals = orbs * orb_count
    piece = cells // orb_count
    coefs = channels * slab * piece
    groups = coefs // LANES
    grid_cells = slab * comp_count * cells
    first_cell = lax.axis_index("orb") * piece
    table = jnp.stack([region_start, region_len, occupation])
    fine = fine_mask.T

    scratch = pltpu.VMEM((cells // LANES, orbs * (channels * slab + PAD), LANES), f32)
    body_rows = orbs * coefs // LANES
    extra = slab * (cells // LANES)
    magic_forward = magic_matrix(magic_taps, cells)
    packed_shape = (orb_count, body_rows + 2 * extra, LANES)
    masked, packed = pl.pallas_call(
        functools.partial(mask_body, piece),
        out_shape=(
            jax.ShapeDtypeStruct(psi.shape, bf16),
            jax.ShapeDtypeStruct(packed_shape, bf16),
        ),
        in_specs=[SMEM, ANY, ANY, VMEM],
        out_specs=(VMEM, ANY),
        scratch_shapes=[
            scratch,
            pltpu.VMEM(packed_shape, bf16),
            pltpu.VMEM(psi.shape, bf16),
            pltpu.VMEM(fine.shape, fine.dtype),
            pltpu.SemaphoreType.DMA((groups + 1,)),
            pltpu.SemaphoreType.DMA((orbs // CHUNK + 1,)),
        ],
        compiler_params=params(),
        name="mask_values_pack",
        cost_estimate=SMALL,
    )(table, psi, fine, magic_forward)

    ends = comp_count - 1
    before = lax.ppermute(masked, "comp", [(i, i + 1) for i in range(ends)])
    after = lax.ppermute(masked, "comp", [(i + 1, i) for i in range(ends)])
    masked_got = lax.all_to_all(packed, "orb", split_axis=0, concat_axis=0, tiled=True)
    parts = masked_got[:, body_rows:].reshape(orb_count * 2, cells // LANES, slab, LANES)
    total = jnp.sum(parts.astype(f32), axis=0).transpose(1, 0, 2).reshape(slab, cells)
    potential = external - xc_factor * jnp.cbrt(total)
    density = lax.dynamic_slice_in_dim(total, first_cell, piece, 1)

    kinetic, values = pl.pallas_call(
        kinetic_body,
        out_shape=(
            jax.ShapeDtypeStruct(psi.shape, f32),
            jax.ShapeDtypeStruct((orbs, slab, cells), f32),
        ),
        in_specs=[VMEM] * 6,
        out_specs=(VMEM, VMEM),
        compiler_params=params(),
        name="kinetic",
        cost_estimate=SMALL,
    )(
        masked,
        before,
        after,
        depth_matrix(kinetic_taps, cells),
        plane_matrix(kinetic_taps, slab),
        magic_forward,
    )

    packed_applied = pl.pallas_call(
        functools.partial(applied_body, piece),
        out_shape=jax.ShapeDtypeStruct((orb_count, body_rows, LANES), bf16),
        in_specs=[SMEM] + [VMEM] * 5,
        out_specs=ANY,
        scratch_shapes=[
            scratch,
            pltpu.VMEM((orb_count, body_rows, LANES), bf16),
            pltpu.SemaphoreType.DMA((groups,)),
        ],
        compiler_params=params(),
        name="applied_pack",
        cost_estimate=SMALL,
    )(
        table,
        kinetic,
        values,
        potential,
        fine,
        adjoint_matrix(magic_taps, cells),
    )
    applied_got = lax.all_to_all(packed_applied, "orb", split_axis=0, concat_axis=0, tiled=True)

    row_shape = jax.ShapeDtypeStruct((orbitals, coefs), bf16)
    kept_shape = jax.ShapeDtypeStruct((orbitals // 2, orbitals), f32)
    sent_shape = jax.ShapeDtypeStruct((orbitals // 2, orbitals), bf16)
    masked_rows, *inter_part = pl.pallas_call(
        self_gram_body,
        out_shape=(row_shape, kept_shape, sent_shape),
        in_specs=[VMEM],
        out_specs=(VMEM, VMEM, VMEM),
        compiler_params=params(),
        name="intersection",
        cost_estimate=SMALL,
    )(masked_got)
    inter = share_out(add_partner(*inter_part))

    applied_got, inter = lax.optimization_barrier((applied_got, inter))
    applied_rows, *lagrange_part = pl.pallas_call(
        cross_gram_body,
        out_shape=(row_shape, kept_shape, sent_shape),
        in_specs=[VMEM, VMEM],
        out_specs=(VMEM, VMEM, VMEM),
        compiler_params=params(),
        name="lagrange",
        cost_estimate=SMALL,
    )(applied_got, masked_rows)
    lagrange = share_out(add_partner(*lagrange_part))
    both = jnp.concatenate([lagrange, inter], axis=1)
    for step in stages()[1]:
        both = exchange(both, step)
    both = give_everywhere((both / grid_cells).astype(bf16))

    width = 512
    following = pl.pallas_call(
        update_body,
        grid=(coefs // width,),
        out_shape=jax.ShapeDtypeStruct((coefs, orbitals), bf16),
        in_specs=[
            pl.BlockSpec((orbitals, width), lambda k: (0, k)),
            pl.BlockSpec((orbitals, width), lambda k: (0, k)),
            pl.BlockSpec((orbitals, orbitals), lambda k: (0, 0)),
            pl.BlockSpec((orbitals, orbitals), lambda k: (0, 1)),
        ],
        out_specs=pl.BlockSpec((width, orbitals), lambda k: (k, 0)),
        compiler_params=params(),
        name="update",
        cost_estimate=SMALL,
    )(masked_rows, applied_rows, both, both)
    psi_next = following.reshape(channels, slab, piece, orbitals).transpose(3, 0, 1, 2)
    return (density, psi_next)


def solution(mesh):
    return jax.shard_map(
        local,
        mesh=mesh,
        in_specs=(
            P("orb", None, "comp", None),
            P(),
            P(),
            P("comp", None),
            P(),
            P(),
            P(),
            P("comp", None),
        ),
        out_specs=(P("comp", "orb"), P(None, None, "comp", "orb")),
        check_vma=False,
    )
```

time: 127 us -> 116 us (0.913)
  starting transfers between devices: 39.9 us -> 28.3 us
  Pallas kernels: 20.5 us -> 16.8 us
  waiting for transfers between devices: 49.6 us -> 52.3 us
  local copies, waits for them, and re-layouts: 10.1 us -> 11.9 us
    ppermute x19 -> x11, starting transfers between devices: 25.4 us -> 9.69 us  [swap(): return lax.ppermute(value, axis, [(i, i ^ bit) for i in range(count)])]
    all_to_all x1, waiting for transfers between devices: 23.6 us -> 10.9 us  [local(): lax.all_to_all(packed_applied, 'orb', split_axis=0, concat_axis=0, tiled=...]
    all_to_all x1, waiting for transfers between devices: 0.01 us -> 11.9 us  [local(): lax.all_to_all(packed, 'orb', split_axis=0, concat_axis=0, tiled=True)]
    ppermute x0 -> x3, waiting for transfers between devices: none -> 9.11 us  [pass_on(): return lax.ppermute(value, axes, pairs)]
    ppermute x19 -> x11, waiting for transfers between devices: 26 us -> 20.4 us  [swap(): return lax.ppermute(value, axis, [(i, i ^ bit) for i in range(count)])]
    ppermute x0 -> x3, starting transfers between devices: none -> 4.9 us  [pass_on(): return lax.ppermute(value, axes, pairs)]
    unnamed x29 -> x30, local copies, waits for them, and re-layouts: 5.58 us -> 9.91 us
    pallas_call x5 -> x4, Pallas kernels: 11.3 us -> 9.13 us  [the longest x1 4.42 us: local(): pl.pallas_call(functools.partial(applied_body, piece), out_shape=jax.Shap...]
  transfers between devices with their start and end apart: 23 -> 18, of which waited for: 16 -> 13; matrix products, arithmetic and copies ran while one was open for 7% -> 5% of each run, Pallas kernels for 9% -> 3%
where the time goes in v2:
time: 116 us
  waiting for transfers between devices  52.3 us (45%)
  starting transfers between devices  28.3 us (24%)
  Pallas kernels  16.8 us (14%)
  local copies, waits for them, and re-layouts  11.9 us (10%)
  matrix products  2.9 us (2%)
  other arithmetic  2.28 us (2%)
    ppermute x11, waiting for transfers between devices, swap(): return lax.ppermute(value, axis, [(i, i ^ bit) for i in range(count)])  20.4 us
    all_to_all x1, waiting for transfers between devices, local(): lax.all_to_all(packed, 'orb', split_axis=0, concat_axis=0, tiled=True)  11.9 us
    all_to_all x1, waiting for transfers between devices, local(): lax.all_to_all(packed_applied, 'orb', split_axis=0, concat_axis=0, tiled=...  10.9 us
    unnamed x30, local copies, waits for them, and re-layouts  9.91 us
    ppermute x11, starting transfers between devices, swap(): return lax.ppermute(value, axis, [(i, i ^ bit) for i in range(count)])  9.69 us
    ppermute x3, waiting for transfers between devices, pass_on(): return lax.ppermute(value, axes, pairs)  9.11 us
    all_to_all x1, starting transfers between devices, local(): lax.all_to_all(packed, 'orb', split_axis=0, concat_axis=0, tiled=True)  7.26 us
    ppermute x3, starting transfers between devices, pass_on(): return lax.ppermute(value, axes, pairs)  4.9 us
  transfers between devices with their start and end apart: 18, of which 13 were waited for; matrix products, arithmetic and copies ran while one was open for 5% of the time, Pallas kernels for 3%

profile of v2, /device:TPU:0, one launch (start us, length us, event | category | flops | bytes accessed | tf_op | source)
XLA Modules:
  0.0 115.5 jit_solution(2397805447165032796)
XLA Ops:
  0.7 1.0 fusion.9
  1.6 0.7 pad_add_fusion.table_ref
  2.4 1.2 %copy-done.2 = bf16[64,4,16,128]{3,2,1,0:T(8,128)(2,1)S(1)} copy-done((bf16[64,4,16,128]{3,2,1,0:T(8,128)(2,1)S(1)}, bf16[64,4,16,128]{3,2,1,0:T(8,128)(2,1)}, u32[]{:S(2)}) %copy-start.2) | copy-done | bytes 1048600
  3.6 0.7 copy-done.10
  4.3 4.7 %mask_values_pack.1 = (bf16[64,4,16,128]{3,2,1,0:T(8,128)(2,1)S(1)}, bf16[8,544,128]{2,1,0:T(8,128)(2,1)}) custom-call(s32[3,512]{1,0:T(4,128)S(1)} %pad_add_fusion.table_ref, bf16[64,4,16,128]{3,2,1,0:T(8,128)(2,1)S(1)} %copy-done.2, s32[8,16]{1,0:T(8,128)S(1)} %bitcast.72, bf16[512,128]{1,0:T(8,128)(2,1)S(1)} %bitcast.69), custom_call_target="tpu_custom_call" | custom-call | flops 1024 | bytes 1024 | tf_op jit(solution)/shard_map/mask_values_pack/pallas_call | solution.py:444
  9.0 7.3 %all-to-all-start = ((bf16[8,544,128]{2,1,0:T(8,128)(2,1)}), bf16[8,544,128]{2,1,0:T(8,128)(2,1)S(1)}, u32[]{:S(2)}, u32[]{:S(2)}) async-start(bf16[8,544,128]{2,1,0:T(8,128)(2,1)} %get-tuple-element.14), calls=%async_computation | async-start | bytes 2228224 | tf_op jit(solution)/shard_map/all_to_all | solution.py:468
  16.3 1.5 %collective-permute-start = (bf16[64,4,16,128]{3,2,1,0:T(8,128)(2,1)S(1)}, bf16[64,4,16,128]{3,2,1,0:T(8,128)(2,1)S(1)}, u32[]{:S(2)}, u32[]{:S(2)}) collective-permute-start(bf16[64,4,16,128]{3,2,1,0:T(8,128)(2,1)S(1)} %get-tuple-element.16.masked_ref), channel_id=1, source_target_pairs={{0,1},{1,2},{2,3},{4,5},{5,6},{6,7},{8,9},{9,10},{10,11},{12,13},{... | collective-permute-start | bytes 3145736 | tf_op jit(solution)/shard_map/ppermute | solution.py:466
  17.8 1.3 %collective-permute-start.1 = (bf16[64,4,16,128]{3,2,1,0:T(8,128)(2,1)S(1)}, bf16[64,4,16,128]{3,2,1,0:T(8,128)(2,1)}, u32[]{:S(2)}, u32[]{:S(2)}) collective-permute-start(bf16[64,4,16,128]{3,2,1,0:T(8,128)(2,1)S(1)} %get-tuple-element.16.masked_ref), channel_id=1, source_target_pairs={{1,0},{2,1},{3,2},{5,4},{6,5},{7,6},{9,8},{10,9},{11,10},{13,12},{... | collective-permute-start | bytes 3145736 | tf_op jit(solution)/shard_map/ppermute | solution.py:467
  19.2 0.4 fusion.12
  19.5 0.6 fusion.6
  20.1 0.2 copy.11
  20.4 0.9 copy.23
  21.2 0.1 copy.14
  21.4 0.1 reshape.117
  21.5 0.4 fusion.11
  21.8 0.1 copy.13
  22.0 0.1 reshape.116
  22.1 0.4 fusion.10
  22.5 0.1 copy.12
  22.6 0.1 reshape.115
  22.8 0.3 convolution_convert_fusion
  23.1 0.1 pad_maximum_fusion.1.plane_ref
  23.2 1.0 copy-done.5
  24.2 1.0 copy-done.1
  25.2 1.2 %copy-done.4 = bf16[64,4,16,128]{3,2,1,0:T(8,128)(2,1)S(1)} copy-done((bf16[64,4,16,128]{3,2,1,0:T(8,128)(2,1)S(1)}, bf16[64,4,16,128]{3,2,1,0:T(8,128)(2,1)}, u32[]{:S(2)}) %copy-start.4) | copy-done | bytes 1048600
  26.4 1.2 %copy-done.6 = bf16[64,4,16,128]{3,2,1,0:T(8,128)(2,1)S(1)} copy-done((bf16[64,4,16,128]{3,2,1,0:T(8,128)(2,1)S(1)}, bf16[64,4,16,128]{3,2,1,0:T(8,128)(2,1)}, u32[]{:S(2)}) %copy-start.6) | copy-done | bytes 1048600
  27.7 3.1 %kinetic.1 = (f32[64,4,16,128]{3,2,1,0:T(8,128)S(1)}, f32[64,16,128]{2,1,0:T(8,128)S(1)}) custom-call(bf16[64,4,16,128]{3,2,1,0:T(8,128)(2,1)S(1)} %copy-done.4, bf16[64,4,16,128]{3,2,1,0:T(8,128)(2,1)S(1)} %copy-done.6, bf16[64,4,16,128]{3,2,1,0:T(8,128)(2,1)} %collective-permute-done.1.after_ref, bf16[512,512]{1,0:T(8,128)(2,1)S(1)} %bitcast.68, ...), custom_call_target="tpu_custom_call" | custom-call | flops 1024 | bytes 1024 | tf_op jit(solution)/shard_map/kinetic/pallas_call | solution.py:474
  30.8 0.8 copy-done.8
  31.6 11.9 %all-to-all-done.got_ref = bf16[8,544,128]{2,1,0:T(8,128)(2,1)S(1)} async-done(((bf16[8,544,128]{2,1,0:T(8,128)(2,1)}), bf16[8,544,128]{2,1,0:T(8,128)(2,1)S(1)}, u32[]{:S(2)}, u32[]{:S(2)}) %all-to-all-start) | async-done | bytes 1114144 | tf_op jit(solution)/shard_map/all_to_all | solution.py:468
  43.6 1.0 copy-done.9
  44.6 4.4 %applied_pack.1 = bf16[8,512,128]{2,1,0:T(8,128)(2,1)} custom-call(s32[3,512]{1,0:T(4,128)S(1)} %pad_add_fusion.table_ref, f32[64,4,16,128]{3,2,1,0:T(8,128)S(1)} %get-tuple-element.17.kinetic_ref, f32[64,16,128]{2,1,0:T(8,128)S(1)} %copy-done.9, f32[16,128]{1,0:T(8,128)S(1)} %multiply_subtract_fusion.potential_ref, s32[8,16]{1,0:T(8,128)S(1)} %bitcast.73, ...), custom_call_target="tpu_custom_call" | custom-call | flops 1024 | bytes 1024 | tf_op jit(solution)/shard_map/applied_pack/pallas_call | solution.py:494
  49.0 3.7 %all-to-all-start.1 = ((bf16[8,512,128]{2,1,0:T(8,128)(2,1)}), bf16[8,512,128]{2,1,0:T(8,128)(2,1)S(1)}, u32[]{:S(2)}, u32[]{:S(2)}) async-start(bf16[8,512,128]{2,1,0:T(8,128)(2,1)} %applied_pack.1), calls=%async_computation.1 | async-start | bytes 2097152 | tf_op jit(solution)/shard_map/all_to_all | solution.py:515
  52.7 0.8 intersection.1
  53.5 0.8 copy-done.7
  54.3 2.4 %collective-permute-start.2 = (bf16[256,512]{1,0:T(8,128)(2,1)S(1)}, bf16[256,512]{1,0:T(8,128)(2,1)S(1)}, u32[]{:S(2)}, u32[]{:S(2)}) collective-permute-start(bf16[256,512]{1,0:T(8,128)(2,1)S(1)} %get-tuple-element.20), channel_id=1, source_target_pairs={{0,1},{1,0},{2,3},{3,2},{4,5},{5,4},{6,7},{7,6},{8,9},{9,8},{10,11... | collective-permute-start | bytes 786440 | tf_op jit(solution)/shard_map/ppermute | solution.py:349
  56.7 1.2 %collective-permute-done.2 = bf16[256,512]{1,0:T(8,128)(2,1)S(1)} collective-permute-done((bf16[256,512]{1,0:T(8,128)(2,1)S(1)}, bf16[256,512]{1,0:T(8,128)(2,1)S(1)}, u32[]{:S(2)}, u32[]{:S(2)}) %collective-permute-start.2) | collective-permute-done | bytes 262176 | tf_op jit(solution)/shard_map/ppermute | solution.py:349
  57.9 1.1 fusion.37
  59.0 1.6 %collective-permute-start.5 = (bf16[64,512]{1,0:T(8,128)(2,1)S(1)}, bf16[64,512]{1,0:T(8,128)(2,1)S(1)}, u32[]{:S(2)}, u32[]{:S(2)}) collective-permute-start(bf16[64,512]{1,0:T(8,128)(2,1)S(1)} %get-tuple-element.36), channel_id=1, source_target_pairs={{0,6},{1,7},{2,4},{3,5},{4,2},{5,3},{6,0},{7,1},{8,14},{9,15},{10,... | collective-permute-start | bytes 196616 | tf_op jit(solution)/shard_map/ppermute | solution.py:386
  60.6 0.3 collective-permute-start.4
  60.9 1.7 %collective-permute-start.3 = (bf16[64,512]{1,0:T(8,128)(2,1)S(1)}, bf16[64,512]{1,0:T(8,128)(2,1)S(1)}, u32[]{:S(2)}, u32[]{:S(2)}) collective-permute-start(bf16[64,512]{1,0:T(8,128)(2,1)S(1)} %get-tuple-element.35), channel_id=1, source_target_pairs={{0,2},{1,3},{2,0},{3,1},{4,6},{5,7},{6,4},{7,5},{8,10},{9,11},{10,... | collective-permute-start | bytes 196616 | tf_op jit(solution)/shard_map/ppermute | solution.py:349
  62.6 4.6 %collective-permute-done.5 = bf16[64,512]{1,0:T(8,128)(2,1)S(1)} collective-permute-done((bf16[64,512]{1,0:T(8,128)(2,1)S(1)}, bf16[64,512]{1,0:T(8,128)(2,1)S(1)}, u32[]{:S(2)}, u32[]{:S(2)}) %collective-permute-start.5) | collective-permute-done | bytes 65568 | tf_op jit(solution)/shard_map/ppermute | solution.py:386
  67.2 1.0 collective-permute-done.4
  68.2 10.9 %all-to-all-done.1.got_ref = bf16[8,512,128]{2,1,0:T(8,128)(2,1)S(1)} async-done(((bf16[8,512,128]{2,1,0:T(8,128)(2,1)}), bf16[8,512,128]{2,1,0:T(8,128)(2,1)S(1)}, u32[]{:S(2)}, u32[]{:S(2)}) %all-to-all-start.1) | async-done | bytes 1048608 | tf_op jit(solution)/shard_map/all_to_all | solution.py:515
  79.1 0.8 lagrange.1
  79.9 1.1 collective-permute-start.6
  81.0 1.2 %collective-permute-done.6 = bf16[256,512]{1,0:T(8,128)(2,1)S(1)} collective-permute-done((bf16[256,512]{1,0:T(8,128)(2,1)S(1)}, bf16[256,512]{1,0:T(8,128)(2,1)S(1)}, u32[]{:S(2)}, u32[]{:S(2)}) %collective-permute-start.6) | collective-permute-done | bytes 262176 | tf_op jit(solution)/shard_map/ppermute | solution.py:349
  82.2 0.1 fusion.36
  82.3 1.3 %collective-permute-start.9 = (bf16[64,512]{1,0:T(8,128)(2,1)S(1)}, bf16[64,512]{1,0:T(8,128)(2,1)S(1)}, u32[]{:S(2)}, u32[]{:S(2)}) collective-permute-start(bf16[64,512]{1,0:T(8,128)(2,1)S(1)} %get-tuple-element.33), channel_id=1, source_target_pairs={{0,6},{1,7},{2,4},{3,5},{4,2},{5,3},{6,0},{7,1},{8,14},{9,15},{10,... | collective-permute-start | bytes 196616 | tf_op jit(solution)/shard_map/ppermute | solution.py:386
  83.6 0.8 collective-permute-start.8
  84.4 1.5 %collective-permute-start.7 = (bf16[64,512]{1,0:T(8,128)(2,1)S(1)}, bf16[64,512]{1,0:T(8,128)(2,1)S(1)}, u32[]{:S(2)}, u32[]{:S(2)}) collective-permute-start(bf16[64,512]{1,0:T(8,128)(2,1)S(1)} %get-tuple-element.32), channel_id=1, source_target_pairs={{0,2},{1,3},{2,0},{3,1},{4,6},{5,7},{6,4},{7,5},{8,10},{9,11},{10,... | collective-permute-start | bytes 196616 | tf_op jit(solution)/shard_map/ppermute | solution.py:349
  85.9 2.3 %collective-permute-done.9 = bf16[64,512]{1,0:T(8,128)(2,1)S(1)} collective-permute-done((bf16[64,512]{1,0:T(8,128)(2,1)S(1)}, bf16[64,512]{1,0:T(8,128)(2,1)S(1)}, u32[]{:S(2)}, u32[]{:S(2)}) %collective-permute-start.9) | collective-permute-done | bytes 65568 | tf_op jit(solution)/shard_map/ppermute | solution.py:386
  88.2 0.8 collective-permute-done.7
  89.2 5.0 %collective-permute-done.10 = bf16[64,1024]{1,0:T(8,128)(2,1)S(1)} collective-permute-done((bf16[64,1024]{1,0:T(8,128)(2,1)S(1)}, bf16[64,1024]{1,0:T(8,128)(2,1)S(1)}, u32[]{:S(2)}, u32[]{:S(2)}) %collective-permute-start.10) | collective-permute-done | bytes 131104 | tf_op jit(solution)/shard_map/ppermute | solution.py:349
  94.2 0.2 collective-permute-start.11
  94.4 7.4 %collective-permute-done.11 = bf16[64,1024]{1,0:T(8,128)(2,1)S(1)} collective-permute-done((bf16[64,1024]{1,0:T(8,128)(2,1)S(1)}, bf16[64,1024]{1,0:T(8,128)(2,1)S(1)}, u32[]{:S(2)}, u32[]{:S(2)}) %collective-permute-start.11) | collective-permute-done | bytes 131104 | tf_op jit(solution)/shard_map/ppermute | solution.py:349
  101.9 0.4 collective-permute-start.12
  102.4 1.1 collective-permute-start.13
  103.5 2.0 %collective-permute-start.14 = (bf16[64,1024]{1,0:T(8,128)(2,1)S(1)}, bf16[64,1024]{1,0:T(8,128)(2,1)S(1)}, u32[]{:S(2)}, u32[]{:S(2)}) collective-permute-start(bf16[64,1024]{1,0:T(8,128)(2,1)S(1)} %get-tuple-element.27), channel_id=1, source_target_pairs={{0,6},{1,7},{2,4},{3,5},{4,2},{5,3},{6,0},{7,1},{8,14},{9,15},{10,... | collective-permute-start | bytes 393224 | tf_op jit(solution)/shard_map/ppermute | solution.py:386
  105.5 2.8 %collective-permute-done.12 = bf16[64,1024]{1,0:T(8,128)(2,1)S(1)} collective-permute-done((bf16[64,1024]{1,0:T(8,128)(2,1)S(1)}, bf16[64,1024]{1,0:T(8,128)(2,1)S(1)}, u32[]{:S(2)}, u32[]{:S(2)}) %collective-permute-start.12) | collective-permute-done | bytes 131104 | tf_op jit(solution)/shard_map/ppermute | solution.py:349
  108.3 2.2 %collective-permute-done.14 = bf16[64,1024]{1,0:T(8,128)(2,1)S(1)} collective-permute-done((bf16[64,1024]{1,0:T(8,128)(2,1)S(1)}, bf16[64,1024]{1,0:T(8,128)(2,1)S(1)}, u32[]{:S(2)}, u32[]{:S(2)}) %collective-permute-start.14) | collective-permute-done | bytes 131104 | tf_op jit(solution)/shard_map/ppermute | solution.py:386
  110.7 0.7 constant_dynamic-slice_fusion.6
  111.3 0.1 broadcast_in_dim.4
  111.5 1.0 collective-permute-done.15
  112.6 3.0 %update.1 = bf16[1024,512]{1,0:T(8,128)(2,1)} custom-call(bf16[512,1024]{1,0:T(8,128)(2,1)S(1)} %get-tuple-element.15.other_ref.masked_ref, bf16[512,1024]{1,0:T(8,128)(2,1)S(1)} %get-tuple-element.22.applied_ref, bf16[512,1024]{1,0:T(8,128)(2,1)S(1)} %constant_dynamic-update-slice_fusion.lagrange_ref.inter_ref, ...), custom_call_target="tpu_custom_call" | custom-call | flops 1024 | bytes 1024 | tf_op jit(solution)/shard_map/update/pallas_call | solution.py:548
  (50 shorter events, 0.7 us)
Async XLA Ops:
  0.6 18.5 %copy-start = (bf16[29,4,4]{0,2,1:T(4,128)(2,1)S(1)}, bf16[29,4,4]{0,2,1:T(4,128)(2,1)}, u32[]{:S(2)}) copy-start(bf16[29,4,4]{0,2,1:T(4,128)(2,1)} %param.13) | copy-start | bytes 2788
  2.4 1.2 %copy-start.2 = (bf16[64,4,16,128]{3,2,1,0:T(8,128)(2,1)S(1)}, bf16[64,4,16,128]{3,2,1,0:T(8,128)(2,1)}, u32[]{:S(2)}) copy-start(bf16[64,4,16,128]{3,2,1,0:T(8,128)(2,1)} %psi_hbm.1) | copy-start | bytes 3145732
  3.6 0.7 copy-start.10
  9.0 11.3 %copy-start.3 = (bf16[64,4,16,128]{3,2,1,0:T(8,128)(2,1)}, bf16[64,4,16,128]{3,2,1,0:T(8,128)(2,1)S(1)}, u32[]{:S(2)}) copy-start(bf16[64,4,16,128]{3,2,1,0:T(8,128)(2,1)S(1)} %get-tuple-element.16.masked_ref) | copy-start | bytes 3145732
  9.0 34.4 %all-to-all-start = ((bf16[8,544,128]{2,1,0:T(8,128)(2,1)}), bf16[8,544,128]{2,1,0:T(8,128)(2,1)S(1)}, u32[]{:S(2)}, u32[]{:S(2)}) async-start(bf16[8,544,128]{2,1,0:T(8,128)(2,1)} %get-tuple-element.14), calls=%async_computation | async-start | bytes 2228224 | tf_op jit(solution)/shard_map/all_to_all | solution.py:468
  16.3 6.5 %copy-start.13 = (bf16[16,4]{0,1:T(4,128)(2,1)S(1)}, bf16[16,4]{0,1:T(4,128)(2,1)}, u32[]{:S(2)}) copy-start(bf16[16,4]{0,1:T(4,128)(2,1)} %param.14) | copy-start | bytes 388
  16.3 6.9 %collective-permute-start = (bf16[64,4,16,128]{3,2,1,0:T(8,128)(2,1)S(1)}, bf16[64,4,16,128]{3,2,1,0:T(8,128)(2,1)S(1)}, u32[]{:S(2)}, u32[]{:S(2)}) collective-permute-start(bf16[64,4,16,128]{3,2,1,0:T(8,128)(2,1)S(1)} %get-tuple-element.16.masked_ref), channel_id=1, source_target_pairs={{0,1},{1,2},{2,3},{4,5},{5,6},{6,7},{8,9},{9,10},{10,11},{12,13},{... | collective-permute-start | bytes 3145736 | tf_op jit(solution)/shard_map/ppermute | solution.py:466
  17.8 6.3 %collective-permute-start.1 = (bf16[64,4,16,128]{3,2,1,0:T(8,128)(2,1)S(1)}, bf16[64,4,16,128]{3,2,1,0:T(8,128)(2,1)}, u32[]{:S(2)}, u32[]{:S(2)}) collective-permute-start(bf16[64,4,16,128]{3,2,1,0:T(8,128)(2,1)S(1)} %get-tuple-element.16.masked_ref), channel_id=1, source_target_pairs={{1,0},{2,1},{3,2},{5,4},{6,5},{7,6},{9,8},{10,9},{11,10},{13,12},{... | collective-permute-start | bytes 3145736 | tf_op jit(solution)/shard_map/ppermute | solution.py:467
  23.1 20.4 %copy-start.12 = (f32[16,128]{1,0:T(8,128)S(1)}, f32[16,128]{1,0:T(8,128)}, u32[]{:S(2)}) copy-start(f32[16,128]{1,0:T(8,128)} %param.15) | copy-start | bytes 24580
  23.1 20.5 %copy-start.11 = (s32[16,8]{0,1:T(8,128)S(1)}, s32[16,8]{0,1:T(8,128)}, u32[]{:S(2)}) copy-start(s32[16,8]{0,1:T(8,128)} %param.11) | copy-start | bytes 1540
  23.2 1.0 copy-start.5
  24.2 1.0 copy-start.1
  25.2 1.2 %copy-start.4 = (bf16[64,4,16,128]{3,2,1,0:T(8,128)(2,1)S(1)}, bf16[64,4,16,128]{3,2,1,0:T(8,128)(2,1)}, u32[]{:S(2)}) copy-start(bf16[64,4,16,128]{3,2,1,0:T(8,128)(2,1)} %copy-done.3) | copy-start | bytes 3145732
  26.4 1.2 %copy-start.6 = (bf16[64,4,16,128]{3,2,1,0:T(8,128)(2,1)S(1)}, bf16[64,4,16,128]{3,2,1,0:T(8,128)(2,1)}, u32[]{:S(2)}) copy-start(bf16[64,4,16,128]{3,2,1,0:T(8,128)(2,1)} %copy-done.5) | copy-start | bytes 3145732
  30.8 0.8 copy-start.8
  43.5 1.0 copy-start.9
  49.0 30.1 %all-to-all-start.1 = ((bf16[8,512,128]{2,1,0:T(8,128)(2,1)}), bf16[8,512,128]{2,1,0:T(8,128)(2,1)S(1)}, u32[]{:S(2)}, u32[]{:S(2)}) async-start(bf16[8,512,128]{2,1,0:T(8,128)(2,1)} %applied_pack.1), calls=%async_computation.1 | async-start | bytes 2097152 | tf_op jit(solution)/shard_map/all_to_all | solution.py:515
  53.5 0.8 copy-start.7
  54.3 3.6 %collective-permute-start.2 = (bf16[256,512]{1,0:T(8,128)(2,1)S(1)}, bf16[256,512]{1,0:T(8,128)(2,1)S(1)}, u32[]{:S(2)}, u32[]{:S(2)}) collective-permute-start(bf16[256,512]{1,0:T(8,128)(2,1)S(1)} %get-tuple-element.20), channel_id=1, source_target_pairs={{0,1},{1,0},{2,3},{3,2},{4,5},{5,4},{6,7},{7,6},{8,9},{9,8},{10,11... | collective-permute-start | bytes 786440 | tf_op jit(solution)/shard_map/ppermute | solution.py:349
  59.0 8.1 %collective-permute-start.5 = (bf16[64,512]{1,0:T(8,128)(2,1)S(1)}, bf16[64,512]{1,0:T(8,128)(2,1)S(1)}, u32[]{:S(2)}, u32[]{:S(2)}) collective-permute-start(bf16[64,512]{1,0:T(8,128)(2,1)S(1)} %get-tuple-element.36), channel_id=1, source_target_pairs={{0,6},{1,7},{2,4},{3,5},{4,2},{5,3},{6,0},{7,1},{8,14},{9,15},{10,... | collective-permute-start | bytes 196616 | tf_op jit(solution)/shard_map/ppermute | solution.py:386
  60.6 7.5 %collective-permute-start.4 = (bf16[64,512]{1,0:T(8,128)(2,1)S(1)}, bf16[64,512]{1,0:T(8,128)(2,1)S(1)}, u32[]{:S(2)}, u32[]{:S(2)}) collective-permute-start(bf16[64,512]{1,0:T(8,128)(2,1)S(1)} %get-tuple-element.37), channel_id=1, source_target_pairs={{0,4},{4,0},{8,12},{12,8},{16,20},{20,16},{24,28},{28,24},{1,5},{5... | collective-permute-start | bytes 196616 | tf_op jit(solution)/shard_map/ppermute | solution.py:349
  60.9 7.2 %collective-permute-start.3 = (bf16[64,512]{1,0:T(8,128)(2,1)S(1)}, bf16[64,512]{1,0:T(8,128)(2,1)S(1)}, u32[]{:S(2)}, u32[]{:S(2)}) collective-permute-start(bf16[64,512]{1,0:T(8,128)(2,1)S(1)} %get-tuple-element.35), channel_id=1, source_target_pairs={{0,2},{1,3},{2,0},{3,1},{4,6},{5,7},{6,4},{7,5},{8,10},{9,11},{10,... | collective-permute-start | bytes 196616 | tf_op jit(solution)/shard_map/ppermute | solution.py:349
  79.9 2.3 %collective-permute-start.6 = (bf16[256,512]{1,0:T(8,128)(2,1)S(1)}, bf16[256,512]{1,0:T(8,128)(2,1)S(1)}, u32[]{:S(2)}, u32[]{:S(2)}) collective-permute-start(bf16[256,512]{1,0:T(8,128)(2,1)S(1)} %get-tuple-element.24), channel_id=1, source_target_pairs={{0,1},{1,0},{2,3},{3,2},{4,5},{5,4},{6,7},{7,6},{8,9},{9,8},{10,11... | collective-permute-start | bytes 786440 | tf_op jit(solution)/shard_map/ppermute | solution.py:349
  82.3 5.9 %collective-permute-start.9 = (bf16[64,512]{1,0:T(8,128)(2,1)S(1)}, bf16[64,512]{1,0:T(8,128)(2,1)S(1)}, u32[]{:S(2)}, u32[]{:S(2)}) collective-permute-start(bf16[64,512]{1,0:T(8,128)(2,1)S(1)} %get-tuple-element.33), channel_id=1, source_target_pairs={{0,6},{1,7},{2,4},{3,5},{4,2},{5,3},{6,0},{7,1},{8,14},{9,15},{10,... | collective-permute-start | bytes 196616 | tf_op jit(solution)/shard_map/ppermute | solution.py:386
  83.6 4.6 %collective-permute-start.8 = (bf16[64,512]{1,0:T(8,128)(2,1)S(1)}, bf16[64,512]{1,0:T(8,128)(2,1)S(1)}, u32[]{:S(2)}, u32[]{:S(2)}) collective-permute-start(bf16[64,512]{1,0:T(8,128)(2,1)S(1)} %get-tuple-element.34), channel_id=1, source_target_pairs={{0,4},{4,0},{8,12},{12,8},{16,20},{20,16},{24,28},{28,24},{1,5},{5... | collective-permute-start | bytes 196616 | tf_op jit(solution)/shard_map/ppermute | solution.py:349
  84.4 4.6 %collective-permute-start.7 = (bf16[64,512]{1,0:T(8,128)(2,1)S(1)}, bf16[64,512]{1,0:T(8,128)(2,1)S(1)}, u32[]{:S(2)}, u32[]{:S(2)}) collective-permute-start(bf16[64,512]{1,0:T(8,128)(2,1)S(1)} %get-tuple-element.32), channel_id=1, source_target_pairs={{0,2},{1,3},{2,0},{3,1},{4,6},{5,7},{6,4},{7,5},{8,10},{9,11},{10,... | collective-permute-start | bytes 196616 | tf_op jit(solution)/shard_map/ppermute | solution.py:349
  89.1 5.1 %collective-permute-start.10 = (bf16[64,1024]{1,0:T(8,128)(2,1)S(1)}, bf16[64,1024]{1,0:T(8,128)(2,1)S(1)}, u32[]{:S(2)}, u32[]{:S(2)}) collective-permute-start(bf16[64,1024]{1,0:T(8,128)(2,1)S(1)} %pad_maximum_fusion), channel_id=1, source_target_pairs={{0,8},{4,12},{8,0},{12,4},{16,24},{20,28},{24,16},{28,20},{1,9},{5... | collective-permute-start | bytes 393224 | tf_op jit(solution)/shard_map/ppermute | solution.py:349
  94.2 7.6 %collective-permute-start.11 = (bf16[64,1024]{1,0:T(8,128)(2,1)S(1)}, bf16[64,1024]{1,0:T(8,128)(2,1)S(1)}, u32[]{:S(2)}, u32[]{:S(2)}) collective-permute-start(bf16[64,1024]{1,0:T(8,128)(2,1)S(1)} %add_convert_fusion), channel_id=1, source_target_pairs={{0,16},{4,20},{8,24},{12,28},{16,0},{20,4},{24,8},{28,12},{1,17},{... | collective-permute-start | bytes 393224 | tf_op jit(solution)/shard_map/ppermute | solution.py:349
  101.9 6.4 %collective-permute-start.12 = (bf16[64,1024]{1,0:T(8,128)(2,1)S(1)}, bf16[64,1024]{1,0:T(8,128)(2,1)S(1)}, u32[]{:S(2)}, u32[]{:S(2)}) collective-permute-start(bf16[64,1024]{1,0:T(8,128)(2,1)S(1)} %get-tuple-element.27), channel_id=1, source_target_pairs={{0,2},{1,3},{2,0},{3,1},{4,6},{5,7},{6,4},{7,5},{8,10},{9,11},{10,... | collective-permute-start | bytes 393224 | tf_op jit(solution)/shard_map/ppermute | solution.py:349
  102.4 5.9 %collective-permute-start.13 = (bf16[64,1024]{1,0:T(8,128)(2,1)S(1)}, bf16[64,1024]{1,0:T(8,128)(2,1)S(1)}, u32[]{:S(2)}, u32[]{:S(2)}) collective-permute-start(bf16[64,1024]{1,0:T(8,128)(2,1)S(1)} %get-tuple-element.27), channel_id=1, source_target_pairs={{0,4},{4,0},{8,12},{12,8},{16,20},{20,16},{24,28},{28,24},{1,5},{5... | collective-permute-start | bytes 393224 | tf_op jit(solution)/shard_map/ppermute | solution.py:349
  103.5 7.1 %collective-permute-start.14 = (bf16[64,1024]{1,0:T(8,128)(2,1)S(1)}, bf16[64,1024]{1,0:T(8,128)(2,1)S(1)}, u32[]{:S(2)}, u32[]{:S(2)}) collective-permute-start(bf16[64,1024]{1,0:T(8,128)(2,1)S(1)} %get-tuple-element.27), channel_id=1, source_target_pairs={{0,6},{1,7},{2,4},{3,5},{4,2},{5,3},{6,0},{7,1},{8,14},{9,15},{10,... | collective-permute-start | bytes 393224 | tf_op jit(solution)/shard_map/ppermute | solution.py:386
  110.6 2.0 %collective-permute-start.15 = (bf16[256,1024]{1,0:T(8,128)(2,1)S(1)}, bf16[256,1024]{1,0:T(8,128)(2,1)S(1)}, u32[]{:S(2)}, u32[]{:S(2)}) collective-permute-start(bf16[256,1024]{1,0:T(8,128)(2,1)S(1)} %constant_dynamic-update-slice_fusion.2), channel_id=1, source_target_pairs={{0,1},{1,0},{2,3},{3,2},{4,5},{5,4},{6,7},{7,6},{8,9},{9,8},{10,11... | collective-permute-start | bytes 1572872 | tf_op jit(solution)/shard_map/ppermute | solution.py:349

commit v3 on v2

--- a/solution.py
+++ b/solution.py
@@ -72,7 +72,7 @@
         ]
 
 
-def pack(scratch, staged, out_ref, sems, orbs, rows, piece):
+def pack(scratch, staged, orbs, rows, piece, copies=None):
     pieces = staged.shape[0]
     blocks = LANES // piece
     pitch = scratch.shape[1] // orbs
@@ -102,10 +102,12 @@
                 for c in range(blocks):
                     row = pl.multiple_of(g * orbs + start, CHUNK)
                     staged[tile * blocks + c, pl.ds(row, CHUNK), :] = held[c]
-        leave(g).start()
+        if copies:
+            leave(g).start()
         return carry
 
     def leave(g):
+        out_ref, sems = copies
         share = pl.ds(pl.multiple_of(g * orbs, CHUNK), orbs)
         return pltpu.make_async_copy(
             staged.at[:, share, :], out_ref.at[:, share, :], sems.at[g]
@@ -116,17 +118,22 @@
         return carry
 
     lax.fori_loop(0, rows // blocks, group, 0)
-    lax.fori_loop(0, rows // blocks, finish, 0)
-
-
-def fine_cells(fine_ref, cells):
-    blocks = fine_ref.shape[0]
-    spot = lax.broadcasted_iota(jnp.int32, (blocks, cells), 1) // ZB
-    onehot = (spot == lax.broadcasted_iota(jnp.int32, (blocks, cells), 0)).astype(f32)
-    wide = lax.dot_general(
-        fine_ref[...].astype(f32), onehot, (((0,), (0,)), ((), ())), preferred_element_type=f32
-    )
-    return wide > 0.5
+    if copies:
+        lax.fori_loop(0, rows // blocks, finish, 0)
+
+
+def fine_cells(table_ref, slab, cells):
+    x = lax.broadcasted_iota(jnp.int32, (slab, LANES), 0)
+    block = lax.broadcasted_iota(jnp.int32, (slab, LANES), 1) // ZB
+    tiles = []
+    for tile in range(cells // LANES):
+        held = jnp.zeros((slab, LANES), jnp.int32)
+        for b in range(LANES // ZB):
+            for p in range(slab):
+                bit = table_ref[3 + tile * (LANES // ZB) + b, p]
+                held = jnp.where((x == p) & (block == b), bit, held)
+        tiles.append(held)
+    return jnp.concatenate(tiles, axis=1) > 0
 
 
 def region(table_ref, orbs, o):
@@ -137,38 +144,24 @@
 def mask_body(
     piece,
     table_ref,
-    psi_hbm,
-    fine_hbm,
+    psi_ref,
     magic_ref,
     masked_ref,
     out_ref,
     scratch,
     staged,
-    psi_ref,
-    fine_ref,
     sems,
-    in_sems,
 ):
     orbs, channels, slab, cells = psi_ref.shape
     rows = channels * slab
     pitch = scratch.shape[1] // orbs
 
-    def arrive(k):
-        share = pl.ds(pl.multiple_of(k * CHUNK, CHUNK), CHUNK)
-        return pltpu.make_async_copy(psi_hbm.at[share], psi_ref.at[share], in_sems.at[k])
-
-    fine_copy = pltpu.make_async_copy(fine_hbm, fine_ref, in_sems.at[orbs // CHUNK])
-    fine_copy.start()
-    for k in range(orbs // CHUNK):
-        arrive(k).start()
     first_orbital = lax.axis_index("orb") * orbs
     plane = lax.axis_index("comp") * slab + lax.broadcasted_iota(jnp.int32, (slab, cells), 0)
-    fine_copy.wait()
-    fine = fine_cells(fine_ref, cells)
+    fine = fine_cells(table_ref, slab, cells)
 
     def chunk(k, total):
         o = pl.multiple_of(k * CHUNK, CHUNK)
-        arrive(k).wait()
         for i in range(CHUNK):
             least, limit = region(table_ref, orbs, o + i)
             inside = (plane >= least) & (plane < limit)
@@ -205,12 +198,12 @@
         staged.at[:, body:, :], out_ref.at[:, body:, :], sems.at[rows * piece // LANES]
     )
     extra.start()
-    pack(scratch, staged, out_ref, sems, orbs, rows, piece)
+    pack(scratch, staged, orbs, rows, piece, (out_ref, sems))
     extra.wait()
 
 
 def kinetic_body(
-    masked_ref, before_ref, after_ref, depth_ref, plane_ref, magic_ref, out_ref, values_ref
+    masked_ref, before_ref, after_ref, depth_ref, plane_ref, magic_ref, out_ref
 ):
     orbs, channels, slab, cells = masked_ref.shape
     rows = channels * slab
@@ -225,7 +218,7 @@
             axis=1,
         )
         along_z = jnp.dot(lhs, depth_ref[...], preferred_element_type=f32)
-        values_ref[pl.ds(o, CHUNK)] = jnp.dot(
+        out_ref[pl.ds(o, CHUNK), channels] = jnp.dot(
             lhs, magic_ref[...], preferred_element_type=f32
         ).reshape(CHUNK, slab, cells)
         for i in range(0, CHUNK, 2):
@@ -260,25 +253,22 @@
     piece,
     table_ref,
     kinetic_ref,
-    values_ref,
     potential_ref,
-    fine_ref,
     adjoint_ref,
     out_ref,
     scratch,
-    staged,
-    sems,
 ):
     orbs, channels, slab, cells = kinetic_ref.shape
+    channels -= 1
     rows = channels * slab
     pitch = scratch.shape[1] // orbs
     plane = lax.axis_index("comp") * slab + lax.broadcasted_iota(jnp.int32, (slab, cells), 0)
-    fine = fine_cells(fine_ref, cells)
+    fine = fine_cells(table_ref, slab, cells)
     potential = potential_ref[...]
 
     def chunk(k, carry):
         o = pl.multiple_of(k * CHUNK, CHUNK)
-        weighted = (potential[None] * values_ref[pl.ds(o, CHUNK)]).astype(bf16)
+        weighted = (potential[None] * kinetic_ref[pl.ds(o, CHUNK), channels]).astype(bf16)
         back = jnp.dot(
             weighted.reshape(CHUNK * slab, cells), adjoint_ref[...], preferred_element_type=f32
         )
@@ -296,7 +286,7 @@
         return carry
 
     lax.fori_loop(0, orbs // CHUNK, chunk, 0)
-    pack(scratch, staged, out_ref, sems, orbs, rows, piece)
+    pack(scratch, out_ref, orbs, rows, piece)
 
 
 def unpack(got_ref, rows_ref):
@@ -433,8 +423,9 @@
     groups = coefs // LANES
     grid_cells = slab * comp_count * cells
     first_cell = lax.axis_index("orb") * piece
-    table = jnp.stack([region_start, region_len, occupation])
-    fine = fine_mask.T
+    fine = jnp.pad(fine_mask.T, ((0, 0), (0, orbitals - slab)))
+    rows = [region_start[None], region_len[None], occupation[None], fine]
+    table = jnp.concatenate(rows, axis=0)
 
     scratch = pltpu.VMEM((cells // LANES, orbs * (channels * slab + PAD), LANES), f32)
     body_rows = orbs * coefs // LANES
@@ -447,20 +438,17 @@
             jax.ShapeDtypeStruct(psi.shape, bf16),
             jax.ShapeDtypeStruct(packed_shape, bf16),
         ),
-        in_specs=[SMEM, ANY, ANY, VMEM],
+        in_specs=[SMEM, VMEM, VMEM],
         out_specs=(VMEM, ANY),
         scratch_shapes=[
             scratch,
             pltpu.VMEM(packed_shape, bf16),
-            pltpu.VMEM(psi.shape, bf16),
-            pltpu.VMEM(fine.shape, fine.dtype),
             pltpu.SemaphoreType.DMA((groups + 1,)),
-            pltpu.SemaphoreType.DMA((orbs // CHUNK + 1,)),
         ],
         compiler_params=params(),
         name="mask_values_pack",
         cost_estimate=SMALL,
-    )(table, psi, fine, magic_forward)
+    )(table, psi, magic_forward)
 
     ends = comp_count - 1
     before = lax.ppermute(masked, "comp", [(i, i + 1) for i in range(ends)])
@@ -471,14 +459,11 @@
     potential = external - xc_factor * jnp.cbrt(total)
     density = lax.dynamic_slice_in_dim(total, first_cell, piece, 1)
 
-    kinetic, values = pl.pallas_call(
+    kinetic = pl.pallas_call(
         kinetic_body,
-        out_shape=(
-            jax.ShapeDtypeStruct(psi.shape, f32),
-            jax.ShapeDtypeStruct((orbs, slab, cells), f32),
-        ),
+        out_shape=jax.ShapeDtypeStruct((orbs, channels + 1, slab, cells), f32),
         in_specs=[VMEM] * 6,
-        out_specs=(VMEM, VMEM),
+        out_specs=VMEM,
         compiler_params=params(),
         name="kinetic",
         cost_estimate=SMALL,
@@ -494,22 +479,16 @@
     packed_applied = pl.pallas_call(
         functools.partial(applied_body, piece),
         out_shape=jax.ShapeDtypeStruct((orb_count, body_rows, LANES), bf16),
-        in_specs=[SMEM] + [VMEM] * 5,
-        out_specs=ANY,
-        scratch_shapes=[
-            scratch,
-            pltpu.VMEM((orb_count, body_rows, LANES), bf16),
-            pltpu.SemaphoreType.DMA((groups,)),
-        ],
+        in_specs=[SMEM] + [VMEM] * 3,
+        out_specs=VMEM,
+        scratch_shapes=[scratch],
         compiler_params=params(),
         name="applied_pack",
         cost_estimate=SMALL,
     )(
         table,
         kinetic,
-        values,
         potential,
-        fine,
         adjoint_matrix(magic_taps, cells),
     )
     applied_got = lax.all_to_all(packed_applied, "orb", split_axis=0, concat_axis=0, tiled=True)
@@ -527,6 +506,8 @@
         cost_estimate=SMALL,
     )(masked_got)
     inter = share_out(add_partner(*inter_part))
+    for step in stages()[1][:-1]:
+        inter = exchange(inter, step)
 
     applied_got, inter = lax.optimization_barrier((applied_got, inter))
     applied_rows, *lagrange_part = pl.pallas_call(
@@ -539,9 +520,9 @@
         cost_estimate=SMALL,
     )(applied_got, masked_rows)
     lagrange = share_out(add_partner(*lagrange_part))
-    both = jnp.concatenate([lagrange, inter], axis=1)
-    for step in stages()[1]:
-        both = exchange(both, step)
+    for step in stages()[1][:-1]:
+        lagrange = exchange(lagrange, step)
+    both = exchange(jnp.concatenate([lagrange, inter], axis=1), stages()[1][-1])
     both = give_everywhere((both / grid_cells).astype(bf16))
 
     width = 512

time: 116 us -> 114 us (0.983)
  local copies, waits for them, and re-layouts: 11.9 us -> 8.56 us
  waiting for transfers between devices: 52.3 us -> 54.2 us
    all_to_all x1, waiting for transfers between devices: 10.9 us -> 6.04 us  [local(): lax.all_to_all(packed_applied, 'orb', split_axis=0, concat_axis=0, tiled=...]
    ppermute x11 -> x12, waiting for transfers between devices: 20.4 us -> 24.8 us  [swap(): return lax.ppermute(value, axis, [(i, i ^ bit) for i in range(count)])]
    unnamed x30 -> x20, local copies, waits for them, and re-layouts: 9.91 us -> 5.74 us
    all_to_all x1, waiting for transfers between devices: 11.9 us -> 13.9 us  [local(): lax.all_to_all(packed, 'orb', split_axis=0, concat_axis=0, tiled=True)]
    ppermute x11 -> x12, starting transfers between devices: 9.69 us -> 8.22 us  [swap(): return lax.ppermute(value, axis, [(i, i ^ bit) for i in range(count)])]
    pallas_call x1, Pallas kernels: 0.81 us -> 2.07 us  [local(): pl.pallas_call(self_gram_body, out_shape=(row_shape, kept_shape, sent_sha...]
  transfers between devices with their start and end apart: 18 -> 19, of which waited for: 13 -> 17; matrix products, arithmetic and copies ran while one was open for 5% -> 4% of each run, Pallas kernels for 3% -> 5%
where the time goes in v3:
time: 114 us
  waiting for transfers between devices  54.2 us (48%)
  starting transfers between devices  27.8 us (24%)
  Pallas kernels  17.8 us (16%)
  local copies, waits for them, and re-layouts  8.56 us (8%)
  matrix products  2.9 us (3%)
  other arithmetic  1.26 us (1%)
    ppermute x12, waiting for transfers between devices, swap(): return lax.ppermute(value, axis, [(i, i ^ bit) for i in range(count)])  24.8 us
    all_to_all x1, waiting for transfers between devices, local(): lax.all_to_all(packed, 'orb', split_axis=0, concat_axis=0, tiled=True)  13.9 us
    ppermute x3, waiting for transfers between devices, pass_on(): return lax.ppermute(value, axes, pairs)  8.71 us
    ppermute x12, starting transfers between devices, swap(): return lax.ppermute(value, axis, [(i, i ^ bit) for i in range(count)])  8.22 us
    all_to_all x1, starting transfers between devices, local(): lax.all_to_all(packed, 'orb', split_axis=0, concat_axis=0, tiled=True)  7.26 us
    all_to_all x1, waiting for transfers between devices, local(): lax.all_to_all(packed_applied, 'orb', split_axis=0, concat_axis=0, tiled=...  6.04 us
    ppermute x3, starting transfers between devices, pass_on(): return lax.ppermute(value, axes, pairs)  5.81 us
    unnamed x20, local copies, waits for them, and re-layouts  5.74 us
  transfers between devices with their start and end apart: 19, of which 17 were waited for; matrix products, arithmetic and copies ran while one was open for 4% of the time, Pallas kernels for 5%

profile of v3, /device:TPU:0, one launch (start us, length us, event | category | flops | bytes accessed | tf_op | source)
XLA Modules:
  0.0 113.5 jit_solution(4483927298753228716)
XLA Ops:
  0.7 1.0 fusion.9
  1.6 0.7 pad_add_fusion.table_ref
  2.4 1.2 %copy-done.6 = bf16[64,4,16,128]{3,2,1,0:T(8,128)(2,1)S(1)} copy-done((bf16[64,4,16,128]{3,2,1,0:T(8,128)(2,1)S(1)}, bf16[64,4,16,128]{3,2,1,0:T(8,128)(2,1)}, u32[]{:S(2)}) %copy-start.6) | copy-done | bytes 1048600
  3.6 4.9 %mask_values_pack.1 = (bf16[64,4,16,128]{3,2,1,0:T(8,128)(2,1)S(1)}, bf16[8,544,128]{2,1,0:T(8,128)(2,1)}) custom-call(s32[11,512]{1,0:T(8,128)S(1)} %pad_add_fusion.table_ref, bf16[64,4,16,128]{3,2,1,0:T(8,128)(2,1)S(1)} %copy-done.6, bf16[512,128]{1,0:T(8,128)(2,1)S(1)} %bitcast.69), custom_call_target="tpu_custom_call" | custom-call | flops 1024 | bytes 1024 | tf_op jit(solution)/shard_map/mask_values_pack/pallas_call | solution.py:435
  8.5 7.3 %all-to-all-start = ((bf16[8,544,128]{2,1,0:T(8,128)(2,1)}), bf16[8,544,128]{2,1,0:T(8,128)(2,1)}, u32[]{:S(2)}, u32[]{:S(2)}) async-start(bf16[8,544,128]{2,1,0:T(8,128)(2,1)} %get-tuple-element.12), calls=%async_computation | async-start | bytes 2228224 | tf_op jit(solution)/shard_map/all_to_all | solution.py:456
  15.8 1.5 %collective-permute-start = (bf16[64,4,16,128]{3,2,1,0:T(8,128)(2,1)S(1)}, bf16[64,4,16,128]{3,2,1,0:T(8,128)(2,1)S(1)}, u32[]{:S(2)}, u32[]{:S(2)}) collective-permute-start(bf16[64,4,16,128]{3,2,1,0:T(8,128)(2,1)S(1)} %get-tuple-element.14.masked_ref), channel_id=1, source_target_pairs={{0,1},{1,2},{2,3},{4,5},{5,6},{6,7},{8,9},{9,10},{10,11},{12,13},{... | collective-permute-start | bytes 3145736 | tf_op jit(solution)/shard_map/ppermute | solution.py:454
  17.3 1.3 %collective-permute-start.1 = (bf16[64,4,16,128]{3,2,1,0:T(8,128)(2,1)S(1)}, bf16[64,4,16,128]{3,2,1,0:T(8,128)(2,1)}, u32[]{:S(2)}, u32[]{:S(2)}) collective-permute-start(bf16[64,4,16,128]{3,2,1,0:T(8,128)(2,1)S(1)} %get-tuple-element.14.masked_ref), channel_id=1, source_target_pairs={{1,0},{2,1},{3,2},{5,4},{6,5},{7,6},{9,8},{10,9},{11,10},{13,12},{... | collective-permute-start | bytes 3145736 | tf_op jit(solution)/shard_map/ppermute | solution.py:455
  18.7 0.4 fusion.12
  19.0 0.6 fusion.6
  19.6 0.2 copy.11
  19.8 0.1 copy.23
  19.9 0.1 copy.14
  20.1 0.1 reshape.117
  20.2 0.4 fusion.11
  20.5 0.1 copy.13
  20.7 0.1 reshape.116
  20.8 0.4 fusion.10
  21.2 0.1 copy.12
  21.3 0.1 reshape.115
  21.5 0.3 convolution_convert_fusion
  21.8 0.1 pad_maximum_fusion.1.plane_ref
  21.9 1.0 copy-done.4
  22.9 0.7 collective-permute-done.1.after_ref
  23.5 1.2 %copy-done.3 = bf16[64,4,16,128]{3,2,1,0:T(8,128)(2,1)S(1)} copy-done((bf16[64,4,16,128]{3,2,1,0:T(8,128)(2,1)S(1)}, bf16[64,4,16,128]{3,2,1,0:T(8,128)(2,1)}, u32[]{:S(2)}) %copy-start.3) | copy-done | bytes 1048600
  24.7 1.2 %copy-done.5 = bf16[64,4,16,128]{3,2,1,0:T(8,128)(2,1)S(1)} copy-done((bf16[64,4,16,128]{3,2,1,0:T(8,128)(2,1)S(1)}, bf16[64,4,16,128]{3,2,1,0:T(8,128)(2,1)}, u32[]{:S(2)}) %copy-start.5) | copy-done | bytes 1048600
  26.0 3.1 %kinetic.1.kinetic_ref = f32[64,5,16,128]{3,2,1,0:T(8,128)S(1)} custom-call(bf16[64,4,16,128]{3,2,1,0:T(8,128)(2,1)S(1)} %copy-done.3, bf16[64,4,16,128]{3,2,1,0:T(8,128)(2,1)S(1)} %copy-done.5, bf16[64,4,16,128]{3,2,1,0:T(8,128)(2,1)} %collective-permute-done.1.after_ref, bf16[512,512]{1,0:T(8,128)(2,1)S(1)} %bitcast.68, ...), custom_call_target="tpu_custom_call" | custom-call | flops 1024 | bytes 1024 | tf_op jit(solution)/shard_map/kinetic/pallas_call | solution.py:462
  29.1 13.9 %all-to-all-done.got_ref = bf16[8,544,128]{2,1,0:T(8,128)(2,1)} async-done(((bf16[8,544,128]{2,1,0:T(8,128)(2,1)}), bf16[8,544,128]{2,1,0:T(8,128)(2,1)}, u32[]{:S(2)}, u32[]{:S(2)}) %all-to-all-start) | async-done | bytes 1114144 | tf_op jit(solution)/shard_map/all_to_all | solution.py:456
  43.1 0.8 slice.4
  44.0 4.0 %applied_pack.1 = bf16[8,512,128]{2,1,0:T(8,128)(2,1)S(1)} custom-call(s32[11,512]{1,0:T(8,128)S(1)} %pad_add_fusion.table_ref, f32[64,5,16,128]{3,2,1,0:T(8,128)S(1)} %kinetic.1.kinetic_ref, f32[16,128]{1,0:T(8,128)S(1)} %multiply_subtract_fusion.potential_ref, bf16[128,512]{1,0:T(8,128)(2,1)S(1)} %bitcast.71), custom_call_target="tpu_custom_call" | custom-call | flops 1024 | bytes 1024 | tf_op jit(solution)/shard_map/applied_pack/pallas_call | solution.py:479
  48.0 1.0 copy-done.1
  48.9 3.6 %all-to-all-start.1 = ((bf16[8,512,128]{2,1,0:T(8,128)(2,1)}), bf16[8,512,128]{2,1,0:T(8,128)(2,1)S(1)}, u32[]{:S(2)}, u32[]{:S(2)}) async-start(bf16[8,512,128]{2,1,0:T(8,128)(2,1)} %copy-done.1), calls=%async_computation.1 | async-start | bytes 2097152 | tf_op jit(solution)/shard_map/all_to_all | solution.py:494
  52.6 2.1 %intersection.1 = (bf16[512,1024]{1,0:T(8,128)(2,1)S(1)}, f32[256,512]{1,0:T(8,128)S(1)}, bf16[256,512]{1,0:T(8,128)(2,1)S(1)}) custom-call(bf16[8,544,128]{2,1,0:T(8,128)(2,1)} %all-to-all-done.got_ref), custom_call_target="tpu_custom_call" | custom-call | flops 1024 | bytes 1024 | tf_op jit(solution)/shard_map/intersection/pallas_call | solution.py:499
  54.6 0.7 collective-permute-start.2
  55.3 1.2 %collective-permute-done.2 = bf16[256,512]{1,0:T(8,128)(2,1)S(1)} collective-permute-done((bf16[256,512]{1,0:T(8,128)(2,1)S(1)}, bf16[256,512]{1,0:T(8,128)(2,1)S(1)}, u32[]{:S(2)}, u32[]{:S(2)}) %collective-permute-start.2) | collective-permute-done | bytes 262176 | tf_op jit(solution)/shard_map/ppermute | solution.py:339
  56.5 0.1 fusion.37
  56.6 2.8 %collective-permute-start.5 = (bf16[64,512]{1,0:T(8,128)(2,1)S(1)}, bf16[64,512]{1,0:T(8,128)(2,1)S(1)}, u32[]{:S(2)}, u32[]{:S(2)}) collective-permute-start(bf16[64,512]{1,0:T(8,128)(2,1)S(1)} %get-tuple-element.32), channel_id=1, source_target_pairs={{0,6},{1,7},{2,4},{3,5},{4,2},{5,3},{6,0},{7,1},{8,14},{9,15},{10,... | collective-permute-start | bytes 196616 | tf_op jit(solution)/shard_map/ppermute | solution.py:376
  59.4 0.8 collective-permute-start.3
  60.2 4.9 %collective-permute-done.5 = bf16[64,512]{1,0:T(8,128)(2,1)S(1)} collective-permute-done((bf16[64,512]{1,0:T(8,128)(2,1)S(1)}, bf16[64,512]{1,0:T(8,128)(2,1)S(1)}, u32[]{:S(2)}, u32[]{:S(2)}) %collective-permute-start.5) | collective-permute-done | bytes 65568 | tf_op jit(solution)/shard_map/ppermute | solution.py:376
  65.0 1.6 %collective-permute-done.4 = bf16[64,512]{1,0:T(8,128)(2,1)S(1)} collective-permute-done((bf16[64,512]{1,0:T(8,128)(2,1)S(1)}, bf16[64,512]{1,0:T(8,128)(2,1)S(1)}, u32[]{:S(2)}, u32[]{:S(2)}) %collective-permute-start.4) | collective-permute-done | bytes 65568 | tf_op jit(solution)/shard_map/ppermute | solution.py:339
  66.7 0.2 collective-permute-start.6
  66.9 6.5 %collective-permute-done.6 = bf16[64,512]{1,0:T(8,128)(2,1)S(1)} collective-permute-done((bf16[64,512]{1,0:T(8,128)(2,1)S(1)}, bf16[64,512]{1,0:T(8,128)(2,1)S(1)}, u32[]{:S(2)}, u32[]{:S(2)}) %collective-permute-start.6) | collective-permute-done | bytes 65568 | tf_op jit(solution)/shard_map/ppermute | solution.py:339
  73.4 6.0 %all-to-all-done.1.got_ref = bf16[8,512,128]{2,1,0:T(8,128)(2,1)S(1)} async-done(((bf16[8,512,128]{2,1,0:T(8,128)(2,1)}), bf16[8,512,128]{2,1,0:T(8,128)(2,1)S(1)}, u32[]{:S(2)}, u32[]{:S(2)}) %all-to-all-start.1) | async-done | bytes 1048608 | tf_op jit(solution)/shard_map/all_to_all | solution.py:494
  79.4 0.8 lagrange.1
  80.3 1.5 %collective-permute-done.7 = bf16[256,512]{1,0:T(8,128)(2,1)S(1)} collective-permute-done((bf16[256,512]{1,0:T(8,128)(2,1)S(1)}, bf16[256,512]{1,0:T(8,128)(2,1)S(1)}, u32[]{:S(2)}, u32[]{:S(2)}) %collective-permute-start.7) | collective-permute-done | bytes 262176 | tf_op jit(solution)/shard_map/ppermute | solution.py:339
  81.8 0.1 fusion.36
  81.9 1.5 %collective-permute-start.10 = (bf16[64,512]{1,0:T(8,128)(2,1)S(1)}, bf16[64,512]{1,0:T(8,128)(2,1)S(1)}, u32[]{:S(2)}, u32[]{:S(2)}) collective-permute-start(bf16[64,512]{1,0:T(8,128)(2,1)S(1)} %get-tuple-element.29), channel_id=1, source_target_pairs={{0,6},{1,7},{2,4},{3,5},{4,2},{5,3},{6,0},{7,1},{8,14},{9,15},{10,... | collective-permute-start | bytes 196616 | tf_op jit(solution)/shard_map/ppermute | solution.py:376
  83.5 0.6 collective-permute-start.9
  84.1 1.4 %collective-permute-start.8 = (bf16[64,512]{1,0:T(8,128)(2,1)S(1)}, bf16[64,512]{1,0:T(8,128)(2,1)S(1)}, u32[]{:S(2)}, u32[]{:S(2)}) collective-permute-start(bf16[64,512]{1,0:T(8,128)(2,1)S(1)} %get-tuple-element.28), channel_id=1, source_target_pairs={{0,2},{1,3},{2,0},{3,1},{4,6},{5,7},{6,4},{7,5},{8,10},{9,11},{10,... | collective-permute-start | bytes 196616 | tf_op jit(solution)/shard_map/ppermute | solution.py:339
  85.5 2.1 %collective-permute-done.10 = bf16[64,512]{1,0:T(8,128)(2,1)S(1)} collective-permute-done((bf16[64,512]{1,0:T(8,128)(2,1)S(1)}, bf16[64,512]{1,0:T(8,128)(2,1)S(1)}, u32[]{:S(2)}, u32[]{:S(2)}) %collective-permute-start.10) | collective-permute-done | bytes 65568 | tf_op jit(solution)/shard_map/ppermute | solution.py:376
  87.6 0.2 collective-permute-done.9
  87.7 0.7 collective-permute-done.8
  88.5 4.3 %collective-permute-done.11 = bf16[64,512]{1,0:T(8,128)(2,1)S(1)} collective-permute-done((bf16[64,512]{1,0:T(8,128)(2,1)S(1)}, bf16[64,512]{1,0:T(8,128)(2,1)S(1)}, u32[]{:S(2)}, u32[]{:S(2)}) %collective-permute-start.11) | collective-permute-done | bytes 65568 | tf_op jit(solution)/shard_map/ppermute | solution.py:339
  92.8 2.3 %collective-permute-start.12 = (bf16[64,1024]{1,0:T(8,128)(2,1)S(1)}, bf16[64,1024]{1,0:T(8,128)(2,1)S(1)}, u32[]{:S(2)}, u32[]{:S(2)}) collective-permute-start(bf16[64,1024]{1,0:T(8,128)(2,1)S(1)} %pad_maximum_fusion), channel_id=1, source_target_pairs={{0,16},{4,20},{8,24},{12,28},{16,0},{20,4},{24,8},{28,12},{1,17},{... | collective-permute-start | bytes 393224 | tf_op jit(solution)/shard_map/ppermute | solution.py:339
  95.1 5.3 %collective-permute-done.12 = bf16[64,1024]{1,0:T(8,128)(2,1)S(1)} collective-permute-done((bf16[64,1024]{1,0:T(8,128)(2,1)S(1)}, bf16[64,1024]{1,0:T(8,128)(2,1)S(1)}, u32[]{:S(2)}, u32[]{:S(2)}) %collective-permute-start.12) | collective-permute-done | bytes 131104 | tf_op jit(solution)/shard_map/ppermute | solution.py:339
  100.6 1.1 collective-permute-start.13
  101.7 1.0 collective-permute-start.14
  102.7 1.5 %collective-permute-start.15 = (bf16[64,1024]{1,0:T(8,128)(2,1)S(1)}, bf16[64,1024]{1,0:T(8,128)(2,1)S(1)}, u32[]{:S(2)}, u32[]{:S(2)}) collective-permute-start(bf16[64,1024]{1,0:T(8,128)(2,1)S(1)} %get-tuple-element.23), channel_id=1, source_target_pairs={{0,6},{1,7},{2,4},{3,5},{4,2},{5,3},{6,0},{7,1},{8,14},{9,15},{10,... | collective-permute-start | bytes 393224 | tf_op jit(solution)/shard_map/ppermute | solution.py:376
  104.1 2.5 %collective-permute-done.13 = bf16[64,1024]{1,0:T(8,128)(2,1)S(1)} collective-permute-done((bf16[64,1024]{1,0:T(8,128)(2,1)S(1)}, bf16[64,1024]{1,0:T(8,128)(2,1)S(1)}, u32[]{:S(2)}, u32[]{:S(2)}) %collective-permute-start.13) | collective-permute-done | bytes 131104 | tf_op jit(solution)/shard_map/ppermute | solution.py:339
  106.6 0.1 collective-permute-done.14
  106.8 1.8 %collective-permute-done.15 = bf16[64,1024]{1,0:T(8,128)(2,1)S(1)} collective-permute-done((bf16[64,1024]{1,0:T(8,128)(2,1)S(1)}, bf16[64,1024]{1,0:T(8,128)(2,1)S(1)}, u32[]{:S(2)}, u32[]{:S(2)}) %collective-permute-start.15) | collective-permute-done | bytes 131104 | tf_op jit(solution)/shard_map/ppermute | solution.py:376
  108.6 0.7 constant_dynamic-slice_fusion.6
  109.3 0.1 broadcast_in_dim.13
  109.5 1.0 collective-permute-done.16
  110.6 3.0 %update.1 = bf16[1024,512]{1,0:T(8,128)(2,1)} custom-call(bf16[512,1024]{1,0:T(8,128)(2,1)S(1)} %get-tuple-element.13.other_ref.masked_ref, bf16[512,1024]{1,0:T(8,128)(2,1)S(1)} %get-tuple-element.18.applied_ref, bf16[512,1024]{1,0:T(8,128)(2,1)S(1)} %constant_dynamic-update-slice_fusion.lagrange_ref.inter_ref, ...), custom_call_target="tpu_custom_call" | custom-call | flops 1024 | bytes 1024 | tf_op jit(solution)/shard_map/update/pallas_call | solution.py:529
  (43 shorter events, 0.8 us)
Async XLA Ops:
  0.6 18.0 %copy-start = (bf16[29,4,4]{0,2,1:T(4,128)(2,1)S(1)}, bf16[29,4,4]{0,2,1:T(4,128)(2,1)}, u32[]{:S(2)}) copy-start(bf16[29,4,4]{0,2,1:T(4,128)(2,1)} %param.13) | copy-start | bytes 2788
  2.4 1.2 %copy-start.6 = (bf16[64,4,16,128]{3,2,1,0:T(8,128)(2,1)S(1)}, bf16[64,4,16,128]{3,2,1,0:T(8,128)(2,1)}, u32[]{:S(2)}) copy-start(bf16[64,4,16,128]{3,2,1,0:T(8,128)(2,1)} %psi_ref.1) | copy-start | bytes 3145732
  8.5 11.3 %copy-start.2 = (bf16[64,4,16,128]{3,2,1,0:T(8,128)(2,1)}, bf16[64,4,16,128]{3,2,1,0:T(8,128)(2,1)S(1)}, u32[]{:S(2)}) copy-start(bf16[64,4,16,128]{3,2,1,0:T(8,128)(2,1)S(1)} %get-tuple-element.14.masked_ref) | copy-start | bytes 3145732
  8.5 34.5 %all-to-all-start = ((bf16[8,544,128]{2,1,0:T(8,128)(2,1)}), bf16[8,544,128]{2,1,0:T(8,128)(2,1)}, u32[]{:S(2)}, u32[]{:S(2)}) async-start(bf16[8,544,128]{2,1,0:T(8,128)(2,1)} %get-tuple-element.12), calls=%async_computation | async-start | bytes 2228224 | tf_op jit(solution)/shard_map/all_to_all | solution.py:456
  15.8 5.7 %copy-start.8 = (bf16[16,4]{0,1:T(4,128)(2,1)S(1)}, bf16[16,4]{0,1:T(4,128)(2,1)}, u32[]{:S(2)}) copy-start(bf16[16,4]{0,1:T(4,128)(2,1)} %param.14) | copy-start | bytes 388
  15.8 6.1 %collective-permute-start = (bf16[64,4,16,128]{3,2,1,0:T(8,128)(2,1)S(1)}, bf16[64,4,16,128]{3,2,1,0:T(8,128)(2,1)S(1)}, u32[]{:S(2)}, u32[]{:S(2)}) collective-permute-start(bf16[64,4,16,128]{3,2,1,0:T(8,128)(2,1)S(1)} %get-tuple-element.14.masked_ref), channel_id=1, source_target_pairs={{0,1},{1,2},{2,3},{4,5},{5,6},{6,7},{8,9},{9,10},{10,11},{12,13},{... | collective-permute-start | bytes 3145736 | tf_op jit(solution)/shard_map/ppermute | solution.py:454
  17.3 6.2 %collective-permute-start.1 = (bf16[64,4,16,128]{3,2,1,0:T(8,128)(2,1)S(1)}, bf16[64,4,16,128]{3,2,1,0:T(8,128)(2,1)}, u32[]{:S(2)}, u32[]{:S(2)}) collective-permute-start(bf16[64,4,16,128]{3,2,1,0:T(8,128)(2,1)S(1)} %get-tuple-element.14.masked_ref), channel_id=1, source_target_pairs={{1,0},{2,1},{3,2},{5,4},{6,5},{7,6},{9,8},{10,9},{11,10},{13,12},{... | collective-permute-start | bytes 3145736 | tf_op jit(solution)/shard_map/ppermute | solution.py:455
  21.9 1.0 copy-start.4
  23.5 1.2 %copy-start.3 = (bf16[64,4,16,128]{3,2,1,0:T(8,128)(2,1)S(1)}, bf16[64,4,16,128]{3,2,1,0:T(8,128)(2,1)}, u32[]{:S(2)}) copy-start(bf16[64,4,16,128]{3,2,1,0:T(8,128)(2,1)} %copy-done.2) | copy-start | bytes 3145732
  24.7 1.2 %copy-start.5 = (bf16[64,4,16,128]{3,2,1,0:T(8,128)(2,1)S(1)}, bf16[64,4,16,128]{3,2,1,0:T(8,128)(2,1)}, u32[]{:S(2)}) copy-start(bf16[64,4,16,128]{3,2,1,0:T(8,128)(2,1)} %copy-done.4) | copy-start | bytes 3145732
  26.0 18.0 %copy-start.7 = (f32[16,128]{1,0:T(8,128)S(1)}, f32[16,128]{1,0:T(8,128)}, u32[]{:S(2)}) copy-start(f32[16,128]{1,0:T(8,128)} %param.15) | copy-start | bytes 24580
  47.9 1.0 copy-start.1
  48.9 30.5 %all-to-all-start.1 = ((bf16[8,512,128]{2,1,0:T(8,128)(2,1)}), bf16[8,512,128]{2,1,0:T(8,128)(2,1)S(1)}, u32[]{:S(2)}, u32[]{:S(2)}) async-start(bf16[8,512,128]{2,1,0:T(8,128)(2,1)} %copy-done.1), calls=%async_computation.1 | async-start | bytes 2097152 | tf_op jit(solution)/shard_map/all_to_all | solution.py:494
  54.6 1.8 %collective-permute-start.2 = (bf16[256,512]{1,0:T(8,128)(2,1)S(1)}, bf16[256,512]{1,0:T(8,128)(2,1)S(1)}, u32[]{:S(2)}, u32[]{:S(2)}) collective-permute-start(bf16[256,512]{1,0:T(8,128)(2,1)S(1)} %get-tuple-element.16), channel_id=1, source_target_pairs={{0,1},{1,0},{2,3},{3,2},{4,5},{5,4},{6,7},{7,6},{8,9},{9,8},{10,11... | collective-permute-start | bytes 786440 | tf_op jit(solution)/shard_map/ppermute | solution.py:339
  56.6 8.4 %collective-permute-start.5 = (bf16[64,512]{1,0:T(8,128)(2,1)S(1)}, bf16[64,512]{1,0:T(8,128)(2,1)S(1)}, u32[]{:S(2)}, u32[]{:S(2)}) collective-permute-start(bf16[64,512]{1,0:T(8,128)(2,1)S(1)} %get-tuple-element.32), channel_id=1, source_target_pairs={{0,6},{1,7},{2,4},{3,5},{4,2},{5,3},{6,0},{7,1},{8,14},{9,15},{10,... | collective-permute-start | bytes 196616 | tf_op jit(solution)/shard_map/ppermute | solution.py:376
  59.4 7.2 %collective-permute-start.4 = (bf16[64,512]{1,0:T(8,128)(2,1)S(1)}, bf16[64,512]{1,0:T(8,128)(2,1)S(1)}, u32[]{:S(2)}, u32[]{:S(2)}) collective-permute-start(bf16[64,512]{1,0:T(8,128)(2,1)S(1)} %get-tuple-element.33), channel_id=1, source_target_pairs={{0,4},{4,0},{8,12},{12,8},{16,20},{20,16},{24,28},{28,24},{1,5},{5... | collective-permute-start | bytes 196616 | tf_op jit(solution)/shard_map/ppermute | solution.py:339
  59.4 7.2 %collective-permute-start.3 = (bf16[64,512]{1,0:T(8,128)(2,1)S(1)}, bf16[64,512]{1,0:T(8,128)(2,1)S(1)}, u32[]{:S(2)}, u32[]{:S(2)}) collective-permute-start(bf16[64,512]{1,0:T(8,128)(2,1)S(1)} %get-tuple-element.31), channel_id=1, source_target_pairs={{0,2},{1,3},{2,0},{3,1},{4,6},{5,7},{6,4},{7,5},{8,10},{9,11},{10,... | collective-permute-start | bytes 196616 | tf_op jit(solution)/shard_map/ppermute | solution.py:339
  66.7 6.7 %collective-permute-start.6 = (bf16[64,512]{1,0:T(8,128)(2,1)S(1)}, bf16[64,512]{1,0:T(8,128)(2,1)S(1)}, u32[]{:S(2)}, u32[]{:S(2)}) collective-permute-start(bf16[64,512]{1,0:T(8,128)(2,1)S(1)} %add_convert_fusion.2), channel_id=1, source_target_pairs={{0,8},{4,12},{8,0},{12,4},{16,24},{20,28},{24,16},{28,20},{1,9},{5... | collective-permute-start | bytes 196616 | tf_op jit(solution)/shard_map/ppermute | solution.py:339
  80.2 1.6 %collective-permute-start.7 = (bf16[256,512]{1,0:T(8,128)(2,1)S(1)}, bf16[256,512]{1,0:T(8,128)(2,1)S(1)}, u32[]{:S(2)}, u32[]{:S(2)}) collective-permute-start(bf16[256,512]{1,0:T(8,128)(2,1)S(1)} %get-tuple-element.20), channel_id=1, source_target_pairs={{0,1},{1,0},{2,3},{3,2},{4,5},{5,4},{6,7},{7,6},{8,9},{9,8},{10,11... | collective-permute-start | bytes 786440 | tf_op jit(solution)/shard_map/ppermute | solution.py:339
  81.9 5.6 %collective-permute-start.10 = (bf16[64,512]{1,0:T(8,128)(2,1)S(1)}, bf16[64,512]{1,0:T(8,128)(2,1)S(1)}, u32[]{:S(2)}, u32[]{:S(2)}) collective-permute-start(bf16[64,512]{1,0:T(8,128)(2,1)S(1)} %get-tuple-element.29), channel_id=1, source_target_pairs={{0,6},{1,7},{2,4},{3,5},{4,2},{5,3},{6,0},{7,1},{8,14},{9,15},{10,... | collective-permute-start | bytes 196616 | tf_op jit(solution)/shard_map/ppermute | solution.py:376
  83.5 4.3 %collective-permute-start.9 = (bf16[64,512]{1,0:T(8,128)(2,1)S(1)}, bf16[64,512]{1,0:T(8,128)(2,1)S(1)}, u32[]{:S(2)}, u32[]{:S(2)}) collective-permute-start(bf16[64,512]{1,0:T(8,128)(2,1)S(1)} %get-tuple-element.30), channel_id=1, source_target_pairs={{0,4},{4,0},{8,12},{12,8},{16,20},{20,16},{24,28},{28,24},{1,5},{5... | collective-permute-start | bytes 196616 | tf_op jit(solution)/shard_map/ppermute | solution.py:339
  84.1 4.3 %collective-permute-start.8 = (bf16[64,512]{1,0:T(8,128)(2,1)S(1)}, bf16[64,512]{1,0:T(8,128)(2,1)S(1)}, u32[]{:S(2)}, u32[]{:S(2)}) collective-permute-start(bf16[64,512]{1,0:T(8,128)(2,1)S(1)} %get-tuple-element.28), channel_id=1, source_target_pairs={{0,2},{1,3},{2,0},{3,1},{4,6},{5,7},{6,4},{7,5},{8,10},{9,11},{10,... | collective-permute-start | bytes 196616 | tf_op jit(solution)/shard_map/ppermute | solution.py:339
  88.5 4.3 %collective-permute-start.11 = (bf16[64,512]{1,0:T(8,128)(2,1)S(1)}, bf16[64,512]{1,0:T(8,128)(2,1)S(1)}, u32[]{:S(2)}, u32[]{:S(2)}) collective-permute-start(bf16[64,512]{1,0:T(8,128)(2,1)S(1)} %add_convert_fusion.1), channel_id=1, source_target_pairs={{0,8},{4,12},{8,0},{12,4},{16,24},{20,28},{24,16},{28,20},{1,9},{5... | collective-permute-start | bytes 196616 | tf_op jit(solution)/shard_map/ppermute | solution.py:339
  92.8 7.6 %collective-permute-start.12 = (bf16[64,1024]{1,0:T(8,128)(2,1)S(1)}, bf16[64,1024]{1,0:T(8,128)(2,1)S(1)}, u32[]{:S(2)}, u32[]{:S(2)}) collective-permute-start(bf16[64,1024]{1,0:T(8,128)(2,1)S(1)} %pad_maximum_fusion), channel_id=1, source_target_pairs={{0,16},{4,20},{8,24},{12,28},{16,0},{20,4},{24,8},{28,12},{1,17},{... | collective-permute-start | bytes 393224 | tf_op jit(solution)/shard_map/ppermute | solution.py:339
  100.6 6.1 %collective-permute-start.13 = (bf16[64,1024]{1,0:T(8,128)(2,1)S(1)}, bf16[64,1024]{1,0:T(8,128)(2,1)S(1)}, u32[]{:S(2)}, u32[]{:S(2)}) collective-permute-start(bf16[64,1024]{1,0:T(8,128)(2,1)S(1)} %get-tuple-element.23), channel_id=1, source_target_pairs={{0,2},{1,3},{2,0},{3,1},{4,6},{5,7},{6,4},{7,5},{8,10},{9,11},{10,... | collective-permute-start | bytes 393224 | tf_op jit(solution)/shard_map/ppermute | solution.py:339
  101.7 5.1 %collective-permute-start.14 = (bf16[64,1024]{1,0:T(8,128)(2,1)S(1)}, bf16[64,1024]{1,0:T(8,128)(2,1)S(1)}, u32[]{:S(2)}, u32[]{:S(2)}) collective-permute-start(bf16[64,1024]{1,0:T(8,128)(2,1)S(1)} %get-tuple-element.23), channel_id=1, source_target_pairs={{0,4},{4,0},{8,12},{12,8},{16,20},{20,16},{24,28},{28,24},{1,5},{5... | collective-permute-start | bytes 393224 | tf_op jit(solution)/shard_map/ppermute | solution.py:339
  102.7 5.9 %collective-permute-start.15 = (bf16[64,1024]{1,0:T(8,128)(2,1)S(1)}, bf16[64,1024]{1,0:T(8,128)(2,1)S(1)}, u32[]{:S(2)}, u32[]{:S(2)}) collective-permute-start(bf16[64,1024]{1,0:T(8,128)(2,1)S(1)} %get-tuple-element.23), channel_id=1, source_target_pairs={{0,6},{1,7},{2,4},{3,5},{4,2},{5,3},{6,0},{7,1},{8,14},{9,15},{10,... | collective-permute-start | bytes 393224 | tf_op jit(solution)/shard_map/ppermute | solution.py:376
  108.5 2.0 %collective-permute-start.16 = (bf16[256,1024]{1,0:T(8,128)(2,1)S(1)}, bf16[256,1024]{1,0:T(8,128)(2,1)S(1)}, u32[]{:S(2)}, u32[]{:S(2)}) collective-permute-start(bf16[256,1024]{1,0:T(8,128)(2,1)S(1)} %constant_dynamic-update-slice_fusion.2), channel_id=1, source_target_pairs={{0,1},{1,0},{2,3},{3,2},{4,5},{5,4},{6,7},{7,6},{8,9},{9,8},{10,11... | collective-permute-start | bytes 1572872 | tf_op jit(solution)/shard_map/ppermute | solution.py:339

commit v4 on v3

--- a/solution.py
+++ b/solution.py
@@ -519,13 +519,15 @@
         name="lagrange",
         cost_estimate=SMALL,
     )(applied_got, masked_rows)
-    lagrange = share_out(add_partner(*lagrange_part))
-    for step in stages()[1][:-1]:
+    lagrange = add_partner(*lagrange_part)
+    inter = exchange(lax.optimization_barrier((inter, lagrange))[0], stages()[1][-1])
+    lagrange = share_out(lagrange)
+    for step in stages()[1]:
         lagrange = exchange(lagrange, step)
-    both = exchange(jnp.concatenate([lagrange, inter], axis=1), stages()[1][-1])
+    both = jnp.concatenate([lagrange, inter], axis=1)
     both = give_everywhere((both / grid_cells).astype(bf16))
 
-    width = 512
+    width = coefs
     following = pl.pallas_call(
         update_body,
         grid=(coefs // width,),

time: 114 us -> 113 us (level)
  waiting for transfers between devices: 54.2 us -> 47.8 us
  starting transfers between devices: 27.8 us -> 33 us
    ppermute x12 -> x13, waiting for transfers between devices: 24.8 us -> 18.6 us  [swap(): return lax.ppermute(value, axis, [(i, i ^ bit) for i in range(count)])]
    ppermute x12 -> x13, starting transfers between devices: 8.22 us -> 14.2 us  [swap(): return lax.ppermute(value, axis, [(i, i ^ bit) for i in range(count)])]
  transfers between devices with their start and end apart: 19 -> 20, of which waited for: 17 -> 17; matrix products, arithmetic and copies ran while one was open for 4% -> 4% of each run, Pallas kernels for 5% -> 5%
where the time goes in v4:
time: 113 us; the launch traced here: 112 us
  waiting for transfers between devices  47.8 us (42%)
  starting transfers between devices  33 us (29%)
  Pallas kernels  17.4 us (15%)
  local copies, waits for them, and re-layouts  8.55 us (8%)
  matrix products  2.9 us (3%)
  other arithmetic  1.26 us (1%)
    ppermute x13, waiting for transfers between devices, swap(): return lax.ppermute(value, axis, [(i, i ^ bit) for i in range(count)])  18.6 us
    ppermute x13, starting transfers between devices, swap(): return lax.ppermute(value, axis, [(i, i ^ bit) for i in range(count)])  14.2 us
    all_to_all x1, waiting for transfers between devices, local(): lax.all_to_all(packed, 'orb', split_axis=0, concat_axis=0, tiled=True)  13.9 us
    ppermute x3, waiting for transfers between devices, pass_on(): return lax.ppermute(value, axes, pairs)  8.55 us
    all_to_all x1, starting transfers between devices, local(): lax.all_to_all(packed, 'orb', split_axis=0, concat_axis=0, tiled=True)  7.26 us
    all_to_all x1, waiting for transfers between devices, local(): lax.all_to_all(packed_applied, 'orb', split_axis=0, concat_axis=0, tiled=...  6.01 us
    unnamed x20, local copies, waits for them, and re-layouts  5.73 us
    ppermute x3, starting transfers between devices, pass_on(): return lax.ppermute(value, axes, pairs)  5.13 us
  transfers between devices with their start and end apart: 20, of which 17 were waited for; matrix products, arithmetic and copies ran while one was open for 4% of the time, Pallas kernels for 5%

profile of v4, /device:TPU:0, one launch (start us, length us, event | category | flops | bytes accessed | tf_op | source)
XLA Modules:
  0.0 112.0 jit_solution(13112038464991835193)
XLA Ops:
  0.7 1.0 fusion.9
  1.6 0.7 pad_add_fusion.table_ref
  2.4 1.2 %copy-done.6 = bf16[64,4,16,128]{3,2,1,0:T(8,128)(2,1)S(1)} copy-done((bf16[64,4,16,128]{3,2,1,0:T(8,128)(2,1)S(1)}, bf16[64,4,16,128]{3,2,1,0:T(8,128)(2,1)}, u32[]{:S(2)}) %copy-start.6) | copy-done | bytes 1048600
  3.6 4.9 %mask_values_pack.1 = (bf16[64,4,16,128]{3,2,1,0:T(8,128)(2,1)S(1)}, bf16[8,544,128]{2,1,0:T(8,128)(2,1)}) custom-call(s32[11,512]{1,0:T(8,128)S(1)} %pad_add_fusion.table_ref, bf16[64,4,16,128]{3,2,1,0:T(8,128)(2,1)S(1)} %copy-done.6, bf16[512,128]{1,0:T(8,128)(2,1)S(1)} %bitcast.69), custom_call_target="tpu_custom_call" | custom-call | flops 1024 | bytes 1024 | tf_op jit(solution)/shard_map/mask_values_pack/pallas_call | solution.py:435
  8.5 7.3 %all-to-all-start = ((bf16[8,544,128]{2,1,0:T(8,128)(2,1)}), bf16[8,544,128]{2,1,0:T(8,128)(2,1)}, u32[]{:S(2)}, u32[]{:S(2)}) async-start(bf16[8,544,128]{2,1,0:T(8,128)(2,1)} %get-tuple-element.13), calls=%async_computation | async-start | bytes 2228224 | tf_op jit(solution)/shard_map/all_to_all | solution.py:456
  15.8 1.5 %collective-permute-start = (bf16[64,4,16,128]{3,2,1,0:T(8,128)(2,1)S(1)}, bf16[64,4,16,128]{3,2,1,0:T(8,128)(2,1)S(1)}, u32[]{:S(2)}, u32[]{:S(2)}) collective-permute-start(bf16[64,4,16,128]{3,2,1,0:T(8,128)(2,1)S(1)} %get-tuple-element.15.masked_ref), channel_id=1, source_target_pairs={{0,1},{1,2},{2,3},{4,5},{5,6},{6,7},{8,9},{9,10},{10,11},{12,13},{... | collective-permute-start | bytes 3145736 | tf_op jit(solution)/shard_map/ppermute | solution.py:454
  17.3 1.3 %collective-permute-start.1 = (bf16[64,4,16,128]{3,2,1,0:T(8,128)(2,1)S(1)}, bf16[64,4,16,128]{3,2,1,0:T(8,128)(2,1)}, u32[]{:S(2)}, u32[]{:S(2)}) collective-permute-start(bf16[64,4,16,128]{3,2,1,0:T(8,128)(2,1)S(1)} %get-tuple-element.15.masked_ref), channel_id=1, source_target_pairs={{1,0},{2,1},{3,2},{5,4},{6,5},{7,6},{9,8},{10,9},{11,10},{13,12},{... | collective-permute-start | bytes 3145736 | tf_op jit(solution)/shard_map/ppermute | solution.py:455
  18.6 0.4 fusion.12
  19.0 0.6 fusion.6
  19.6 0.2 copy.11
  19.9 0.1 copy.14
  20.1 0.1 reshape.117
  20.2 0.4 fusion.11
  20.5 0.1 copy.13
  20.7 0.1 reshape.116
  20.8 0.4 fusion.10
  21.2 0.1 copy.12
  21.3 0.1 reshape.115
  21.5 0.3 convolution_convert_fusion
  21.8 0.1 pad_maximum_fusion.plane_ref
  21.9 1.0 copy-done.4
  22.8 0.7 collective-permute-done.1.after_ref
  23.5 1.2 %copy-done.3 = bf16[64,4,16,128]{3,2,1,0:T(8,128)(2,1)S(1)} copy-done((bf16[64,4,16,128]{3,2,1,0:T(8,128)(2,1)S(1)}, bf16[64,4,16,128]{3,2,1,0:T(8,128)(2,1)}, u32[]{:S(2)}) %copy-start.3) | copy-done | bytes 1048600
  24.7 1.2 %copy-done.5 = bf16[64,4,16,128]{3,2,1,0:T(8,128)(2,1)S(1)} copy-done((bf16[64,4,16,128]{3,2,1,0:T(8,128)(2,1)S(1)}, bf16[64,4,16,128]{3,2,1,0:T(8,128)(2,1)}, u32[]{:S(2)}) %copy-start.5) | copy-done | bytes 1048600
  26.0 3.1 %kinetic.1.kinetic_ref = f32[64,5,16,128]{3,2,1,0:T(8,128)S(1)} custom-call(bf16[64,4,16,128]{3,2,1,0:T(8,128)(2,1)S(1)} %copy-done.3, bf16[64,4,16,128]{3,2,1,0:T(8,128)(2,1)S(1)} %copy-done.5, bf16[64,4,16,128]{3,2,1,0:T(8,128)(2,1)} %collective-permute-done.1.after_ref, bf16[512,512]{1,0:T(8,128)(2,1)S(1)} %bitcast.68, ...), custom_call_target="tpu_custom_call" | custom-call | flops 1024 | bytes 1024 | tf_op jit(solution)/shard_map/kinetic/pallas_call | solution.py:462
  29.1 13.9 %all-to-all-done.got_ref = bf16[8,544,128]{2,1,0:T(8,128)(2,1)} async-done(((bf16[8,544,128]{2,1,0:T(8,128)(2,1)}), bf16[8,544,128]{2,1,0:T(8,128)(2,1)}, u32[]{:S(2)}, u32[]{:S(2)}) %all-to-all-start) | async-done | bytes 1114144 | tf_op jit(solution)/shard_map/all_to_all | solution.py:456
  43.0 0.8 slice.4
  44.0 4.0 %applied_pack.1 = bf16[8,512,128]{2,1,0:T(8,128)(2,1)S(1)} custom-call(s32[11,512]{1,0:T(8,128)S(1)} %pad_add_fusion.table_ref, f32[64,5,16,128]{3,2,1,0:T(8,128)S(1)} %kinetic.1.kinetic_ref, f32[16,128]{1,0:T(8,128)S(1)} %multiply_subtract_fusion.potential_ref, bf16[128,512]{1,0:T(8,128)(2,1)S(1)} %bitcast.71), custom_call_target="tpu_custom_call" | custom-call | flops 1024 | bytes 1024 | tf_op jit(solution)/shard_map/applied_pack/pallas_call | solution.py:479
  48.0 1.0 copy-done.1
  48.9 3.6 %all-to-all-start.1 = ((bf16[8,512,128]{2,1,0:T(8,128)(2,1)}), bf16[8,512,128]{2,1,0:T(8,128)(2,1)S(1)}, u32[]{:S(2)}, u32[]{:S(2)}) async-start(bf16[8,512,128]{2,1,0:T(8,128)(2,1)} %copy-done.1), calls=%async_computation.1 | async-start | bytes 2097152 | tf_op jit(solution)/shard_map/all_to_all | solution.py:494
  52.6 2.1 %intersection.1 = (bf16[512,1024]{1,0:T(8,128)(2,1)S(1)}, f32[256,512]{1,0:T(8,128)S(1)}, bf16[256,512]{1,0:T(8,128)(2,1)S(1)}) custom-call(bf16[8,544,128]{2,1,0:T(8,128)(2,1)} %all-to-all-done.got_ref), custom_call_target="tpu_custom_call" | custom-call | flops 1024 | bytes 1024 | tf_op jit(solution)/shard_map/intersection/pallas_call | solution.py:499
  54.6 0.7 collective-permute-start.2
  55.3 1.2 %collective-permute-done.2 = bf16[256,512]{1,0:T(8,128)(2,1)S(1)} collective-permute-done((bf16[256,512]{1,0:T(8,128)(2,1)S(1)}, bf16[256,512]{1,0:T(8,128)(2,1)S(1)}, u32[]{:S(2)}, u32[]{:S(2)}) %collective-permute-start.2) | collective-permute-done | bytes 262176 | tf_op jit(solution)/shard_map/ppermute | solution.py:339
  56.5 0.1 fusion.39
  56.6 2.8 %collective-permute-start.5 = (bf16[64,512]{1,0:T(8,128)(2,1)S(1)}, bf16[64,512]{1,0:T(8,128)(2,1)S(1)}, u32[]{:S(2)}, u32[]{:S(2)}) collective-permute-start(bf16[64,512]{1,0:T(8,128)(2,1)S(1)} %get-tuple-element.34), channel_id=1, source_target_pairs={{0,6},{1,7},{2,4},{3,5},{4,2},{5,3},{6,0},{7,1},{8,14},{9,15},{10,... | collective-permute-start | bytes 196616 | tf_op jit(solution)/shard_map/ppermute | solution.py:376
  59.4 0.8 collective-permute-start.3
  60.2 4.8 %collective-permute-done.5 = bf16[64,512]{1,0:T(8,128)(2,1)S(1)} collective-permute-done((bf16[64,512]{1,0:T(8,128)(2,1)S(1)}, bf16[64,512]{1,0:T(8,128)(2,1)S(1)}, u32[]{:S(2)}, u32[]{:S(2)}) %collective-permute-start.5) | collective-permute-done | bytes 65568 | tf_op jit(solution)/shard_map/ppermute | solution.py:376
  65.0 1.6 %collective-permute-done.4 = bf16[64,512]{1,0:T(8,128)(2,1)S(1)} collective-permute-done((bf16[64,512]{1,0:T(8,128)(2,1)S(1)}, bf16[64,512]{1,0:T(8,128)(2,1)S(1)}, u32[]{:S(2)}, u32[]{:S(2)}) %collective-permute-start.4) | collective-permute-done | bytes 65568 | tf_op jit(solution)/shard_map/ppermute | solution.py:339
  66.7 0.2 collective-permute-start.6
  66.9 6.5 %collective-permute-done.6 = bf16[64,512]{1,0:T(8,128)(2,1)S(1)} collective-permute-done((bf16[64,512]{1,0:T(8,128)(2,1)S(1)}, bf16[64,512]{1,0:T(8,128)(2,1)S(1)}, u32[]{:S(2)}, u32[]{:S(2)}) %collective-permute-start.6) | collective-permute-done | bytes 65568 | tf_op jit(solution)/shard_map/ppermute | solution.py:339
  73.4 6.0 %all-to-all-done.1.got_ref = bf16[8,512,128]{2,1,0:T(8,128)(2,1)S(1)} async-done(((bf16[8,512,128]{2,1,0:T(8,128)(2,1)}), bf16[8,512,128]{2,1,0:T(8,128)(2,1)S(1)}, u32[]{:S(2)}, u32[]{:S(2)}) %all-to-all-start.1) | async-done | bytes 1048608 | tf_op jit(solution)/shard_map/all_to_all | solution.py:494
  79.4 0.8 lagrange.1
  80.3 1.5 %collective-permute-done.7 = bf16[256,512]{1,0:T(8,128)(2,1)S(1)} collective-permute-done((bf16[256,512]{1,0:T(8,128)(2,1)S(1)}, bf16[256,512]{1,0:T(8,128)(2,1)S(1)}, u32[]{:S(2)}, u32[]{:S(2)}) %collective-permute-start.7) | collective-permute-done | bytes 262176 | tf_op jit(solution)/shard_map/ppermute | solution.py:339
  81.8 0.1 fusion.38
  81.9 1.6 %collective-permute-start.10 = (bf16[64,512]{1,0:T(8,128)(2,1)S(1)}, bf16[64,512]{1,0:T(8,128)(2,1)S(1)}, u32[]{:S(2)}, u32[]{:S(2)}) collective-permute-start(bf16[64,512]{1,0:T(8,128)(2,1)S(1)} %get-tuple-element.31), channel_id=1, source_target_pairs={{0,6},{1,7},{2,4},{3,5},{4,2},{5,3},{6,0},{7,1},{8,14},{9,15},{10,... | collective-permute-start | bytes 196616 | tf_op jit(solution)/shard_map/ppermute | solution.py:376
  83.5 0.6 collective-permute-start.9
  84.1 1.4 %collective-permute-start.8 = (bf16[64,512]{1,0:T(8,128)(2,1)S(1)}, bf16[64,512]{1,0:T(8,128)(2,1)S(1)}, u32[]{:S(2)}, u32[]{:S(2)}) collective-permute-start(bf16[64,512]{1,0:T(8,128)(2,1)S(1)} %get-tuple-element.30), channel_id=1, source_target_pairs={{0,2},{1,3},{2,0},{3,1},{4,6},{5,7},{6,4},{7,5},{8,10},{9,11},{10,... | collective-permute-start | bytes 196616 | tf_op jit(solution)/shard_map/ppermute | solution.py:339
  85.5 2.1 %collective-permute-done.10 = bf16[64,512]{1,0:T(8,128)(2,1)S(1)} collective-permute-done((bf16[64,512]{1,0:T(8,128)(2,1)S(1)}, bf16[64,512]{1,0:T(8,128)(2,1)S(1)}, u32[]{:S(2)}, u32[]{:S(2)}) %collective-permute-start.10) | collective-permute-done | bytes 65568 | tf_op jit(solution)/shard_map/ppermute | solution.py:376
  87.5 0.2 collective-permute-done.9
  87.7 0.7 collective-permute-done.8
  88.5 4.3 %collective-permute-start.13 = (bf16[64,512]{1,0:T(8,128)(2,1)S(1)}, bf16[64,512]{1,0:T(8,128)(2,1)S(1)}, u32[]{:S(2)}, u32[]{:S(2)}) collective-permute-start(bf16[64,512]{1,0:T(8,128)(2,1)S(1)} %convert_add_fusion.4), channel_id=1, source_target_pairs={{0,16},{4,20},{8,24},{12,28},{16,0},{20,4},{24,8},{28,12},{1,17},{... | collective-permute-start | bytes 196616 | tf_op jit(solution)/shard_map/ppermute | solution.py:339
  92.8 2.7 %collective-permute-start.12 = (bf16[64,512]{1,0:T(8,128)(2,1)S(1)}, bf16[64,512]{1,0:T(8,128)(2,1)S(1)}, u32[]{:S(2)}, u32[]{:S(2)}) collective-permute-start(bf16[64,512]{1,0:T(8,128)(2,1)S(1)} %add_convert_fusion), channel_id=1, source_target_pairs={{0,16},{4,20},{8,24},{12,28},{16,0},{20,4},{24,8},{28,12},{1,17},{... | collective-permute-start | bytes 196616 | tf_op jit(solution)/shard_map/ppermute | solution.py:339
  95.6 1.3 %collective-permute-done.13 = bf16[64,512]{1,0:T(8,128)(2,1)S(1)} collective-permute-done((bf16[64,512]{1,0:T(8,128)(2,1)S(1)}, bf16[64,512]{1,0:T(8,128)(2,1)S(1)}, u32[]{:S(2)}, u32[]{:S(2)}) %collective-permute-start.13) | collective-permute-done | bytes 65568 | tf_op jit(solution)/shard_map/ppermute | solution.py:339
  96.9 1.2 %collective-permute-done.12 = bf16[64,512]{1,0:T(8,128)(2,1)S(1)} collective-permute-done((bf16[64,512]{1,0:T(8,128)(2,1)S(1)}, bf16[64,512]{1,0:T(8,128)(2,1)S(1)}, u32[]{:S(2)}, u32[]{:S(2)}) %collective-permute-start.12) | collective-permute-done | bytes 65568 | tf_op jit(solution)/shard_map/ppermute | solution.py:339
  98.2 2.6 %collective-permute-start.14 = (bf16[64,1024]{1,0:T(8,128)(2,1)S(1)}, bf16[64,1024]{1,0:T(8,128)(2,1)S(1)}, u32[]{:S(2)}, u32[]{:S(2)}) collective-permute-start(bf16[64,1024]{1,0:T(8,128)(2,1)S(1)} %get-tuple-element.25), channel_id=1, source_target_pairs={{0,2},{1,3},{2,0},{3,1},{4,6},{5,7},{6,4},{7,5},{8,10},{9,11},{10,... | collective-permute-start | bytes 393224 | tf_op jit(solution)/shard_map/ppermute | solution.py:339
  100.8 0.8 collective-permute-start.15
  101.5 0.8 collective-permute-start.16
  102.3 2.8 %collective-permute-done.14 = bf16[64,1024]{1,0:T(8,128)(2,1)S(1)} collective-permute-done((bf16[64,1024]{1,0:T(8,128)(2,1)S(1)}, bf16[64,1024]{1,0:T(8,128)(2,1)S(1)}, u32[]{:S(2)}, u32[]{:S(2)}) %collective-permute-start.14) | collective-permute-done | bytes 131104 | tf_op jit(solution)/shard_map/ppermute | solution.py:339
  105.1 0.6 collective-permute-done.15
  105.7 1.7 %collective-permute-done.16 = bf16[64,1024]{1,0:T(8,128)(2,1)S(1)} collective-permute-done((bf16[64,1024]{1,0:T(8,128)(2,1)S(1)}, bf16[64,1024]{1,0:T(8,128)(2,1)S(1)}, u32[]{:S(2)}, u32[]{:S(2)}) %collective-permute-start.16) | collective-permute-done | bytes 131104 | tf_op jit(solution)/shard_map/ppermute | solution.py:376
  107.5 0.7 constant_dynamic-slice_fusion.6
  108.2 0.1 broadcast_in_dim.13
  108.4 1.0 collective-permute-done.17
  109.4 2.6 %update.1 = bf16[1024,512]{1,0:T(8,128)(2,1)} custom-call(bf16[512,1024]{1,0:T(8,128)(2,1)S(1)} %get-tuple-element.14.other_ref.masked_ref, bf16[512,1024]{1,0:T(8,128)(2,1)S(1)} %get-tuple-element.19.applied_ref, bf16[512,1024]{1,0:T(8,128)(2,1)S(1)} %constant_dynamic-update-slice_fusion.lagrange_ref.inter_ref, ...), custom_call_target="tpu_custom_call" | custom-call | flops 1024 | bytes 1024 | tf_op jit(solution)/shard_map/update/pallas_call | solution.py:531
  (46 shorter events, 0.9 us)
Async XLA Ops:
  0.6 18.0 %copy-start = (bf16[29,4,4]{0,2,1:T(4,128)(2,1)S(1)}, bf16[29,4,4]{0,2,1:T(4,128)(2,1)}, u32[]{:S(2)}) copy-start(bf16[29,4,4]{0,2,1:T(4,128)(2,1)} %param.13) | copy-start | bytes 2788
  2.4 1.2 %copy-start.6 = (bf16[64,4,16,128]{3,2,1,0:T(8,128)(2,1)S(1)}, bf16[64,4,16,128]{3,2,1,0:T(8,128)(2,1)}, u32[]{:S(2)}) copy-start(bf16[64,4,16,128]{3,2,1,0:T(8,128)(2,1)} %psi_ref.1) | copy-start | bytes 3145732
  8.5 11.3 %copy-start.2 = (bf16[64,4,16,128]{3,2,1,0:T(8,128)(2,1)}, bf16[64,4,16,128]{3,2,1,0:T(8,128)(2,1)S(1)}, u32[]{:S(2)}) copy-start(bf16[64,4,16,128]{3,2,1,0:T(8,128)(2,1)S(1)} %get-tuple-element.15.masked_ref) | copy-start | bytes 3145732
  8.5 34.5 %all-to-all-start = ((bf16[8,544,128]{2,1,0:T(8,128)(2,1)}), bf16[8,544,128]{2,1,0:T(8,128)(2,1)}, u32[]{:S(2)}, u32[]{:S(2)}) async-start(bf16[8,544,128]{2,1,0:T(8,128)(2,1)} %get-tuple-element.13), calls=%async_computation | async-start | bytes 2228224 | tf_op jit(solution)/shard_map/all_to_all | solution.py:456
  15.8 5.7 %copy-start.8 = (bf16[16,4]{0,1:T(4,128)(2,1)S(1)}, bf16[16,4]{0,1:T(4,128)(2,1)}, u32[]{:S(2)}) copy-start(bf16[16,4]{0,1:T(4,128)(2,1)} %param.14) | copy-start | bytes 388
  15.8 6.1 %collective-permute-start = (bf16[64,4,16,128]{3,2,1,0:T(8,128)(2,1)S(1)}, bf16[64,4,16,128]{3,2,1,0:T(8,128)(2,1)S(1)}, u32[]{:S(2)}, u32[]{:S(2)}) collective-permute-start(bf16[64,4,16,128]{3,2,1,0:T(8,128)(2,1)S(1)} %get-tuple-element.15.masked_ref), channel_id=1, source_target_pairs={{0,1},{1,2},{2,3},{4,5},{5,6},{6,7},{8,9},{9,10},{10,11},{12,13},{... | collective-permute-start | bytes 3145736 | tf_op jit(solution)/shard_map/ppermute | solution.py:454
  17.3 6.2 %collective-permute-start.1 = (bf16[64,4,16,128]{3,2,1,0:T(8,128)(2,1)S(1)}, bf16[64,4,16,128]{3,2,1,0:T(8,128)(2,1)}, u32[]{:S(2)}, u32[]{:S(2)}) collective-permute-start(bf16[64,4,16,128]{3,2,1,0:T(8,128)(2,1)S(1)} %get-tuple-element.15.masked_ref), channel_id=1, source_target_pairs={{1,0},{2,1},{3,2},{5,4},{6,5},{7,6},{9,8},{10,9},{11,10},{13,12},{... | collective-permute-start | bytes 3145736 | tf_op jit(solution)/shard_map/ppermute | solution.py:455
  21.9 1.0 copy-start.4
  23.5 1.2 %copy-start.3 = (bf16[64,4,16,128]{3,2,1,0:T(8,128)(2,1)S(1)}, bf16[64,4,16,128]{3,2,1,0:T(8,128)(2,1)}, u32[]{:S(2)}) copy-start(bf16[64,4,16,128]{3,2,1,0:T(8,128)(2,1)} %copy-done.2) | copy-start | bytes 3145732
  24.7 1.2 %copy-start.5 = (bf16[64,4,16,128]{3,2,1,0:T(8,128)(2,1)S(1)}, bf16[64,4,16,128]{3,2,1,0:T(8,128)(2,1)}, u32[]{:S(2)}) copy-start(bf16[64,4,16,128]{3,2,1,0:T(8,128)(2,1)} %copy-done.4) | copy-start | bytes 3145732
  26.0 18.0 %copy-start.7 = (f32[16,128]{1,0:T(8,128)S(1)}, f32[16,128]{1,0:T(8,128)}, u32[]{:S(2)}) copy-start(f32[16,128]{1,0:T(8,128)} %param.15) | copy-start | bytes 24580
  47.9 1.0 copy-start.1
  48.9 30.5 %all-to-all-start.1 = ((bf16[8,512,128]{2,1,0:T(8,128)(2,1)}), bf16[8,512,128]{2,1,0:T(8,128)(2,1)S(1)}, u32[]{:S(2)}, u32[]{:S(2)}) async-start(bf16[8,512,128]{2,1,0:T(8,128)(2,1)} %copy-done.1), calls=%async_computation.1 | async-start | bytes 2097152 | tf_op jit(solution)/shard_map/all_to_all | solution.py:494
  54.6 1.9 %collective-permute-start.2 = (bf16[256,512]{1,0:T(8,128)(2,1)S(1)}, bf16[256,512]{1,0:T(8,128)(2,1)S(1)}, u32[]{:S(2)}, u32[]{:S(2)}) collective-permute-start(bf16[256,512]{1,0:T(8,128)(2,1)S(1)} %get-tuple-element.17), channel_id=1, source_target_pairs={{0,1},{1,0},{2,3},{3,2},{4,5},{5,4},{6,7},{7,6},{8,9},{9,8},{10,11... | collective-permute-start | bytes 786440 | tf_op jit(solution)/shard_map/ppermute | solution.py:339
  56.6 8.4 %collective-permute-start.5 = (bf16[64,512]{1,0:T(8,128)(2,1)S(1)}, bf16[64,512]{1,0:T(8,128)(2,1)S(1)}, u32[]{:S(2)}, u32[]{:S(2)}) collective-permute-start(bf16[64,512]{1,0:T(8,128)(2,1)S(1)} %get-tuple-element.34), channel_id=1, source_target_pairs={{0,6},{1,7},{2,4},{3,5},{4,2},{5,3},{6,0},{7,1},{8,14},{9,15},{10,... | collective-permute-start | bytes 196616 | tf_op jit(solution)/shard_map/ppermute | solution.py:376
  59.4 7.2 %collective-permute-start.4 = (bf16[64,512]{1,0:T(8,128)(2,1)S(1)}, bf16[64,512]{1,0:T(8,128)(2,1)S(1)}, u32[]{:S(2)}, u32[]{:S(2)}) collective-permute-start(bf16[64,512]{1,0:T(8,128)(2,1)S(1)} %get-tuple-element.35), channel_id=1, source_target_pairs={{0,4},{4,0},{8,12},{12,8},{16,20},{20,16},{24,28},{28,24},{1,5},{5... | collective-permute-start | bytes 196616 | tf_op jit(solution)/shard_map/ppermute | solution.py:339
  59.4 7.2 %collective-permute-start.3 = (bf16[64,512]{1,0:T(8,128)(2,1)S(1)}, bf16[64,512]{1,0:T(8,128)(2,1)S(1)}, u32[]{:S(2)}, u32[]{:S(2)}) collective-permute-start(bf16[64,512]{1,0:T(8,128)(2,1)S(1)} %get-tuple-element.33), channel_id=1, source_target_pairs={{0,2},{1,3},{2,0},{3,1},{4,6},{5,7},{6,4},{7,5},{8,10},{9,11},{10,... | collective-permute-start | bytes 196616 | tf_op jit(solution)/shard_map/ppermute | solution.py:339
  66.7 6.7 %collective-permute-start.6 = (bf16[64,512]{1,0:T(8,128)(2,1)S(1)}, bf16[64,512]{1,0:T(8,128)(2,1)S(1)}, u32[]{:S(2)}, u32[]{:S(2)}) collective-permute-start(bf16[64,512]{1,0:T(8,128)(2,1)S(1)} %add_convert_fusion.2), channel_id=1, source_target_pairs={{0,8},{4,12},{8,0},{12,4},{16,24},{20,28},{24,16},{28,20},{1,9},{5... | collective-permute-start | bytes 196616 | tf_op jit(solution)/shard_map/ppermute | solution.py:339
  80.2 1.6 %collective-permute-start.7 = (bf16[256,512]{1,0:T(8,128)(2,1)S(1)}, bf16[256,512]{1,0:T(8,128)(2,1)S(1)}, u32[]{:S(2)}, u32[]{:S(2)}) collective-permute-start(bf16[256,512]{1,0:T(8,128)(2,1)S(1)} %get-tuple-element.21), channel_id=1, source_target_pairs={{0,1},{1,0},{2,3},{3,2},{4,5},{5,4},{6,7},{7,6},{8,9},{9,8},{10,11... | collective-permute-start | bytes 786440 | tf_op jit(solution)/shard_map/ppermute | solution.py:339
  81.9 5.6 %collective-permute-start.10 = (bf16[64,512]{1,0:T(8,128)(2,1)S(1)}, bf16[64,512]{1,0:T(8,128)(2,1)S(1)}, u32[]{:S(2)}, u32[]{:S(2)}) collective-permute-start(bf16[64,512]{1,0:T(8,128)(2,1)S(1)} %get-tuple-element.31), channel_id=1, source_target_pairs={{0,6},{1,7},{2,4},{3,5},{4,2},{5,3},{6,0},{7,1},{8,14},{9,15},{10,... | collective-permute-start | bytes 196616 | tf_op jit(solution)/shard_map/ppermute | solution.py:376
  83.5 4.3 %collective-permute-start.9 = (bf16[64,512]{1,0:T(8,128)(2,1)S(1)}, bf16[64,512]{1,0:T(8,128)(2,1)S(1)}, u32[]{:S(2)}, u32[]{:S(2)}) collective-permute-start(bf16[64,512]{1,0:T(8,128)(2,1)S(1)} %get-tuple-element.32), channel_id=1, source_target_pairs={{0,4},{4,0},{8,12},{12,8},{16,20},{20,16},{24,28},{28,24},{1,5},{5... | collective-permute-start | bytes 196616 | tf_op jit(solution)/shard_map/ppermute | solution.py:339
  84.1 4.3 %collective-permute-start.8 = (bf16[64,512]{1,0:T(8,128)(2,1)S(1)}, bf16[64,512]{1,0:T(8,128)(2,1)S(1)}, u32[]{:S(2)}, u32[]{:S(2)}) collective-permute-start(bf16[64,512]{1,0:T(8,128)(2,1)S(1)} %get-tuple-element.30), channel_id=1, source_target_pairs={{0,2},{1,3},{2,0},{3,1},{4,6},{5,7},{6,4},{7,5},{8,10},{9,11},{10,... | collective-permute-start | bytes 196616 | tf_op jit(solution)/shard_map/ppermute | solution.py:339
  88.5 4.3 %collective-permute-start.11 = (bf16[64,512]{1,0:T(8,128)(2,1)S(1)}, bf16[64,512]{1,0:T(8,128)(2,1)S(1)}, u32[]{:S(2)}, u32[]{:S(2)}) collective-permute-start(bf16[64,512]{1,0:T(8,128)(2,1)S(1)} %add_convert_fusion.1), channel_id=1, source_target_pairs={{0,8},{4,12},{8,0},{12,4},{16,24},{20,28},{24,16},{28,20},{1,9},{5... | collective-permute-start | bytes 196616 | tf_op jit(solution)/shard_map/ppermute | solution.py:339
  88.5 8.3 %collective-permute-start.13 = (bf16[64,512]{1,0:T(8,128)(2,1)S(1)}, bf16[64,512]{1,0:T(8,128)(2,1)S(1)}, u32[]{:S(2)}, u32[]{:S(2)}) collective-permute-start(bf16[64,512]{1,0:T(8,128)(2,1)S(1)} %convert_add_fusion.4), channel_id=1, source_target_pairs={{0,16},{4,20},{8,24},{12,28},{16,0},{20,4},{24,8},{28,12},{1,17},{... | collective-permute-start | bytes 196616 | tf_op jit(solution)/shard_map/ppermute | solution.py:339
  92.8 5.2 %collective-permute-start.12 = (bf16[64,512]{1,0:T(8,128)(2,1)S(1)}, bf16[64,512]{1,0:T(8,128)(2,1)S(1)}, u32[]{:S(2)}, u32[]{:S(2)}) collective-permute-start(bf16[64,512]{1,0:T(8,128)(2,1)S(1)} %add_convert_fusion), channel_id=1, source_target_pairs={{0,16},{4,20},{8,24},{12,28},{16,0},{20,4},{24,8},{28,12},{1,17},{... | collective-permute-start | bytes 196616 | tf_op jit(solution)/shard_map/ppermute | solution.py:339
  98.2 6.9 %collective-permute-start.14 = (bf16[64,1024]{1,0:T(8,128)(2,1)S(1)}, bf16[64,1024]{1,0:T(8,128)(2,1)S(1)}, u32[]{:S(2)}, u32[]{:S(2)}) collective-permute-start(bf16[64,1024]{1,0:T(8,128)(2,1)S(1)} %get-tuple-element.25), channel_id=1, source_target_pairs={{0,2},{1,3},{2,0},{3,1},{4,6},{5,7},{6,4},{7,5},{8,10},{9,11},{10,... | collective-permute-start | bytes 393224 | tf_op jit(solution)/shard_map/ppermute | solution.py:339
  100.8 5.0 %collective-permute-start.15 = (bf16[64,1024]{1,0:T(8,128)(2,1)S(1)}, bf16[64,1024]{1,0:T(8,128)(2,1)S(1)}, u32[]{:S(2)}, u32[]{:S(2)}) collective-permute-start(bf16[64,1024]{1,0:T(8,128)(2,1)S(1)} %get-tuple-element.25), channel_id=1, source_target_pairs={{0,4},{4,0},{8,12},{12,8},{16,20},{20,16},{24,28},{28,24},{1,5},{5... | collective-permute-start | bytes 393224 | tf_op jit(solution)/shard_map/ppermute | solution.py:339
  101.5 5.9 %collective-permute-start.16 = (bf16[64,1024]{1,0:T(8,128)(2,1)S(1)}, bf16[64,1024]{1,0:T(8,128)(2,1)S(1)}, u32[]{:S(2)}, u32[]{:S(2)}) collective-permute-start(bf16[64,1024]{1,0:T(8,128)(2,1)S(1)} %get-tuple-element.25), channel_id=1, source_target_pairs={{0,6},{1,7},{2,4},{3,5},{4,2},{5,3},{6,0},{7,1},{8,14},{9,15},{10,... | collective-permute-start | bytes 393224 | tf_op jit(solution)/shard_map/ppermute | solution.py:376
  107.4 2.0 %collective-permute-start.17 = (bf16[256,1024]{1,0:T(8,128)(2,1)S(1)}, bf16[256,1024]{1,0:T(8,128)(2,1)S(1)}, u32[]{:S(2)}, u32[]{:S(2)}) collective-permute-start(bf16[256,1024]{1,0:T(8,128)(2,1)S(1)} %constant_dynamic-update-slice_fusion.2), channel_id=1, source_target_pairs={{0,1},{1,0},{2,3},{3,2},{4,5},{5,4},{6,7},{7,6},{8,9},{9,8},{10,11... | collective-permute-start | bytes 1572872 | tf_op jit(solution)/shard_map/ppermute | solution.py:339
